TPU v7x, 128 devices: a whole 4x4x4 slice. The times are simulated.
128 devices in a mesh: seq: 32 (over z, x, core), mp: 4 (over y).
Axes of the slice: x: 4, y: 4, z: 4, core: 2. Of those that a mesh axis runs over, the one named last changes fastest.
Arguments:
- hidden_in: float32 [16384, 1024], P('seq'), may hold values from -6 to 6
- mix_gain: float32 [1024], replicated, may hold values from 0.1 to 1.9
- in_weight: bfloat16 [1024, 3, 1024], P(None, None, 'mp'), may hold values from -0.1875 to 0.1875
- conv_weight: float32 [3, 1024], P(None, 'mp'), may hold values from -3 to 3
- out_weight: bfloat16 [1024, 1024], P('mp'), may hold values from -0.1875 to 0.1875
- ffn_gain: float32 [1024], replicated, may hold values from 0.1 to 1.9
- gate_up_weight: bfloat16 [1024, 2, 4608], P(None, None, 'mp'), may hold values from -0.1875 to 0.1875
- down_weight: bfloat16 [4608, 1024], P('mp'), may hold values from -0.09375 to 0.09375
- seq_starts: int32 [32], P('seq'), may hold values from 1 to 512, as said below
- out_grad: float32 [16384, 1024], P('seq'), may hold values from -6 to 6
Outputs:
- hidden_out: float32 [16384, 1024], P('seq')
- hidden_grad: float32 [16384, 1024], P('seq')
- mix_gain_grad: float32 [1024], replicated
- in_weight_grad: float32 [1024, 3, 1024], P('seq', None, 'mp')
- conv_weight_grad: float32 [3, 1024], P(None, 'mp')
- out_weight_grad: float32 [1024, 1024], P('mp', 'seq')
- ffn_gain_grad: float32 [1024], replicated
- gate_up_grad: float32 [1024, 2, 4608], P('seq', None, 'mp')
- down_grad: float32 [4608, 1024], P('mp', 'seq')
Inputs may be any that keep to these rules, and one draw needn't show every extreme that they name: seq_starts[0] lies in 1 to 256, the last entry in 256 to 511, and every other entry is 512: one sequence runs from inside the first slab to inside the last.
All inputs are finite; a program needn't handle non-finite values.
Results may differ from a plain program's by a relative error of at most 0.012.
Values may be sent and summed in bfloat16 or wider, within the bound.
No kernel may reach another device: no remote copies, remote signals or barrier semaphores. Data moves between devices by JAX's collectives and lax.ppermute only.
A program may use at most 128 MiB of HBM per device.

v0:
```python
import jax
import jax.numpy as jnp
from jax import lax
from jax.sharding import PartitionSpec as P

EPS = 1e-05


def from_behind(value, axis, by):
    devices = lax.axis_size(axis)
    pairs = [(i, i + by) for i in range(devices) if 0 <= i + by < devices]
    return lax.ppermute(value, axis, pairs)


def norm_back(grad_unit, unit_rows, inv_rows):
    return inv_rows * (
        grad_unit - unit_rows * jnp.mean(grad_unit * unit_rows, axis=1, keepdims=True)
    )


def on_device(
    hidden_in,
    mix_gain,
    in_weight,
    conv_weight,
    out_weight,
    ffn_gain,
    gate_up_weight,
    down_weight,
    seq_starts,
    out_grad,
):
    rows = hidden_in.shape[0]
    opens_here = (jnp.arange(rows, dtype=jnp.int32) == seq_starts[0]).astype(jnp.float32)
    before_here = jnp.concatenate([jnp.zeros((1,), jnp.float32), opens_here[:-1]])
    keep_one = (1.0 - opens_here)[:, None]
    keep_two = ((1.0 - opens_here) * (1.0 - before_here))[:, None]
    inv_first = lax.rsqrt(jnp.mean(hidden_in * hidden_in, axis=1, keepdims=True) + EPS)
    unit_first = hidden_in * inv_first
    normed = (unit_first * mix_gain).astype(jnp.bfloat16)
    project = jnp.einsum("td,dkc->tkc", normed, in_weight, preferred_element_type=jnp.float32)
    b_part = project[:, 0]
    c_part = project[:, 1]
    x_part = project[:, 2]
    mixed_in = (b_part * x_part).astype(jnp.bfloat16)
    came_state = from_behind(mixed_in[rows - 2 :], "seq", 1)
    padded = jnp.concatenate([came_state, mixed_in], 0).astype(jnp.float32)
    tap_two = padded[:-2] * keep_two
    tap_one = padded[1:-1] * keep_one
    convolved = conv_weight[0] * tap_two + conv_weight[1] * tap_one + conv_weight[2] * padded[2:]
    gated = (c_part * convolved).astype(jnp.bfloat16)
    branch = lax.psum(jnp.dot(gated, out_weight, preferred_element_type=jnp.float32), "mp")
    middle = hidden_in + branch
    inv_second = lax.rsqrt(jnp.mean(middle * middle, axis=1, keepdims=True) + EPS)
    unit_second = middle * inv_second
    normed_two = (unit_second * ffn_gain).astype(jnp.bfloat16)
    gate_up = jnp.einsum(
        "td,dkf->tkf", normed_two, gate_up_weight, preferred_element_type=jnp.float32
    )
    gate_val = gate_up[:, 0]
    upper_val = gate_up[:, 1]
    sigma = jax.nn.sigmoid(gate_val)
    active = (gate_val * sigma * upper_val).astype(jnp.bfloat16)
    ffn_out = lax.psum(jnp.dot(active, down_weight, preferred_element_type=jnp.float32), "mp")
    hidden_out = middle + ffn_out
    grad_low = out_grad.astype(jnp.bfloat16)
    down_part = jnp.einsum("tf,td->fd", active, grad_low, preferred_element_type=jnp.float32)
    grad_active = jnp.einsum("td,fd->tf", grad_low, down_weight, preferred_element_type=jnp.float32)
    grad_gate = grad_active * upper_val * sigma * (1.0 + gate_val * (1.0 - sigma))
    grad_upper = grad_active * gate_val * sigma
    grad_gu = jnp.stack([grad_gate, grad_upper], axis=1).astype(jnp.bfloat16)
    gate_up_part = jnp.einsum(
        "td,tkf->dkf", normed_two, grad_gu, preferred_element_type=jnp.float32
    )
    grad_normed_two = lax.psum(
        jnp.einsum("tkf,dkf->td", grad_gu, gate_up_weight, preferred_element_type=jnp.float32), "mp"
    )
    ffn_gain_part = jnp.sum(grad_normed_two * unit_second, axis=0)
    grad_middle = out_grad + norm_back(grad_normed_two * ffn_gain, unit_second, inv_second)
    grad_branch = grad_middle.astype(jnp.bfloat16)
    out_part = jnp.einsum("tc,td->cd", gated, grad_branch, preferred_element_type=jnp.float32)
    grad_gated = jnp.einsum(
        "td,cd->tc", grad_branch, out_weight, preferred_element_type=jnp.float32
    )
    grad_c = grad_gated * convolved
    grad_conv = grad_gated * c_part
    grad_padded = (
        jnp.pad(conv_weight[0] * grad_conv * keep_two, ((0, 2), (0, 0)))
        + jnp.pad(conv_weight[1] * grad_conv * keep_one, ((1, 1), (0, 0)))
        + jnp.pad(conv_weight[2] * grad_conv, ((2, 0), (0, 0)))
    )
    conv_part = jnp.stack(
        [
            jnp.sum(grad_conv * tap_two, axis=0),
            jnp.sum(grad_conv * tap_one, axis=0),
            jnp.sum(grad_conv * padded[2:], axis=0),
        ],
        axis=0,
    )
    came_grad = from_behind(grad_padded[:2], "seq", -1)
    grad_mixed = grad_padded[2:] + jnp.pad(came_grad, ((rows - 2, 0), (0, 0)))
    grad_mixed = lax.optimization_barrier(grad_mixed.astype(jnp.bfloat16)).astype(jnp.float32)
    grad_project = jnp.stack([grad_mixed * x_part, grad_c, grad_mixed * b_part], axis=1).astype(
        jnp.bfloat16
    )
    in_part = jnp.einsum("td,tkc->dkc", normed, grad_project, preferred_element_type=jnp.float32)
    grad_normed = lax.psum(
        jnp.einsum("tkc,dkc->td", grad_project, in_weight, preferred_element_type=jnp.float32), "mp"
    )
    mix_gain_part = jnp.sum(grad_normed * unit_first, axis=0)
    hidden_grad = grad_middle + norm_back(grad_normed * mix_gain, unit_first, inv_first)
    mix_gain_grad, conv_weight_grad, ffn_gain_grad = lax.psum(
        (mix_gain_part, conv_part, ffn_gain_part), "seq"
    )
    in_done, out_done, gate_up_done, down_done = (
        lax.psum_scatter(in_part, "seq", scatter_dimension=0, tiled=True),
        lax.psum_scatter(out_part, "seq", scatter_dimension=1, tiled=True),
        lax.psum_scatter(gate_up_part, "seq", scatter_dimension=0, tiled=True),
        lax.psum_scatter(down_part, "seq", scatter_dimension=1, tiled=True),
    )
    return (
        hidden_out,
        hidden_grad,
        mix_gain_grad,
        in_done,
        conv_weight_grad,
        out_done,
        ffn_gain_grad,
        gate_up_done,
        down_done,
    )


def solution(mesh):
    placed = (
        P("seq", None),
        P(),
        P(None, None, "mp"),
        P(None, "mp"),
        P("mp", None),
        P(),
        P(None, None, "mp"),
        P("mp", None),
        P("seq"),
        P("seq", None),
    )
    return jax.shard_map(
        on_device,
        mesh=mesh,
        in_specs=placed,
        out_specs=(
            P("seq", None),
            P("seq", None),
            P(),
            P("seq", None, "mp"),
            P(None, "mp"),
            P("mp", "seq"),
            P(),
            P("seq", None, "mp"),
            P("mp", "seq"),
        ),
        check_vma=False,
    )
```

profile of v0, /device:TPU:2, one launch (start us, length us, event | category | flops | bytes accessed | tf_op | source)
XLA Modules:
  0.0 627.1 jit_solution(17792927167968718337)
XLA Ops:
  7.3 2.0 multiply_reduce_fusion.5
  9.6 2.5 fusion.31
  12.2 2.1 collective-permute-start
  15.0 2.2 collective-permute-done
  18.3 1.8 fusion.43
  20.1 61.1 %all-reduce.10.cloned.1.call-done = f32[512,1024]{1,0:T(8,128)} async-done(((f32[512,1024]{1,0:T(8,128)}), f32[512,1024]{1,0:T(8,128)}) %all-reduce.10.cloned.1.call-update) | async-done | bytes 2097168 | tf_op jit(solution)/shard_map/psum | solution.py:52
  81.3 2.7 multiply_reduce_fusion.4
  84.0 1.3 copy-done.2
  85.3 5.2 fusion.2
  90.5 3.4 fusion.9
  95.3 4.0 fusion.4
  99.4 4.1 fusion.44
  103.5 54.5 %all-reduce.12.cloned.1.call-done = f32[512,1024]{1,0:T(8,128)} async-done(((f32[512,1024]{1,0:T(8,128)}), f32[512,1024]{1,0:T(8,128)}) %all-reduce.12.cloned.1.call-update) | async-done | bytes 2097168 | tf_op jit(solution)/shard_map/psum | solution.py:75
  158.0 3.0 multiply_reduce_fusion
  161.0 2.1 multiply_add_fusion.1
  163.6 1.7 copy-done.11
  166.5 2.2 collective-permute-start.1
  168.8 1.2 collective-permute-done.1
  170.2 2.3 convolution_bitcast_fusion
  172.6 6.9 %fusion.7 = f32[1024,2,1152]{2,0,1:T(8,128)} fusion(bf16[512,1,1152]{2,0,1:T(8,128)(2,1)} %copy-done.17, bf16[512,1,1152]{2,0,1:T(8,128)(2,1)} %copy-done.16, f32[512,1024]{1,0:T(8,128)S(1)} %copy-done.3, f32[1024]{0:T(1024)S(1)} %copy-done.18, f32[512]{0:T(512)S(1)} %add_rsqrt_fusion), kind=kOutput, calls=%fused_computation.23 | convolution fusion | flops 2422210560 | bytes 13899776 | tf_op jit(solution)/shard_map/td,tkf->dkf/dot_general | solution.py:72
  179.6 3.1 fusion.15
  182.8 4.9 fusion.24
  187.8 1.2 copy-done.12
  189.0 5.4 fusion.19
  195.0 73.5 %all-reduce.14.cloned.1.call-done = (f32[512,1024]{1,0:T(8,128)}, f32[512,1024]{1,0:T(8,128)}) async-done(((f32[512,1024]{1,0:T(8,128)}, f32[512,1024]{1,0:T(8,128)}), (f32[512,1024]{1,0:T(8,128)}, f32[512,1024]{1,0:T(8,128)})) %all-reduce.14.cloned.1.call-update) | async-done | bytes 4194320 | tf_op jit(solution)/shard_map/psum | solution.py:64
  268.5 3.6 add.85
  272.8 123.9 %all-reduce.4 = (f32[1024]{0:T(1024)}, f32[3,256]{1,0:T(4,128)}, f32[1024]{0:T(1024)}) all-reduce(f32[1024]{0:T(1024)S(1)} %get-tuple-element.20, f32[3,256]{1,0:T(4,128)S(1)} %pad_maximum_fusion.6, f32[1024]{0:T(1024)S(1)} %get-tuple-element.18), channel_id=1, replica_groups=mesh['seq'=32,'mp'=4] {'seq'}, use_global_device_ids=true, to_apply=%region_9.10 | all-reduce | flops 2816 | bytes 22528 | tf_op jit(solution)/shard_map/psum | solution.py:112
  396.7 4.9 multiply_add_fusion
  401.6 1.9 copy.23
  403.5 45.2 %reduce-scatter.7.cloned.1.call-done = f32[256,32]{0,1:T(8,128)} async-done(((f32[256,1024]{0,1:T(8,128)}), f32[256,32]{0,1:T(8,128)}) %reduce-scatter.7.cloned.1.call-update) | async-done | bytes 32784 | tf_op jit(solution)/shard_map/reduce_scatter | solution.py:117
  448.7 84.3 %reduce-scatter.5.cloned.1.call-done = f32[32,3,256]{2,0,1:T(8,128)} async-done(((f32[1024,3,256]{2,0,1:T(8,128)}), f32[32,3,256]{2,0,1:T(8,128)}) %reduce-scatter.5.cloned.1.call-update) | async-done | bytes 98320 | tf_op jit(solution)/shard_map/reduce_scatter | solution.py:116
  533.0 87.3 %reduce-scatter.11.cloned.1.call-done = f32[1152,32]{0,1:T(8,128)} async-done(((f32[1152,1024]{0,1:T(8,128)}), f32[1152,32]{0,1:T(8,128)}) %reduce-scatter.11.cloned.1.call-update) | async-done | bytes 147472 | tf_op jit(solution)/shard_map/reduce_scatter | solution.py:119
  (86 shorter events, 6.8 us)
Async XLA Ops:
  7.2 83.3 %copy-start = (bf16[1152,1024]{1,0:T(8,128)(2,1)S(1)}, bf16[1152,1024]{1,0:T(8,128)(2,1)}, u32[]{:S(2)}) copy-start(bf16[1152,1024]{1,0:T(8,128)(2,1)} %param.17) | copy-start | bytes 7077892
  7.2 2.0 copy-start.19
  7.2 74.1 %all-reduce.10.cloned.1.call-start = ((), (), s32[]{:S(2)}) async-start(), calls=%async_computation.4 | async-start | bytes 4194304 | tf_op jit(solution)/shard_map/psum | solution.py:52
  7.2 2.3 copy-start.4
  9.6 5.3 copy-start.22
  12.1 6.2 copy-start.10
  12.1 6.2 copy-start.14
  12.2 5.0 collective-permute-start
  20.1 65.2 %copy-start.18 = (f32[1024]{0:T(1024)S(1)}, f32[1024]{0:T(1024)}, u32[]{:S(2)}) copy-start(f32[1024]{0:T(1024)} %param.15) | copy-start | bytes 12292
  20.1 137.9 %all-reduce.12.cloned.1.call-start = ((), (), s32[]{:S(2)}) async-start(), calls=%async_computation.5 | async-start | bytes 4194304 | tf_op jit(solution)/shard_map/psum | solution.py:75
  81.3 14.0 %slice-start = ((s8[4718592]{0:T(1024)(128)(4,1)}), s8[4194304]{0:T(1024)(128)(4,1)S(1)}, s32[]{:S(2)}) async-start(s8[4718592]{0:T(1024)(128)(4,1)} %bitcast.98), calls=%async_computation.11 | async-start | bytes 8388608
  84.0 1.3 copy-start.2
  85.3 5.2 copy-start.7
  85.3 10.0 %slice-start.1 = ((s8[4718592]{0:T(1024)(128)(4,1)}), s8[524288]{0:T(1024)(128)(4,1)S(1)}, s32[]{:S(2)}) async-start(s8[4718592]{0:T(1024)(128)(4,1)} %bitcast.98), calls=%async_computation.12 | async-start | bytes 1048576
  93.9 1.4 copy-start.17
  99.3 169.2 %all-reduce.14.cloned.1.call-start = ((), (), s32[]{:S(2)}) async-start(), calls=%async_computation.10 | async-start | bytes 8388608 | tf_op jit(solution)/shard_map/psum | solution.py:64
  103.5 57.5 %copy-start.3 = (f32[512,1024]{1,0:T(8,128)S(1)}, f32[512,1024]{1,0:T(8,128)}, u32[]{:S(2)}) copy-start(f32[512,1024]{1,0:T(8,128)} %copy-done.2) | copy-start | bytes 6291460
  158.0 3.0 copy-start.8
  160.9 2.2 copy-start.15
  163.1 3.1 copy-start.6
  163.1 2.2 copy-start.11
  163.1 2.3 copy-start.13
  166.5 3.7 copy-start.23
  166.5 3.5 collective-permute-start.1
  172.6 229.0 %reduce-scatter.9.cloned.1.call-start = ((), (), s32[]{:S(2)}) async-start(), calls=%async_computation.8 | async-start | bytes 9732096 | tf_op jit(solution)/shard_map/reduce_scatter | solution.py:118
  179.5 269.2 %reduce-scatter.7.cloned.1.call-start = ((), (), s32[]{:S(2)}) async-start(), calls=%async_computation.7 | async-start | bytes 1081344 | tf_op jit(solution)/shard_map/reduce_scatter | solution.py:117
  182.7 350.3 %reduce-scatter.5.cloned.1.call-start = ((), (), s32[]{:S(2)}) async-start(), calls=%async_computation.6 | async-start | bytes 3244032 | tf_op jit(solution)/shard_map/reduce_scatter | solution.py:116
  187.7 1.3 copy-start.12
  187.7 432.6 %reduce-scatter.11.cloned.1.call-start = ((), (), s32[]{:S(2)}) async-start(), calls=%async_computation.9 | async-start | bytes 4866048 | tf_op jit(solution)/shard_map/reduce_scatter | solution.py:119
  268.5 3.6 copy-start.5
  268.5 3.6 copy-start.9
  396.7 223.6 %copy-start.1 = (bf16[1152,1024]{1,0:T(8,128)(2,1)S(1)}, bf16[1152,1024]{1,0:T(8,128)(2,1)}, u32[]{:S(2)}) copy-start(bf16[1152,1024]{1,0:T(8,128)(2,1)} %param.17) | copy-start | bytes 7077892
  (3 other events, 2.4 us)
Sparse Core Ops, SparseCore 0:
  20.2 61.0 all-reduce.9
  99.4 58.4 all-reduce.11
  172.7 95.7 all-reduce.13
  272.6 95.2 reduce-scatter.8
  371.8 76.8 reduce-scatter.6
  453.2 79.7 reduce-scatter.4
  537.3 82.9 reduce-scatter.10
where the time goes:
time: 628 us; the launch traced here: 627 us
  waiting for transfers between devices  409 us (65%)
  blocking collectives  124 us (20%)
  matrix products  44 us (7%)
  other arithmetic  21.5 us (3%)
  between operations  15.1 us (2%)
  local copies, waits for them, and re-layouts  8.71 us (1%)
    psum x1, blocking collectives, on_device(): lax.psum((mix_gain_part, conv_part, ffn_gain_part), 'seq')  124 us
    reduce_scatter x1, waiting for transfers between devices, on_device(): lax.psum_scatter(down_part, 'seq', scatter_dimension=1, tiled=True)  87.3 us
    reduce_scatter x1, waiting for transfers between devices, on_device(): lax.psum_scatter(in_part, 'seq', scatter_dimension=0, tiled=True)  84.3 us
    psum x1, waiting for transfers between devices, on_device(): lax.psum(jnp.dot(active, down_weight, preferred_element_type=jnp.float32)...  73.5 us
    psum x1, waiting for transfers between devices, on_device(): lax.psum(jnp.dot(gated, out_weight, preferred_element_type=jnp.float32),...  61.1 us
    psum x1, waiting for transfers between devices, on_device(): lax.psum(jnp.einsum('tkf,dkf->td', grad_gu, gate_up_weight, preferred_ele...  54.5 us
    reduce_scatter x1, waiting for transfers between devices, on_device(): lax.psum_scatter(out_part, 'seq', scatter_dimension=1, tiled=True)  45.2 us
  transfers between devices with their start and end apart: 9, of which 8 were waited for; matrix products, arithmetic and copies ran while one was open for 6% of the time, Pallas kernels for 0%

commit v1 on v0

v1 whole, which is shorter than its diff:
```python
import jax
import jax.numpy as jnp
from jax import lax
from jax.sharding import PartitionSpec as P

EPS = 1e-05
LOW = jnp.bfloat16
FULL = jnp.float32
MP = 4
X_DIM = 4
Z_DIM = 4


def ring_shift(size, by):
    return [(i, (i + by) % size) for i in range(size)]


def seq_index(z, x, core):
    return (z * X_DIM + x) * 2 + core


def seq_shift(dz, dx, flip):
    return [
        (
            seq_index(z, x, core),
            seq_index((z + dz) % Z_DIM, (x + dx) % X_DIM, core ^ flip),
        )
        for z in range(Z_DIM)
        for x in range(X_DIM)
        for core in range(2)
    ]


def slab_shift(value, by):
    devices = lax.axis_size("seq")
    pairs = [(i, i + by) for i in range(devices) if 0 <= i + by < devices]
    return lax.ppermute(value, "seq", pairs)


def dot(left, right, contract):
    return lax.dot_general(left, right, (contract, ((), ())), preferred_element_type=FULL)


def sum_rows(part):
    rows = part.shape[0] // MP
    total = part[:rows].astype(FULL)
    came = [
        lax.ppermute(part[o * rows : (o + 1) * rows], "mp", ring_shift(MP, o)) for o in (1, 3, 2)
    ]
    for value in came:
        total = total + value.astype(FULL)
    return total


def gather_rows(rows):
    came = {o: lax.ppermute(rows, "mp", ring_shift(MP, -o)) for o in (1, 3, 2)}
    return jnp.concatenate([rows, came[1], came[2], came[3]], axis=0)


def take(value, index, axis):
    return lax.dynamic_index_in_dim(value, index, axis, keepdims=False)


def scatter_sum(part, order):
    me = lax.axis_index("seq")
    core, x, z = me % 2, (me // 2) % X_DIM, me // (2 * X_DIM)
    cols = part.shape[1]
    part = part.reshape(Z_DIM, X_DIM, 2, -1, cols)
    came = lax.ppermute(take(part, 1 - core, 2), "seq", seq_shift(0, 0, 1))
    part = take(part, core, 2).astype(FULL) + came.astype(FULL)
    for name in order:
        mine, axis = (x, 1) if name == "x" else (z, 0)
        axis = min(axis, part.ndim - 3)
        total = take(part, mine, axis)
        low = part.astype(LOW)
        for o in (1, 3, 2):
            shift = seq_shift(0, o, 0) if name == "x" else seq_shift(o, 0, 0)
            came = lax.ppermute(take(low, (mine + o) % 4, axis), "seq", shift)
            total = total + came.astype(FULL)
        part = total
    return part


def norm_back(grad_unit, unit_rows, inv_rows):
    return inv_rows * (
        grad_unit - unit_rows * jnp.mean(grad_unit * unit_rows, axis=1, keepdims=True)
    )


def turn(value, by):
    rows = value.shape[0]
    return lax.dynamic_slice_in_dim(jnp.concatenate([value, value], 0), by, rows, 0)


def on_device(
    hidden_in,
    mix_gain,
    in_weight,
    conv_weight,
    out_weight,
    ffn_gain,
    gate_up_weight,
    down_weight,
    seq_starts,
    out_grad,
):
    rows, width = hidden_in.shape
    mine = rows // MP
    channels = conv_weight.shape[1]
    me = lax.axis_index("mp")
    start = me * mine
    place = (jnp.arange(rows, dtype=jnp.int32) + start) % rows
    opens = place == seq_starts[0]
    after_open = place == seq_starts[0] + 1
    keep_one = (1.0 - opens.astype(FULL))[:, None]
    keep_two = (1.0 - (opens | after_open).astype(FULL))[:, None]
    is_first = (place == 0)[:, None]
    is_second = (place == 1)[:, None]
    is_last = (place == rows - 1)[:, None]
    is_before_last = (place == rows - 2)[:, None]

    w_in = in_weight.reshape(width, -1)
    w_gu = gate_up_weight.reshape(width, -1)

    tail_in = slab_shift(hidden_in[rows - 8 :], 1)
    inv_tail = lax.rsqrt(jnp.mean(tail_in * tail_in, axis=1, keepdims=True) + EPS)
    tail_normed = (tail_in * inv_tail * mix_gain).astype(LOW)
    tail_project = dot(tail_normed, w_in, ((1,), (0,)))
    came_state = (
        (tail_project[:, :channels] * tail_project[:, 2 * channels :]).astype(LOW).astype(FULL)
    )
    came_two, came_one = came_state[6:7], came_state[7:8]

    hidden = turn(hidden_in, start)
    inv_first = lax.rsqrt(jnp.mean(hidden * hidden, axis=1, keepdims=True) + EPS)
    unit_first = hidden * inv_first
    normed = (unit_first * mix_gain).astype(LOW)
    project = dot(normed, w_in, ((1,), (0,)))
    b_part = project[:, :channels]
    c_part = project[:, channels : 2 * channels]
    x_part = project[:, 2 * channels :]
    mixed = (b_part * x_part).astype(LOW).astype(FULL)
    back_one = jnp.concatenate([mixed[-1:], mixed[:-1]], 0)
    back_two = jnp.concatenate([mixed[-2:], mixed[:-2]], 0)
    tap_one = jnp.where(is_first, came_one, back_one) * keep_one
    tap_two = jnp.where(is_first, came_two, jnp.where(is_second, came_one, back_two)) * keep_two
    convolved = conv_weight[0] * tap_two + conv_weight[1] * tap_one + conv_weight[2] * mixed
    gated = (c_part * convolved).astype(LOW)
    branch = sum_rows(dot(gated, out_weight, ((1,), (0,))).astype(LOW))
    middle = hidden[:mine] + branch
    inv_second = lax.rsqrt(jnp.mean(middle * middle, axis=1, keepdims=True) + EPS)
    unit_second = middle * inv_second
    normed_two = gather_rows((unit_second * ffn_gain).astype(LOW))

    out_grad_turned = turn(out_grad, start)
    grad_low = out_grad_turned.astype(LOW)
    grad_active = dot(grad_low, down_weight, ((1,), (1,)))
    gate_up = dot(normed_two, w_gu, ((1,), (0,)))
    hidden_units = down_weight.shape[0]
    gate_val = gate_up[:, :hidden_units]
    upper_val = gate_up[:, hidden_units:]
    sigma = jax.nn.sigmoid(gate_val)
    active = (gate_val * sigma * upper_val).astype(LOW)
    grad_gate = grad_active * upper_val * sigma * (1.0 + gate_val * (1.0 - sigma))
    grad_upper = grad_active * gate_val * sigma
    grad_gu = jnp.concatenate([grad_gate.astype(LOW), grad_upper.astype(LOW)], axis=1)
    grad_normed_two = sum_rows(dot(grad_gu, w_gu, ((1,), (1,))).astype(LOW))
    ffn_gain_part = jnp.sum(grad_normed_two * unit_second, axis=0)
    grad_middle = out_grad_turned[:mine] + norm_back(
        grad_normed_two * ffn_gain, unit_second, inv_second
    )
    ffn_rows = sum_rows(dot(active, down_weight, ((1,), (0,))).astype(LOW))
    hidden_out = turn(gather_rows((middle + ffn_rows).astype(LOW)), (rows - start) % rows)
    gate_up_part = dot(normed_two, grad_gu, ((0,), (0,))).astype(LOW)
    down_part = dot(grad_low, active, ((0,), (0,))).astype(LOW)
    gate_up_done = scatter_sum(gate_up_part, "xz")
    down_done = scatter_sum(down_part, "zx")

    grad_branch = gather_rows(grad_middle.astype(LOW))
    grad_gated = dot(grad_branch, out_weight, ((1,), (1,)))
    head = lax.dynamic_slice_in_dim(grad_branch, (rows - start) % rows, 8, 0)
    head_c = lax.dynamic_slice_in_dim(c_part, (rows - start) % rows, 8, 0)
    head_conv = dot(head, out_weight, ((1,), (1,))) * head_c
    first_open = seq_starts[0]
    head_one = (first_open != 0).astype(FULL)
    head_two = ((first_open != 0) & (first_open != 1)).astype(FULL)
    head_grad = jnp.concatenate(
        [
            conv_weight[0:1] * head_conv[0:1] * head_one,
            conv_weight[0:1] * head_conv[1:2] * head_two
            + conv_weight[1:2] * head_conv[0:1] * head_one,
        ],
        axis=0,
    )
    came_grad = slab_shift(head_grad, -1)
    grad_c = grad_gated * convolved
    grad_conv = grad_gated * c_part
    to_two = conv_weight[0] * grad_conv * keep_two
    to_one = conv_weight[1] * grad_conv * keep_one
    from_one = jnp.concatenate([to_one[1:], to_one[:1]], 0)
    from_two = jnp.concatenate([to_two[2:], to_two[:2]], 0)
    grad_mixed = (
        conv_weight[2] * grad_conv
        + jnp.where(is_last, came_grad[1:2], from_one)
        + jnp.where(is_last, 0.0, jnp.where(is_before_last, came_grad[0:1], from_two))
    )
    conv_part = jnp.stack(
        [
            jnp.sum(grad_conv * tap_two, axis=0),
            jnp.sum(grad_conv * tap_one, axis=0),
            jnp.sum(grad_conv * mixed, axis=0),
        ],
        axis=0,
    )
    grad_mixed = grad_mixed.astype(LOW).astype(FULL)
    grad_project = jnp.concatenate(
        [(grad_mixed * x_part).astype(LOW), grad_c.astype(LOW), (grad_mixed * b_part).astype(LOW)],
        axis=1,
    )
    grad_normed_part = dot(grad_project, w_in, ((1,), (1,)))
    mix_gain_part = jnp.sum(grad_normed_part * unit_first, axis=0)
    grad_normed = sum_rows(grad_normed_part.astype(LOW))
    hidden_grad = grad_middle + norm_back(
        grad_normed * mix_gain, unit_first[:mine], inv_first[:mine]
    )
    hidden_grad = turn(gather_rows(hidden_grad.astype(LOW)), (rows - start) % rows)
    in_out_part = jnp.concatenate(
        [
            dot(normed, grad_project, ((0,), (0,))).astype(LOW),
            dot(grad_branch, gated, ((0,), (0,))).astype(LOW),
        ],
        axis=1,
    )
    in_out_done = scatter_sum(in_out_part, "zx")
    mix_gain_grad, ffn_gain_grad = lax.psum((mix_gain_part, ffn_gain_part), ("seq", "mp"))
    conv_weight_grad = lax.psum(conv_part, "seq")
    local = in_out_done.shape[0]
    return (
        hidden_out.astype(FULL),
        hidden_grad.astype(FULL),
        mix_gain_grad,
        in_out_done[:, : 3 * channels].reshape(local, 3, channels),
        conv_weight_grad,
        in_out_done[:, 3 * channels :].T,
        ffn_gain_grad,
        gate_up_done.reshape(local, 2, hidden_units),
        down_done.T,
    )


def solution(mesh):
    placed = (
        P("seq", None),
        P(),
        P(None, None, "mp"),
        P(None, "mp"),
        P("mp", None),
        P(),
        P(None, None, "mp"),
        P("mp", None),
        P("seq"),
        P("seq", None),
    )
    return jax.shard_map(
        on_device,
        mesh=mesh,
        in_specs=placed,
        out_specs=(
            P("seq", None),
            P("seq", None),
            P(),
            P("seq", None, "mp"),
            P(None, "mp"),
            P("mp", "seq"),
            P(),
            P("seq", None, "mp"),
            P("mp", "seq"),
        ),
        check_vma=False,
    )
```

time: 628 us -> 377 us (0.60)
  waiting for transfers between devices: 409 us -> 94.2 us
  starting transfers between devices: 4.57 us -> 64.5 us
  local copies, waits for them, and re-layouts: 8.71 us -> 30.6 us
  matrix products: 44 us -> 27.7 us
  between operations: 15.1 us -> 2.27 us
    reduce_scatter x4 -> x0, waiting for transfers between devices: 217 us -> none  [the longest x1 87.3 us: on_device(): lax.psum_scatter(down_part, 'seq', scatter_dimension=1, tiled=True)]
    psum x3 -> x0, waiting for transfers between devices: 189 us -> none  [the longest x1 73.5 us: on_device(): lax.psum(jnp.dot(active, down_weight, preferred_element_type=jnp.float32)...]
    ppermute x2 -> x47, waiting for transfers between devices: 3.36 us -> 94.2 us  [the longest x18 52.7 us: scatter_sum(): came = lax.ppermute(take(low, (mine + o) % 4, axis), 'seq', shift)]
    ppermute x2 -> x47, starting transfers between devices: 4.28 us -> 64.5 us  [the longest x12 20.2 us: gather_rows(): came = {o: lax.ppermute(rows, 'mp', ring_shift(MP, -o)) for o in (1, 3, 2)}]
    dot_general x12 -> x14, matrix products: 44 us -> 27.7 us  [dot(): lax.dot_general(left, right, (contract, ((), ())), preferred_element_type...]
    convert_element_type x5 -> x15, other arithmetic: 1.22 us -> 14.3 us  [the longest x6 5.14 us: scatter_sum(): low = part.astype(LOW)]
    add x4 -> x2, other arithmetic: 10.7 us -> 0.1 us  [scatter_sum(): total = total + came.astype(FULL)]
    unnamed x53 -> x72, local copies, waits for them, and re-layouts: 8.7 us -> 17.6 us
  transfers between devices with their start and end apart: 9 -> 47, of which waited for: 8 -> 20; matrix products, arithmetic and copies ran while one was open for 6% -> 15% of each run, Pallas kernels for 0% -> 0%
where the time goes in v1:
time: 377 us; the launch traced here: 372 us
  blocking collectives  128 us (34%)
  waiting for transfers between devices  94.2 us (25%)
  starting transfers between devices  64.5 us (17%)
  local copies, waits for them, and re-layouts  30.6 us (8%)
  matrix products  27.7 us (7%)
  other arithmetic  24.6 us (7%)
    psum x1, blocking collectives, on_device(): lax.psum((mix_gain_part, ffn_gain_part), ('seq', 'mp'))  67.7 us
    psum x1, blocking collectives, on_device(): conv_weight_grad = lax.psum(conv_part, 'seq')  60.5 us
    ppermute x18, waiting for transfers between devices, scatter_sum(): came = lax.ppermute(take(low, (mine + o) % 4, axis), 'seq', shift)  52.7 us
    dot_general x14, matrix products, dot(): lax.dot_general(left, right, (contract, ((), ())), preferred_element_type...  27.7 us
    ppermute x12, waiting for transfers between devices, sum_rows(): lax.ppermute(part[o * rows:(o + 1) * rows], 'mp', ring_shift(MP, o))  25.4 us
    ppermute x12, starting transfers between devices, gather_rows(): came = {o: lax.ppermute(rows, 'mp', ring_shift(MP, -o)) for o in (1, 3, 2)}  20.2 us
    ppermute x18, starting transfers between devices, scatter_sum(): came = lax.ppermute(take(low, (mine + o) % 4, axis), 'seq', shift)  20.1 us
    ppermute x12, starting transfers between devices, sum_rows(): lax.ppermute(part[o * rows:(o + 1) * rows], 'mp', ring_shift(MP, o))  19.8 us
  transfers between devices with their start and end apart: 47, of which 20 were waited for; matrix products, arithmetic and copies ran while one was open for 15% of the time, Pallas kernels for 0%

profile of v1, /device:TPU:2, one launch (start us, length us, event | category | flops | bytes accessed | tf_op | source)
XLA Modules:
  0.0 372.0 jit_solution(1331360236886239283)
XLA Ops:
  5.0 2.6 copy.19
  19.8 3.0 collective-permute-start.3
  24.0 4.0 %collective-permute-done.1 = bf16[128,1024]{1,0:T(8,128)(2,1)S(1)} collective-permute-done((bf16[128,1024]{1,0:T(8,128)(2,1)S(1)}, bf16[128,1024]{1,0:T(8,128)(2,1)S(1)}, u32[]{:S(2)}, u32[]{:S(2)}) %collective-permute-start.1) | collective-permute-done | bytes 262176 | tf_op jit(solution)/shard_map/ppermute | solution.py:48
  28.0 6.9 %collective-permute-done.3 = bf16[128,1024]{1,0:T(8,128)(2,1)S(1)} collective-permute-done((bf16[128,1024]{1,0:T(8,128)(2,1)S(1)}, bf16[128,1024]{1,0:T(8,128)(2,1)S(1)}, u32[]{:S(2)}, u32[]{:S(2)}) %collective-permute-start.3) | collective-permute-done | bytes 262176 | tf_op jit(solution)/shard_map/ppermute | solution.py:48
  39.1 2.3 collective-permute-start.5
  42.9 5.4 %copy.23 = bf16[128,8,2,1152]{3,1,2,0:T(8,128)(2,1)} copy(bf16[128,8,2,1152]{3,2,1,0:T(2,128)(2,1)} %bitcast.151) | data formatting | bytes 9437184
  50.5 3.1 collective-permute-done.5
  53.6 5.4 %fusion.27 = f32[512,2304]{1,0:T(8,128)S(1)} fusion(bf16[1024,2304]{1,0:T(8,128)(2,1)} %bitcast.152, bf16[128,1024]{1,0:T(8,128)(2,1)} %collective-permute-done.6, bf16[128,1024]{1,0:T(8,128)(2,1)} %collective-permute-done.5, bf16[128,1024]{1,0:T(8,128)(2,1)} %collective-permute-done.4, bf16[128,1024]{1,0:T(8,128)(2,1)} %multiply_convert_fusion.5), kind=kOutput, calls=%fused_computation.98 | convolution fusion | flops 2420113408 | bytes 10485760 | tf_op jit(solution)/shard_map/dot_general | solution.py:41
  59.1 2.4 multiply_convert_fusion.1
  64.7 2.6 fusion.3
  75.2 3.9 %convolution_convert_fusion = bf16[1024,2304]{1,0:T(8,128)(2,1)S(1)} fusion(bf16[512,1152]{1,0:T(8,128)(2,1)S(1)} %get-tuple-element.53, bf16[512,1152]{1,0:T(8,128)(2,1)S(1)} %get-tuple-element.52, bf16[128,1024]{1,0:T(8,128)(2,1)} %collective-permute-done.6, bf16[128,1024]{1,0:T(8,128)(2,1)} %collective-permute-done.5, ...), kind=kOutput, calls=%fused_computation | convolution fusion | flops 2427191296 | bytes 8126464 | tf_op jit(solution)/shard_map/dot_general | solution.py:41
  89.6 5.8 %collective-permute-done.9 = bf16[128,1024]{1,0:T(8,128)(2,1)S(1)} collective-permute-done((bf16[128,1024]{1,0:T(8,128)(2,1)S(1)}, bf16[128,1024]{1,0:T(8,128)(2,1)S(1)}, u32[]{:S(2)}, u32[]{:S(2)}) %collective-permute-start.9) | collective-permute-done | bytes 262176 | tf_op jit(solution)/shard_map/ppermute | solution.py:48
  98.5 2.4 collective-permute-done.18
  101.0 5.7 %collective-permute-done.17 = bf16[128,1024]{1,0:T(8,128)(2,1)S(1)} collective-permute-done((bf16[128,1024]{1,0:T(8,128)(2,1)S(1)}, bf16[128,1024]{1,0:T(8,128)(2,1)S(1)}, u32[]{:S(2)}, u32[]{:S(2)}) %collective-permute-start.17) | collective-permute-done | bytes 262176 | tf_op jit(solution)/shard_map/ppermute | solution.py:56
  110.0 4.2 %collective-permute-start.10 = (bf16[128,1024]{1,0:T(8,128)(2,1)S(1)}, bf16[128,1024]{1,0:T(8,128)(2,1)S(1)}, u32[]{:S(2)}, u32[]{:S(2)}) collective-permute-start(bf16[128,1024]{1,0:T(8,128)(2,1)S(1)} %get-tuple-element.45), channel_id=1, source_target_pairs={{0,3},{1,0},{2,1},{3,2},{4,7},{5,4},{6,5},{7,6},{8,11},{9,8},{10,9... | collective-permute-start | bytes 786440 | tf_op jit(solution)/shard_map/ppermute | solution.py:56
  115.3 2.8 collective-permute-done.10
  125.6 60.5 %psum.22 = f32[3,256]{1,0:T(4,128)} all-reduce(f32[3,256]{1,0:T(4,128)S(1)} %pad_maximum_fusion.13), channel_id=1, replica_groups=mesh['seq'=32,'mp'=4] {'seq'}, use_global_device_ids=true, to_apply=%region_10.11 | all-reduce | flops 768 | bytes 6144 | tf_op jit(solution)/shard_map/psum | solution.py:236
  191.4 3.6 collective-permute-start.22
  196.2 4.7 %collective-permute-done.20 = bf16[128,1024]{1,0:T(8,128)(2,1)S(1)} collective-permute-done((bf16[128,1024]{1,0:T(8,128)(2,1)S(1)}, bf16[128,1024]{1,0:T(8,128)(2,1)S(1)}, u32[]{:S(2)}, u32[]{:S(2)}) %collective-permute-start.20) | collective-permute-done | bytes 262176 | tf_op jit(solution)/shard_map/ppermute | solution.py:48
  200.9 3.1 collective-permute-done.22
  210.7 2.9 copy.20
  214.7 67.7 %all-reduce = (f32[1024]{0:T(1024)}, f32[1024]{0:T(1024)}) all-reduce(f32[1024]{0:T(1024)S(1)} %get-tuple-element.58, f32[1024]{0:T(1024)S(1)} %get-tuple-element.18), channel_id=1, replica_groups=mesh['seq'=32,'mp'=4] {'seq','mp'}, use_global_device_ids=true, to_apply=%region_6.7 | all-reduce | flops 2048 | bytes 16384 | tf_op jit(solution)/shard_map/psum | solution.py:235
  287.6 2.8 dynamic-slice_convert_fusion
  292.3 2.6 collective-permute-start.43
  297.5 12.0 %collective-permute-done.41 = bf16[4,32,1152]{2,1,0:T(8,128)(2,1)S(1)} collective-permute-done((bf16[4,32,1152]{2,1,0:T(8,128)(2,1)S(1)}, bf16[4,32,1152]{2,1,0:T(8,128)(2,1)S(1)}, u32[]{:S(2)}, u32[]{:S(2)}) %collective-permute-start.41) | collective-permute-done | bytes 294944 | tf_op jit(solution)/shard_map/ppermute | solution.py:78
  311.6 8.8 %collective-permute-done.27 = bf16[4,32,1024]{2,1,0:T(8,128)(2,1)S(1)} collective-permute-done((bf16[4,32,1024]{2,1,0:T(8,128)(2,1)S(1)}, bf16[4,32,1024]{2,1,0:T(8,128)(2,1)S(1)}, u32[]{:S(2)}, u32[]{:S(2)}) %collective-permute-start.27) | collective-permute-done | bytes 262176 | tf_op jit(solution)/shard_map/ppermute | solution.py:78
  324.8 2.7 collective-permute-start.32
  327.5 2.4 fusion.53
  335.0 9.2 %collective-permute-done.31 = bf16[32,1024]{1,0:T(8,128)(2,1)S(1)} collective-permute-done((bf16[32,1024]{1,0:T(8,128)(2,1)S(1)}, bf16[32,1024]{1,0:T(8,128)(2,1)S(1)}, u32[]{:S(2)}, u32[]{:S(2)}) %collective-permute-start.31) | collective-permute-done | bytes 65568 | tf_op jit(solution)/shard_map/ppermute | solution.py:78
  346.5 3.4 collective-permute-done.36
  349.9 9.7 %collective-permute-done.35 = bf16[4,32,2304]{2,1,0:T(8,128)(2,1)S(1)} collective-permute-done((bf16[4,32,2304]{2,1,0:T(8,128)(2,1)S(1)}, bf16[4,32,2304]{2,1,0:T(8,128)(2,1)S(1)}, u32[]{:S(2)}, u32[]{:S(2)}) %collective-permute-start.35) | collective-permute-done | bytes 589856 | tf_op jit(solution)/shard_map/ppermute | solution.py:78
  363.9 6.3 %collective-permute-done.37 = bf16[32,2304]{1,0:T(8,128)(2,1)S(1)} collective-permute-done((bf16[32,2304]{1,0:T(8,128)(2,1)S(1)}, bf16[32,2304]{1,0:T(8,128)(2,1)S(1)}, u32[]{:S(2)}, u32[]{:S(2)}) %collective-permute-start.37) | collective-permute-done | bytes 147488 | tf_op jit(solution)/shard_map/ppermute | solution.py:78
  (225 shorter events, 104.7 us)
Async XLA Ops:
  19.8 15.2 %collective-permute-start.3 = (bf16[128,1024]{1,0:T(8,128)(2,1)S(1)}, bf16[128,1024]{1,0:T(8,128)(2,1)S(1)}, u32[]{:S(2)}, u32[]{:S(2)}) collective-permute-start(bf16[128,1024]{1,0:T(8,128)(2,1)S(1)} %get-tuple-element.77), channel_id=1, source_target_pairs={{0,2},{1,3},{2,0},{3,1},{4,6},{5,7},{6,4},{7,5},{8,10},{9,11},{10,... | collective-permute-start | bytes 786440 | tf_op jit(solution)/shard_map/ppermute | solution.py:48
  37.1 13.4 %collective-permute-start.6 = (bf16[128,1024]{1,0:T(8,128)(2,1)}, bf16[128,1024]{1,0:T(8,128)(2,1)}, u32[]{:S(2)}, u32[]{:S(2)}) collective-permute-start(bf16[128,1024]{1,0:T(8,128)(2,1)} %multiply_convert_fusion.5), channel_id=1, source_target_pairs={{0,1},{1,2},{2,3},{3,0},{4,5},{5,6},{6,7},{7,4},{8,9},{9,10},{10,1... | collective-permute-start | bytes 786440 | tf_op jit(solution)/shard_map/ppermute | solution.py:56
  39.1 14.5 %collective-permute-start.5 = (bf16[128,1024]{1,0:T(8,128)(2,1)}, bf16[128,1024]{1,0:T(8,128)(2,1)}, u32[]{:S(2)}, u32[]{:S(2)}) collective-permute-start(bf16[128,1024]{1,0:T(8,128)(2,1)} %multiply_convert_fusion.5), channel_id=1, source_target_pairs={{0,2},{1,3},{2,0},{3,1},{4,6},{5,7},{6,4},{7,5},{8,10},{9,11},{10,... | collective-permute-start | bytes 786440 | tf_op jit(solution)/shard_map/ppermute | solution.py:56
  67.4 15.9 %collective-permute-start.13 = (bf16[128,1024]{1,0:T(8,128)(2,1)S(1)}, bf16[128,1024]{1,0:T(8,128)(2,1)S(1)}, u32[]{:S(2)}, u32[]{:S(2)}) collective-permute-start(bf16[128,1024]{1,0:T(8,128)(2,1)S(1)} %get-tuple-element.70), channel_id=1, source_target_pairs={{0,1},{1,2},{2,3},{3,0},{4,5},{5,6},{6,7},{7,4},{8,9},{9,10},{10,1... | collective-permute-start | bytes 786440 | tf_op jit(solution)/shard_map/ppermute | solution.py:48
  69.1 15.7 %collective-permute-start.15 = (bf16[128,1024]{1,0:T(8,128)(2,1)S(1)}, bf16[128,1024]{1,0:T(8,128)(2,1)S(1)}, u32[]{:S(2)}, u32[]{:S(2)}) collective-permute-start(bf16[128,1024]{1,0:T(8,128)(2,1)S(1)} %get-tuple-element.71), channel_id=1, source_target_pairs={{0,2},{1,3},{2,0},{3,1},{4,6},{5,7},{6,4},{7,5},{8,10},{9,11},{10,... | collective-permute-start | bytes 786440 | tf_op jit(solution)/shard_map/ppermute | solution.py:48
  71.4 13.5 %collective-permute-start.14 = (bf16[128,1024]{1,0:T(8,128)(2,1)S(1)}, bf16[128,1024]{1,0:T(8,128)(2,1)S(1)}, u32[]{:S(2)}, u32[]{:S(2)}) collective-permute-start(bf16[128,1024]{1,0:T(8,128)(2,1)S(1)} %get-tuple-element.72), channel_id=1, source_target_pairs={{0,3},{1,0},{2,1},{3,2},{4,7},{5,4},{6,5},{7,6},{8,11},{9,8},{10,9... | collective-permute-start | bytes 786440 | tf_op jit(solution)/shard_map/ppermute | solution.py:48
  72.8 14.9 %collective-permute-start.7 = (bf16[128,1024]{1,0:T(8,128)(2,1)S(1)}, bf16[128,1024]{1,0:T(8,128)(2,1)S(1)}, u32[]{:S(2)}, u32[]{:S(2)}) collective-permute-start(bf16[128,1024]{1,0:T(8,128)(2,1)S(1)} %get-tuple-element.73), channel_id=1, source_target_pairs={{0,1},{1,2},{2,3},{3,0},{4,5},{5,6},{6,7},{7,4},{8,9},{9,10},{10,1... | collective-permute-start | bytes 786440 | tf_op jit(solution)/shard_map/ppermute | solution.py:48
  73.5 21.9 %collective-permute-start.9 = (bf16[128,1024]{1,0:T(8,128)(2,1)S(1)}, bf16[128,1024]{1,0:T(8,128)(2,1)S(1)}, u32[]{:S(2)}, u32[]{:S(2)}) collective-permute-start(bf16[128,1024]{1,0:T(8,128)(2,1)S(1)} %get-tuple-element.74), channel_id=1, source_target_pairs={{0,2},{1,3},{2,0},{3,1},{4,6},{5,7},{6,4},{7,5},{8,10},{9,11},{10,... | collective-permute-start | bytes 786440 | tf_op jit(solution)/shard_map/ppermute | solution.py:48
  83.3 13.5 %collective-permute-start.8 = (bf16[128,1024]{1,0:T(8,128)(2,1)S(1)}, bf16[128,1024]{1,0:T(8,128)(2,1)S(1)}, u32[]{:S(2)}, u32[]{:S(2)}) collective-permute-start(bf16[128,1024]{1,0:T(8,128)(2,1)S(1)} %get-tuple-element.75), channel_id=1, source_target_pairs={{0,3},{1,0},{2,1},{3,2},{4,7},{5,4},{6,5},{7,6},{8,11},{9,8},{10,9... | collective-permute-start | bytes 786440 | tf_op jit(solution)/shard_map/ppermute | solution.py:48
  84.8 205.6 %collective-permute-start.40 = (bf16[4,4,32,1152]{3,2,1,0:T(8,128)(2,1)}, bf16[4,4,32,1152]{3,2,1,0:T(8,128)(2,1)}, u32[]{:S(2)}, u32[]{:S(2)}) collective-permute-start(bf16[4,4,32,1152]{3,2,1,0:T(8,128)(2,1)} %dynamic-slice_bitcast_fusion.1), channel_id=1, source_target_pairs={{0,4},{4,0},{8,12},{12,8},{16,20},{20,16},{24,28},{28,24},{32,36},... | collective-permute-start | bytes 3538952 | tf_op jit(solution)/shard_map/ppermute | solution.py:69
  84.9 239.9 %collective-permute-start.33 = (bf16[4,4,32,2304]{3,2,1,0:T(8,128)(2,1)}, bf16[4,4,32,2304]{3,2,1,0:T(8,128)(2,1)}, u32[]{:S(2)}, u32[]{:S(2)}) collective-permute-start(bf16[4,4,32,2304]{3,2,1,0:T(8,128)(2,1)} %dynamic-slice_bitcast_fusion), channel_id=1, source_target_pairs={{0,4},{4,0},{8,12},{12,8},{16,20},{20,16},{24,28},{28,24},{32,36},... | collective-permute-start | bytes 7077896 | tf_op jit(solution)/shard_map/ppermute | solution.py:69
  87.6 13.4 %collective-permute-start.18 = (bf16[128,1024]{1,0:T(8,128)(2,1)S(1)}, bf16[128,1024]{1,0:T(8,128)(2,1)S(1)}, u32[]{:S(2)}, u32[]{:S(2)}) collective-permute-start(bf16[128,1024]{1,0:T(8,128)(2,1)S(1)} %get-tuple-element.42), channel_id=1, source_target_pairs={{0,1},{1,2},{2,3},{3,0},{4,5},{5,6},{6,7},{7,4},{8,9},{9,10},{10,1... | collective-permute-start | bytes 786440 | tf_op jit(solution)/shard_map/ppermute | solution.py:56
  96.8 13.2 %collective-permute-start.16 = (bf16[128,1024]{1,0:T(8,128)(2,1)S(1)}, bf16[128,1024]{1,0:T(8,128)(2,1)S(1)}, u32[]{:S(2)}, u32[]{:S(2)}) collective-permute-start(bf16[128,1024]{1,0:T(8,128)(2,1)S(1)} %get-tuple-element.42), channel_id=1, source_target_pairs={{0,3},{1,0},{2,1},{3,2},{4,7},{5,4},{6,5},{7,6},{8,11},{9,8},{10,9... | collective-permute-start | bytes 786440 | tf_op jit(solution)/shard_map/ppermute | solution.py:56
  101.0 21.8 %collective-permute-start.12 = (bf16[128,1024]{1,0:T(8,128)(2,1)S(1)}, bf16[128,1024]{1,0:T(8,128)(2,1)S(1)}, u32[]{:S(2)}, u32[]{:S(2)}) collective-permute-start(bf16[128,1024]{1,0:T(8,128)(2,1)S(1)} %get-tuple-element.45), channel_id=1, source_target_pairs={{0,1},{1,2},{2,3},{3,0},{4,5},{5,6},{6,7},{7,4},{8,9},{9,10},{10,1... | collective-permute-start | bytes 786440 | tf_op jit(solution)/shard_map/ppermute | solution.py:56
  106.7 14.8 %collective-permute-start.11 = (bf16[128,1024]{1,0:T(8,128)(2,1)S(1)}, bf16[128,1024]{1,0:T(8,128)(2,1)S(1)}, u32[]{:S(2)}, u32[]{:S(2)}) collective-permute-start(bf16[128,1024]{1,0:T(8,128)(2,1)S(1)} %get-tuple-element.45), channel_id=1, source_target_pairs={{0,2},{1,3},{2,0},{3,1},{4,6},{5,7},{6,4},{7,5},{8,10},{9,11},{10,... | collective-permute-start | bytes 786440 | tf_op jit(solution)/shard_map/ppermute | solution.py:56
  118.1 68.1 %collective-permute-start.19 = (f32[2,256]{1,0:T(2,128)S(1)}, f32[2,256]{1,0:T(2,128)S(1)}, u32[]{:S(2)}, u32[]{:S(2)}) collective-permute-start(f32[2,256]{1,0:T(2,128)S(1)} %pad_maximum_fusion.14), channel_id=1, source_target_pairs={{4,0},{8,4},{12,8},{16,12},{20,16},{24,20},{28,24},{32,28},{36,32}... | collective-permute-start | bytes 6152 | tf_op jit(solution)/shard_map/ppermute | solution.py:37
  191.4 12.6 %collective-permute-start.22 = (bf16[128,1024]{1,0:T(8,128)(2,1)S(1)}, bf16[128,1024]{1,0:T(8,128)(2,1)S(1)}, u32[]{:S(2)}, u32[]{:S(2)}) collective-permute-start(bf16[128,1024]{1,0:T(8,128)(2,1)S(1)} %get-tuple-element.68), channel_id=1, source_target_pairs={{0,2},{1,3},{2,0},{3,1},{4,6},{5,7},{6,4},{7,5},{8,10},{9,11},{10,... | collective-permute-start | bytes 786440 | tf_op jit(solution)/shard_map/ppermute | solution.py:48
  205.3 78.0 %collective-permute-start.24 = (bf16[128,1024]{1,0:T(8,128)(2,1)S(1)}, bf16[128,1024]{1,0:T(8,128)(2,1)S(1)}, u32[]{:S(2)}, u32[]{:S(2)}) collective-permute-start(bf16[128,1024]{1,0:T(8,128)(2,1)S(1)} %get-tuple-element.39), channel_id=1, source_target_pairs={{0,2},{1,3},{2,0},{3,1},{4,6},{5,7},{6,4},{7,5},{8,10},{9,11},{10,... | collective-permute-start | bytes 786440 | tf_op jit(solution)/shard_map/ppermute | solution.py:56
  207.2 75.3 %collective-permute-start.23 = (bf16[128,1024]{1,0:T(8,128)(2,1)S(1)}, bf16[128,1024]{1,0:T(8,128)(2,1)S(1)}, u32[]{:S(2)}, u32[]{:S(2)}) collective-permute-start(bf16[128,1024]{1,0:T(8,128)(2,1)S(1)} %get-tuple-element.39), channel_id=1, source_target_pairs={{0,3},{1,0},{2,1},{3,2},{4,7},{5,4},{6,5},{7,6},{8,11},{9,8},{10,9... | collective-permute-start | bytes 786440 | tf_op jit(solution)/shard_map/ppermute | solution.py:56
  213.6 70.4 %collective-permute-start.25 = (bf16[128,1024]{1,0:T(8,128)(2,1)S(1)}, bf16[128,1024]{1,0:T(8,128)(2,1)S(1)}, u32[]{:S(2)}, u32[]{:S(2)}) collective-permute-start(bf16[128,1024]{1,0:T(8,128)(2,1)S(1)} %get-tuple-element.39), channel_id=1, source_target_pairs={{0,1},{1,2},{2,3},{3,0},{4,5},{5,6},{6,7},{7,4},{8,9},{9,10},{10,1... | collective-permute-start | bytes 786440 | tf_op jit(solution)/shard_map/ppermute | solution.py:56
  282.4 13.9 %collective-permute-start.26 = (bf16[4,4,32,1024]{3,2,1,0:T(8,128)(2,1)}, bf16[4,4,32,1024]{3,2,1,0:T(8,128)(2,1)S(1)}, u32[]{:S(2)}, u32[]{:S(2)}) collective-permute-start(bf16[4,4,32,1024]{3,2,1,0:T(8,128)(2,1)} %dynamic-slice_bitcast_fusion.2), channel_id=1, source_target_pairs={{0,4},{4,0},{8,12},{12,8},{16,20},{20,16},{24,28},{28,24},{32,36},... | collective-permute-start | bytes 3145736 | tf_op jit(solution)/shard_map/ppermute | solution.py:69
  292.2 17.4 %collective-permute-start.41 = (bf16[4,32,1152]{2,1,0:T(8,128)(2,1)S(1)}, bf16[4,32,1152]{2,1,0:T(8,128)(2,1)S(1)}, u32[]{:S(2)}, u32[]{:S(2)}) collective-permute-start(bf16[4,32,1152]{2,1,0:T(8,128)(2,1)S(1)} %get-tuple-element.61), channel_id=1, source_target_pairs={{0,32},{4,36},{8,40},{12,44},{16,48},{20,52},{24,56},{28,60},{32,6... | collective-permute-start | bytes 884744 | tf_op jit(solution)/shard_map/ppermute | solution.py:78
  292.3 17.3 %collective-permute-start.43 = (bf16[4,32,1152]{2,1,0:T(8,128)(2,1)S(1)}, bf16[4,32,1152]{2,1,0:T(8,128)(2,1)S(1)}, u32[]{:S(2)}, u32[]{:S(2)}) collective-permute-start(bf16[4,32,1152]{2,1,0:T(8,128)(2,1)S(1)} %get-tuple-element.62), channel_id=1, source_target_pairs={{0,64},{4,68},{8,72},{12,76},{16,80},{20,84},{24,88},{28,92},{32,9... | collective-permute-start | bytes 884744 | tf_op jit(solution)/shard_map/ppermute | solution.py:78
  294.9 15.6 %collective-permute-start.42 = (bf16[4,32,1152]{2,1,0:T(8,128)(2,1)S(1)}, bf16[4,32,1152]{2,1,0:T(8,128)(2,1)S(1)}, u32[]{:S(2)}, u32[]{:S(2)}) collective-permute-start(bf16[4,32,1152]{2,1,0:T(8,128)(2,1)S(1)} %get-tuple-element.63), channel_id=1, source_target_pairs={{0,96},{4,100},{8,104},{12,108},{16,112},{20,116},{24,120},{28,124... | collective-permute-start | bytes 884744 | tf_op jit(solution)/shard_map/ppermute | solution.py:78
  296.9 23.5 %collective-permute-start.27 = (bf16[4,32,1024]{2,1,0:T(8,128)(2,1)S(1)}, bf16[4,32,1024]{2,1,0:T(8,128)(2,1)S(1)}, u32[]{:S(2)}, u32[]{:S(2)}) collective-permute-start(bf16[4,32,1024]{2,1,0:T(8,128)(2,1)S(1)} %get-tuple-element.64), channel_id=1, source_target_pairs={{0,32},{4,36},{8,40},{12,44},{16,48},{20,52},{24,56},{28,60},{32,6... | collective-permute-start | bytes 786440 | tf_op jit(solution)/shard_map/ppermute | solution.py:78
  309.6 12.9 %collective-permute-start.29 = (bf16[4,32,1024]{2,1,0:T(8,128)(2,1)S(1)}, bf16[4,32,1024]{2,1,0:T(8,128)(2,1)S(1)}, u32[]{:S(2)}, u32[]{:S(2)}) collective-permute-start(bf16[4,32,1024]{2,1,0:T(8,128)(2,1)S(1)} %get-tuple-element.65), channel_id=1, source_target_pairs={{0,64},{4,68},{8,72},{12,76},{16,80},{20,84},{24,88},{28,92},{32,9... | collective-permute-start | bytes 786440 | tf_op jit(solution)/shard_map/ppermute | solution.py:78
  309.6 13.7 %collective-permute-start.28 = (bf16[4,32,1024]{2,1,0:T(8,128)(2,1)S(1)}, bf16[4,32,1024]{2,1,0:T(8,128)(2,1)S(1)}, u32[]{:S(2)}, u32[]{:S(2)}) collective-permute-start(bf16[4,32,1024]{2,1,0:T(8,128)(2,1)S(1)} %get-tuple-element.66), channel_id=1, source_target_pairs={{0,96},{4,100},{8,104},{12,108},{16,112},{20,116},{24,120},{28,124... | collective-permute-start | bytes 786440 | tf_op jit(solution)/shard_map/ppermute | solution.py:78
  310.7 19.3 %collective-permute-start.44 = (bf16[32,1152]{1,0:T(8,128)(2,1)S(1)}, bf16[32,1152]{1,0:T(8,128)(2,1)S(1)}, u32[]{:S(2)}, u32[]{:S(2)}) collective-permute-start(bf16[32,1152]{1,0:T(8,128)(2,1)S(1)} %get-tuple-element.85), channel_id=1, source_target_pairs={{0,8},{4,12},{8,16},{12,20},{16,24},{20,28},{24,0},{28,4},{32,40},... | collective-permute-start | bytes 221192 | tf_op jit(solution)/shard_map/ppermute | solution.py:78
  330.1 14.1 %collective-permute-start.31 = (bf16[32,1024]{1,0:T(8,128)(2,1)S(1)}, bf16[32,1024]{1,0:T(8,128)(2,1)S(1)}, u32[]{:S(2)}, u32[]{:S(2)}) collective-permute-start(bf16[32,1024]{1,0:T(8,128)(2,1)S(1)} %get-tuple-element.90), channel_id=1, source_target_pairs={{0,24},{4,28},{8,0},{12,4},{16,8},{20,12},{24,16},{28,20},{32,56},... | collective-permute-start | bytes 196616 | tf_op jit(solution)/shard_map/ppermute | solution.py:78
  330.2 16.3 %collective-permute-start.34 = (bf16[4,32,2304]{2,1,0:T(8,128)(2,1)S(1)}, bf16[4,32,2304]{2,1,0:T(8,128)(2,1)S(1)}, u32[]{:S(2)}, u32[]{:S(2)}) collective-permute-start(bf16[4,32,2304]{2,1,0:T(8,128)(2,1)S(1)} %get-tuple-element.55), channel_id=1, source_target_pairs={{0,8},{4,12},{8,16},{12,20},{16,24},{20,28},{24,0},{28,4},{32,40},... | collective-permute-start | bytes 1769480 | tf_op jit(solution)/shard_map/ppermute | solution.py:78
  332.2 17.8 %collective-permute-start.36 = (bf16[4,32,2304]{2,1,0:T(8,128)(2,1)S(1)}, bf16[4,32,2304]{2,1,0:T(8,128)(2,1)S(1)}, u32[]{:S(2)}, u32[]{:S(2)}) collective-permute-start(bf16[4,32,2304]{2,1,0:T(8,128)(2,1)S(1)} %get-tuple-element.56), channel_id=1, source_target_pairs={{0,16},{4,20},{8,24},{12,28},{16,0},{20,4},{24,8},{28,12},{32,48},... | collective-permute-start | bytes 1769480 | tf_op jit(solution)/shard_map/ppermute | solution.py:78
  334.2 25.5 %collective-permute-start.35 = (bf16[4,32,2304]{2,1,0:T(8,128)(2,1)S(1)}, bf16[4,32,2304]{2,1,0:T(8,128)(2,1)S(1)}, u32[]{:S(2)}, u32[]{:S(2)}) collective-permute-start(bf16[4,32,2304]{2,1,0:T(8,128)(2,1)S(1)} %get-tuple-element.57), channel_id=1, source_target_pairs={{0,24},{4,28},{8,0},{12,4},{16,8},{20,12},{24,16},{28,20},{32,56},... | collective-permute-start | bytes 1769480 | tf_op jit(solution)/shard_map/ppermute | solution.py:78
  (45 other events, 560.0 us)

commit v2 on v0

v2 whole, which is shorter than its diff:
```python
import functools
import math

import jax
import jax.numpy as jnp
from jax import lax
from jax.experimental import pallas as pl
from jax.experimental.pallas import tpu as pltpu
from jax.sharding import PartitionSpec as P

EPS = 1e-05
LOW = jnp.bfloat16
FULL = jnp.float32
MP = 4
X_DIM = 4
ORDER = (0, 1, 3, 2)
Z_DIM = 4


def ring_shift(size, by):
    return [(i, (i + by) % size) for i in range(size)]


def seq_index(z, x, core):
    return (z * X_DIM + x) * 2 + core


def seq_shift(dz, dx, flip):
    return [
        (
            seq_index(z, x, core),
            seq_index((z + dz) % Z_DIM, (x + dx) % X_DIM, core ^ flip),
        )
        for z in range(Z_DIM)
        for x in range(X_DIM)
        for core in range(2)
    ]


def slab_shift(value, by):
    devices = lax.axis_size("seq")
    pairs = [(i, i + by) for i in range(devices) if 0 <= i + by < devices]
    return lax.ppermute(value, "seq", pairs)


def head_spread(value):
    devices = lax.axis_size("seq")
    came = 0
    for j in range(MP):
        pairs = [(s * MP, (s - 1) * MP + j) for s in range(1, devices)]
        came = came + lax.ppermute(value, ("seq", "mp"), pairs)
    return came


def dot(left, right, contract=((1,), (0,))):
    return lax.dot_general(left, right, (contract, ((), ())), preferred_element_type=FULL)


BY_ROWS = ((1,), (1,))
OVER_TOKENS = ((0,), (0,))


def send_rows(parts):
    return {o: lax.ppermute(parts[o], "mp", ring_shift(MP, o)) for o in (2, 1, 3)}


def gather_rows(rows, order=(2, 1, 3)):
    return {o: lax.ppermute(rows, "mp", ring_shift(MP, -o)) for o in order}


def take(value, index, axis):
    return lax.dynamic_index_in_dim(value, index, axis, keepdims=False)


def seq_place():
    me = lax.axis_index("seq")
    return me % 2, (me // 2) % X_DIM, me // (2 * X_DIM)


def line_sum(part, name):
    _, x, z = seq_place()
    mine = x if name == "x" else z
    total = take(part, mine, 0).astype(FULL)
    for o in (2, 1, 3):
        shift = seq_shift(0, o, 0) if name == "x" else seq_shift(o, 0, 0)
        came = lax.ppermute(take(part, (mine + o) % 4, 0).astype(LOW), "seq", shift)
        total = total + came.astype(FULL)
    return total


def all_sum(value):
    value = value + lax.ppermute(value, "seq", seq_shift(0, 0, 1))
    for dz, dx in ((0, 1), (1, 0)):
        shifts = [seq_shift(dz * o, dx * o, 0) for o in (2, 1, 3)]
        value = value + sum(lax.ppermute(value, "seq", shift) for shift in shifts)
    return value


def chip_line_scatter(part):
    groups = [
        [seq_index(z, x, core) for x in range(X_DIM) for core in range(2)] for z in range(Z_DIM)
    ]
    return lax.psum_scatter(
        part, "seq", scatter_dimension=0, axis_index_groups=groups, tiled=True
    )


def after(values, *others):
    return lax.optimization_barrier((values, others))[0]


def turn(value, by):
    rows = value.shape[0]
    return lax.dynamic_slice_in_dim(jnp.concatenate([value, value], 0), by, rows, 0)


def inv_rms(values):
    return lax.rsqrt(jnp.mean(values * values, axis=1, keepdims=True) + EPS)


def norm_back(grad_unit, unit_rows, inv_rows):
    return inv_rows * (
        grad_unit - unit_rows * jnp.mean(grad_unit * unit_rows, axis=1, keepdims=True)
    )


def whole(shape):
    return pl.BlockSpec(shape, lambda i, s, t: (0,) * len(shape))


def quarter(o, rows, width):
    return pl.BlockSpec((rows, width), lambda i, s, t: ((s[0] + o) % MP, 0))


def call(kernel, place, inputs, outs, grid=1, vmem=0, scratch=()):
    in_specs = [spec or whole(array.shape) for array, spec in inputs]
    out_specs = [spec or whole(shape) for shape, _, spec in outs]
    held = 0
    for (array, _), spec in zip(inputs, in_specs):
        held += math.prod(spec.block_shape) * array.dtype.itemsize
    for (_, dtype, _), spec in zip(outs, out_specs):
        held += math.prod(spec.block_shape) * jnp.dtype(dtype).itemsize
    return pl.pallas_call(
        kernel,
        grid_spec=pltpu.PrefetchScalarGridSpec(
            num_scalar_prefetch=2, grid=(grid,), in_specs=in_specs, out_specs=out_specs,
            scratch_shapes=scratch,
        ),
        out_shape=[jax.ShapeDtypeStruct(shape, dtype) for shape, dtype, _ in outs],
        compiler_params=pltpu.CompilerParams(vmem_limit_bytes=vmem or 2 * held + (8 << 20)),
        cost_estimate=pl.CostEstimate(flops=0, bytes_accessed=0, transcendentals=0),
    )(*place, *[array for array, _ in inputs])


def places(s_ref, rows, columns):
    row = lax.broadcasted_iota(jnp.int32, (rows, columns), 0) + s_ref[0] * (rows // MP)
    return jnp.where(row >= rows, row - rows, row)


def taps(s_ref, t_ref, mixed, tail_mixed):
    rows, columns = mixed.shape
    place = places(s_ref, rows, columns)
    keep_one = place != t_ref[0]
    keep_two = keep_one & (place != t_ref[0] + 1)
    back_one = pltpu.roll(mixed, 1, 0)
    back_two = pltpu.roll(mixed, 2, 0)
    last = tail_mixed[7:8]
    before_last = tail_mixed[6:7]
    tap_one = jnp.where(keep_one, jnp.where(place == 0, last, back_one), 0.0)
    tap_two = jnp.where(
        keep_two, jnp.where(place == 0, before_last, jnp.where(place == 1, last, back_two)), 0.0
    )
    return place, keep_one, keep_two, tap_one, tap_two


def mix_kernel(
    s_ref, t_ref, h0_ref, h1_ref, h2_ref, h3_ref, tail_ref, gain_ref, w_ref, conv_ref, out_ref,
    normed_ref, b_ref, c_ref, x_ref,
    gated_ref, convolved_ref, tail_mixed_ref, p0_ref, p1_ref, p2_ref, p3_ref,
):
    gain = gain_ref[...]
    rows = p0_ref.shape[0]
    for o, ref in enumerate((h0_ref, h1_ref, h2_ref, h3_ref)):
        hidden = ref[...]
        normed_ref[o * rows : (o + 1) * rows, :] = (hidden * inv_rms(hidden) * gain).astype(LOW)
    normed = normed_ref[...]
    parts = [dot(normed, w_ref[k]) for k in range(3)]
    for part, ref in zip(parts, (b_ref, c_ref, x_ref)):
        ref[...] = part
    tail = tail_ref[...]
    tail = (tail * inv_rms(tail) * gain).astype(LOW)
    tail_mixed = (dot(tail, w_ref[0]) * dot(tail, w_ref[2])).astype(LOW).astype(FULL)
    tail_mixed_ref[...] = tail_mixed
    mixed = (parts[0] * parts[2]).astype(LOW).astype(FULL)
    _, _, _, tap_one, tap_two = taps(s_ref, t_ref, mixed, tail_mixed)
    conv = conv_ref[...]
    convolved = conv[0:1] * tap_two + conv[1:2] * tap_one + conv[2:3] * mixed
    convolved_ref[...] = convolved
    gated = (parts[1] * convolved).astype(LOW)
    gated_ref[...] = gated
    branch = dot(gated, out_ref[...])
    for o, ref in enumerate((p0_ref, p1_ref, p2_ref, p3_ref)):
        ref[...] = branch[o * rows : (o + 1) * rows].astype(ref.dtype)


def middle_kernel(s_ref, t_ref, hidden_ref, p0_ref, r1_ref, r2_ref, r3_ref, middle_ref, low_ref):
    total = hidden_ref[...] + p0_ref[...]
    for ref in (r1_ref, r2_ref, r3_ref):
        total = total + ref[...].astype(FULL)
    middle_ref[...] = total
    low_ref[...] = total.astype(LOW)


def slabs_of(part, order):
    return jnp.concatenate([part[i * 32 : (i + 1) * 32] for i in order], 0)


BIG = 60 << 20
SCATTER_ORDER = [
    seq_index(z, x, core) for x in range(X_DIM) for core in range(2) for z in range(Z_DIM)
]


def ffn_grad_kernel(
    steps, s_ref, t_ref, normed_ref, grad_gu_ref, low_ref, active_ref, part_ref, turned_ref
):
    step = pl.program_id(0)

    @pl.when(step == 0)
    def _():
        turned_ref[...] = jnp.transpose(normed_ref[...])

    @pl.when(step == steps)
    def _():
        turned_ref[...] = jnp.transpose(low_ref[...])

    @pl.when(step < steps)
    def _():
        part_ref[...] = slabs_of(dot(turned_ref[...], grad_gu_ref[...]).astype(LOW), SCATTER_ORDER)

    @pl.when(step >= steps)
    def _():
        part_ref[...] = slabs_of(dot(turned_ref[...], active_ref[...]).astype(LOW), SCATTER_ORDER)


def ffn_out_kernel(s_ref, t_ref, active_ref, down_ref, out_ref):
    part = dot(active_ref[...], down_ref[...]).astype(LOW)
    rows = part.shape[0] // MP
    for i, o in enumerate(ORDER):
        place = lax.rem(s_ref[0] + o, MP) * rows
        out_ref[pl.ds(pl.multiple_of(place, rows), rows), :] = part[i * rows : (i + 1) * rows]


def place_kernel(s_ref, t_ref, c0_ref, c1_ref, c2_ref, c3_ref, out_ref):
    for o, ref in enumerate((c0_ref, c1_ref, c2_ref, c3_ref)):

        @pl.when(pl.program_id(0) == o)
        def _():
            out_ref[...] = ref[...].astype(FULL)


def place_add_kernel(s_ref, t_ref, c0_ref, c1_ref, c2_ref, c3_ref, more_ref, out_ref):
    for o, ref in enumerate((c0_ref, c1_ref, c2_ref, c3_ref)):

        @pl.when(pl.program_id(0) == o)
        def _():
            out_ref[...] = ref[...].astype(FULL) + more_ref[...].astype(FULL)


def branch_kernel(
    s_ref, t_ref, p0_ref, r1_ref, r2_ref, r3_ref, middle_ref, gain_ref, out_grad_ref,
    grad_ref, low_ref, gain_part_ref,
):
    total = p0_ref[...].astype(FULL)
    for ref in (r1_ref, r2_ref, r3_ref):
        total = total + ref[...].astype(FULL)
    middle = middle_ref[...]
    inv = inv_rms(middle)
    unit = middle * inv
    gain_part_ref[...] = jnp.sum(total * unit, axis=0, keepdims=True)
    grad = out_grad_ref[...] + norm_back(total * gain_ref[...], unit, inv)
    grad_ref[...] = grad
    low_ref[...] = grad.astype(LOW)


def mix_back_kernel(
    s_ref, t_ref, g0_ref, g1_ref, g2_ref, g3_ref, gated_ref, head_ref, head_c_ref, b_ref, c_ref, x_ref,
    convolved_ref, tail_mixed_ref, conv_ref, out_ref, w_ref, normed_ref, gain_ref,
    ffn_gain_ref, part_ref, conv_part_ref, p0_ref, p1_ref, p2_ref, p3_ref,
):
    out_weight = out_ref[...]
    conv = conv_ref[...]
    grad_gated = jnp.concatenate(
        [dot(ref[...], out_weight, BY_ROWS) for ref in (g0_ref, g1_ref, g2_ref, g3_ref)], 0
    )
    head = dot(head_ref[...], out_weight, BY_ROWS)[:8] * head_c_ref[...]
    came_before_last = conv[0:1] * head[0:1]
    came_last = conv[0:1] * head[1:2] + conv[1:2] * head[0:1]
    b_part, c_part, x_part = b_ref[...], c_ref[...], x_ref[...]
    mixed = (b_part * x_part).astype(LOW).astype(FULL)
    place, keep_one, keep_two, tap_one, tap_two = taps(s_ref, t_ref, mixed, tail_mixed_ref[...])
    rows = mixed.shape[0]
    grad_conv = grad_gated * c_part
    conv_part_ref[...] = jnp.concatenate(
        [jnp.sum(grad_conv * tap, axis=0, keepdims=True) for tap in (tap_two, tap_one, mixed)], 0
    )
    to_one = jnp.where(keep_one, conv[1:2] * grad_conv, 0.0)
    to_two = jnp.where(keep_two, conv[0:1] * grad_conv, 0.0)
    from_one = pltpu.roll(to_one, rows - 1, 0)
    from_two = pltpu.roll(to_two, rows - 2, 0)
    is_last, is_before_last = place == rows - 1, place == rows - 2
    grad_mixed = (
        conv[2:3] * grad_conv
        + jnp.where(is_last, came_last, from_one)
        + jnp.where(is_last, 0.0, jnp.where(is_before_last, came_before_last, from_two))
    )
    grad_mixed = grad_mixed.astype(LOW).astype(FULL)
    grads = [
        (grad_mixed * x_part).astype(LOW),
        (grad_gated * convolved_ref[...]).astype(LOW),
        (grad_mixed * b_part).astype(LOW),
    ]
    columns = mixed.shape[1]
    turned = jnp.transpose(normed_ref[...])
    for k, grad in enumerate(grads):
        part_ref[:, k * columns : (k + 1) * columns] = slabs_of(
            dot(turned, grad).astype(LOW), SCATTER_ORDER
        )
    branch = jnp.concatenate([ref[...] for ref in (g0_ref, g1_ref, g2_ref, g3_ref)], 0)
    part_ref[:, 3 * columns :] = slabs_of(
        dot(jnp.transpose(branch), gated_ref[...]).astype(LOW), SCATTER_ORDER
    )
    quarter_rows = rows // MP
    sends = (p0_ref, p1_ref, p2_ref, p3_ref)
    gain_part = 0.0
    for o, ref in enumerate(sends):
        cut = slice(o * quarter_rows, (o + 1) * quarter_rows)
        part = sum(dot(grads[k][cut], w_ref[k], BY_ROWS) for k in range(3))
        ref[:quarter_rows, :] = part.astype(ref.dtype)
        gain_part = gain_part + jnp.sum(
            part * normed_ref[cut, :].astype(FULL), axis=0, keepdims=True
        )
    spare = jnp.zeros((14, gain_part.shape[1]), FULL)
    small = jnp.concatenate([gain_part / gain_ref[...], ffn_gain_ref[...], spare], 0)
    for ref in sends:
        ref[quarter_rows:, :] = small.astype(ref.dtype)


def hidden_kernel(
    s_ref, t_ref, p0_ref, r1_ref, r2_ref, r3_ref, hidden_ref, gain_ref, grad_ref,
    low_ref, small_ref,
):
    total = p0_ref[...]
    for ref in (r1_ref, r2_ref, r3_ref):
        total = total + ref[...].astype(FULL)
    rows = hidden_ref.shape[0]
    small_ref[...] = total[rows:]
    hidden = hidden_ref[...]
    inv = inv_rms(hidden)
    grad = grad_ref[...] + norm_back(total[:rows] * gain_ref[...], hidden * inv, inv)
    low_ref[...] = grad.astype(LOW)


def on_device(
    hidden_in,
    mix_gain,
    in_weight,
    conv_weight,
    out_weight,
    ffn_gain,
    gate_up_weight,
    down_weight,
    seq_starts,
    out_grad,
):
    rows, width = hidden_in.shape
    mine = rows // MP
    channels = conv_weight.shape[1]
    hidden_units = down_weight.shape[0]
    me = lax.axis_index("mp")
    start = me * mine
    natural = (rows - start) % rows
    place = (me.astype(jnp.int32)[None], seq_starts)
    mix_gain = mix_gain[None]
    ffn_gain = ffn_gain[None]
    w_in = jnp.transpose(in_weight, (1, 0, 2))
    w_gu = jnp.transpose(gate_up_weight, (1, 0, 2))
    own_rows = quarter(0, mine, width)

    tail_in = slab_shift(hidden_in[rows - 8 :], 1)
    quarter_low = ((mine, width), LOW, None)
    quarter_full = ((mine, width), FULL, None)
    low_part = ((rows, channels), LOW, None)
    full_part = ((rows, channels), FULL, None)
    outs = call(
        mix_kernel,
        place,
        [(hidden_in, quarter(o, mine, width)) for o in range(MP)]
        + [(v, None) for v in (tail_in, mix_gain, w_in, conv_weight, out_weight)],
        [((rows, width), LOW, None), full_part, full_part, full_part]
        + [low_part, full_part, ((8, channels), FULL, None)]
        + [quarter_full, quarter_low, quarter_low, quarter_low],
        vmem=BIG,
    )
    normed, b_part, c_part, x_part, gated, convolved, tail_mixed, p0, p1, p2, p3 = outs
    came = send_rows({1: p1, 2: p2, 3: p3})
    w_gu = after(gate_up_weight, came[1]).reshape(width, -1)
    came, w_gu = lax.optimization_barrier((came, w_gu))
    middle, middle_low = call(
        middle_kernel,
        place,
        [(hidden_in, own_rows), (p0, None), (came[1], None), (came[2], None), (came[3], None)],
        [quarter_full, quarter_low],
    )
    mids = {0: middle_low, **gather_rows(middle_low, (1, 3, 2))}
    late_grad = after(out_grad, middle_low)
    grad_low = jnp.concatenate(
        [lax.dynamic_slice_in_dim(late_grad, ((me + o) % MP) * mine, mine, 0) for o in ORDER], 0
    ).astype(LOW)
    grad_active = dot(grad_low, down_weight, BY_ROWS)
    mids[1], mids[3], grad_active = lax.optimization_barrier((mids[1], mids[3], grad_active))

    def ffn(offsets, grad_active):
        middle = jnp.concatenate([mids[o] for o in offsets], 0).astype(FULL)
        normed = (middle * inv_rms(middle) * ffn_gain).astype(LOW)
        gate_up = dot(normed, w_gu)
        gate, upper = gate_up[:, :hidden_units], gate_up[:, hidden_units:]
        sigma = jax.nn.sigmoid(gate)
        active = (gate * sigma * upper).astype(LOW)
        grad_gate = grad_active * upper * sigma * (1.0 + gate * (1.0 - sigma))
        grad_upper = grad_active * gate * sigma
        grad_gu = jnp.concatenate([grad_gate.astype(LOW), grad_upper.astype(LOW)], 1)
        back = dot(grad_gu, w_gu, BY_ROWS)
        return normed, active, grad_gu, back

    near = ffn(ORDER[:3], grad_active[: 3 * mine])
    near_low = near[3].astype(LOW)
    p0 = near_low[:mine]
    came_near = [
        lax.ppermute(near_low[mine : 2 * mine], "mp", ring_shift(MP, 1)),
        lax.ppermute(near_low[2 * mine :], "mp", ring_shift(MP, 3)),
    ]
    mids[2], far_grad = after((mids[2], grad_active[3 * mine :]), near_low)
    far = ffn(ORDER[3:], far_grad)
    far_low = far[3].astype(LOW)
    came = [*came_near, lax.ppermute(far_low, "mp", ring_shift(MP, 2))]
    normed_two, active, grad_gu = [
        jnp.concatenate([a, b], 0) for a, b in zip(near[:3], far[:3])
    ]
    normed_two, active, grad_gu, grad_low = after(
        (normed_two, active, grad_gu, grad_low), far_low
    )
    ffn_part = call(
        ffn_out_kernel,
        place,
        [(active, None), (down_weight, None)],
        [((rows, width), LOW, None)],
        vmem=BIG,
    )[0]
    ffn_out = lax.psum(ffn_part, "mp")
    normed_two, active, grad_gu, grad_low = after(
        (normed_two, active, grad_gu, grad_low), came_near[0]
    )
    block = hidden_units
    steps = 2 * hidden_units // block
    gate_up_block = pl.BlockSpec((rows, block), lambda i, s, t: (0, jnp.minimum(i, steps - 1)))
    down_block = pl.BlockSpec((rows, block), lambda i, s, t: (0, jnp.maximum(i - steps, 0)))
    ffn_grad_part = call(
        functools.partial(ffn_grad_kernel, steps),
        place,
        [(normed_two, None), (grad_gu, gate_up_block), (grad_low, None), (active, down_block)],
        [
            (
                (width, 3 * hidden_units),
                LOW,
                pl.BlockSpec((width, block), lambda i, s, t: (0, i)),
            )
        ],
        grid=3 * hidden_units // block,
        scratch=[pltpu.VMEM((width, rows), LOW)],
        vmem=BIG,
    )[0]
    ffn_line = chip_line_scatter(ffn_grad_part)
    head_c = lax.dynamic_slice_in_dim(after(c_part, near_low), natural, 8, 0)
    head_c = slab_shift(head_c, -1)
    came, ffn_part, head_c, ffn_grad_part = lax.optimization_barrier(
        (tuple(came), ffn_part, head_c, ffn_grad_part)
    )
    grad_middle, grad_branch, ffn_gain_part = call(
        branch_kernel,
        place,
        [(v, None) for v in (p0, *came, middle, ffn_gain)] + [(out_grad, own_rows)],
        [quarter_full, quarter_low, ((1, width), FULL, None)],
        vmem=BIG,
    )
    branches = {o: lax.ppermute(grad_branch, "mp", ring_shift(MP, -o)) for o in (1, 3)}
    head = head_spread(grad_branch[:16])
    branches[2] = lax.ppermute(after(grad_branch, head), "mp", ring_shift(MP, 2))
    branches, head = lax.optimization_barrier((branches, head))

    outs = call(
        mix_back_kernel,
        place,
        [(grad_branch, None)]
        + [(branches[o], None) for o in (1, 2, 3)]
        + [
            (v, None)
            for v in (
                gated, head, head_c, b_part, c_part, x_part, convolved, tail_mixed, conv_weight,
                out_weight, w_in, normed, mix_gain, ffn_gain_part,
            )
        ],
        [((width, 4 * channels), LOW, None), ((3, channels), FULL, None)]
        + [((mine + 16, width), LOW if o else FULL, None) for o in range(MP)],
        vmem=BIG,
    )
    in_out_part, conv_part, p0, p1, p2, p3 = outs
    in_out_line = chip_line_scatter(in_out_part)
    came = send_rows({1: p1, 2: p2, 3: p3})
    hidden_low, small = call(
        hidden_kernel,
        place,
        [(v, None) for v in (p0, came[1], came[2], came[3])]
        + [(hidden_in, own_rows), (mix_gain, None), (grad_middle, None)],
        [quarter_low, ((16, width), FULL, None)],
    )
    ends = gather_rows(hidden_low)
    conv_row = jnp.pad(conv_part.reshape(1, -1), ((0, 0), (0, width - 3 * channels)))
    small = all_sum(jnp.concatenate([small[:2], conv_row], 0))
    ends, ffn_out, ffn_line = lax.optimization_barrier((ends, ffn_out, ffn_line))
    chunk = pl.BlockSpec((mine, width), lambda i, s, t: ((s[0] + i) % MP, 0))
    hidden_grad = call(
        place_kernel,
        place,
        [(v, None) for v in (hidden_low, ends[1], ends[2], ends[3])],
        [((rows, width), FULL, chunk)],
        grid=MP,
    )[0]
    hidden_out = call(
        place_add_kernel,
        place,
        [(mids[o], None) for o in range(MP)] + [(ffn_out, chunk)],
        [((rows, width), FULL, chunk)],
        grid=MP,
    )[0]
    in_out_line, small = after((in_out_line, small), hidden_grad, hidden_out)
    line = jnp.concatenate([ffn_line, in_out_line], 1).reshape(Z_DIM, 32, -1)
    done = line_sum(line, "z")
    ffn_done = done[:, : 3 * hidden_units]
    in_out_done = done[:, 3 * hidden_units :]
    mix_gain_grad, ffn_gain_grad = small[0], small[1]
    conv_weight_grad = small[2, : 3 * channels].reshape(3, channels)
    local = in_out_done.shape[0]
    return (
        hidden_out,
        hidden_grad,
        mix_gain_grad,
        in_out_done[:, : 3 * channels].reshape(local, 3, channels),
        conv_weight_grad,
        in_out_done[:, 3 * channels :].T,
        ffn_gain_grad,
        ffn_done[:, : 2 * hidden_units].reshape(local, 2, hidden_units),
        ffn_done[:, 2 * hidden_units :].T,
    )


def solution(mesh):
    placed = (
        P("seq", None),
        P(),
        P(None, None, "mp"),
        P(None, "mp"),
        P("mp", None),
        P(),
        P(None, None, "mp"),
        P("mp", None),
        P("seq"),
        P("seq", None),
    )
    return jax.shard_map(
        on_device,
        mesh=mesh,
        in_specs=placed,
        out_specs=(
            P("seq", None),
            P("seq", None),
            P(),
            P("seq", None, "mp"),
            P(None, "mp"),
            P("mp", "seq"),
            P(),
            P("seq", None, "mp"),
            P("mp", "seq"),
        ),
        check_vma=False,
    )
```

time: 628 us -> 216 us (0.34)
  waiting for transfers between devices: 409 us -> 72.4 us
  blocking collectives: 124 us -> 0 us
  starting transfers between devices: 4.57 us -> 54.6 us
  matrix products: 44 us -> 8.78 us
  Pallas kernels: 0 us -> 35.1 us
  other arithmetic: 21.5 us -> 8.5 us
  local copies, waits for them, and re-layouts: 8.71 us -> 16.6 us
    reduce_scatter x4 -> x2, waiting for transfers between devices: 217 us -> 0.01 us  [chip_line_scatter(): lax.psum_scatter(part, 'seq', scatter_dimension=0, axis_index_groups=grou...]
    psum x3 -> x1, waiting for transfers between devices: 189 us -> 0.01 us  [on_device(): ffn_out = lax.psum(ffn_part, 'mp')]
    psum x1 -> x0, blocking collectives: 124 us -> none  [on_device(): lax.psum((mix_gain_part, conv_part, ffn_gain_part), 'seq')]
    ppermute x2 -> x34, waiting for transfers between devices: 3.36 us -> 71.9 us  [the longest x6 27 us: send_rows(): lax.ppermute(parts[o], 'mp', ring_shift(MP, o))]
    ppermute x2 -> x34, starting transfers between devices: 4.28 us -> 54.5 us  [the longest x6 10.5 us: all_sum(): value = value + sum((lax.ppermute(value, 'seq', shift) for shift in shifts))]
    dot_general x12 -> x5, matrix products: 44 us -> 8.78 us  [dot(): lax.dot_general(left, right, (contract, ((), ())), preferred_element_type...]
    pallas_call x0 -> x9, Pallas kernels: none -> 35.1 us  [call(): pl.pallas_call(kernel, grid_spec=pltpu.PrefetchScalarGridSpec(num_scalar_...]
    add x4 -> x5, other arithmetic: 10.7 us -> 0.79 us  [the longest x1 0.63 us: head_spread(): came = came + lax.ppermute(value, ('seq', 'mp'), pairs)]
  transfers between devices with their start and end apart: 9 -> 37, of which waited for: 8 -> 18; matrix products, arithmetic and copies ran while one was open for 6% -> 8% of each run, Pallas kernels for 0% -> 14%
where the time goes in v2:
time: 216 us; the launch traced here: 213 us
  waiting for transfers between devices  72.4 us (34%)
  starting transfers between devices  54.6 us (25%)
  Pallas kernels  35.1 us (16%)
  local copies, waits for them, and re-layouts  16.6 us (8%)
  between operations  16.5 us (8%)
  matrix products  8.78 us (4%)
  other arithmetic  8.5 us (4%)
    pallas_call x9, Pallas kernels, call(): pl.pallas_call(kernel, grid_spec=pltpu.PrefetchScalarGridSpec(num_scalar_...  35.1 us
    ppermute x6, waiting for transfers between devices, send_rows(): lax.ppermute(parts[o], 'mp', ring_shift(MP, o))  27 us
    ppermute x2, waiting for transfers between devices, on_device(): lax.ppermute(grad_branch, 'mp', ring_shift(MP, -o))  12.8 us
    ppermute x6, waiting for transfers between devices, gather_rows(): return {o: lax.ppermute(rows, 'mp', ring_shift(MP, -o)) for o in order}  12.1 us
    ppermute x6, starting transfers between devices, all_sum(): value = value + sum((lax.ppermute(value, 'seq', shift) for shift in shifts))  10.5 us
    ppermute x6, starting transfers between devices, send_rows(): lax.ppermute(parts[o], 'mp', ring_shift(MP, o))  10.4 us
    unnamed x40, local copies, waits for them, and re-layouts  8.87 us
    ppermute x6, starting transfers between devices, gather_rows(): return {o: lax.ppermute(rows, 'mp', ring_shift(MP, -o)) for o in order}  8.87 us
  transfers between devices with their start and end apart: 37, of which 18 were waited for; matrix products, arithmetic and copies ran while one was open for 8% of the time, Pallas kernels for 14%

profile of v2, /device:TPU:2, one launch (start us, length us, event | category | flops | bytes accessed | tf_op | source)
XLA Modules:
  0.0 212.6 jit_solution(12708142322998313658)
XLA Ops:
  11.4 2.7 %collective-permute-done.tail_ref = f32[8,1024]{1,0:T(8,128)S(1)} collective-permute-done((f32[8,1024]{1,0:T(8,128)S(1)}, f32[8,1024]{1,0:T(8,128)S(1)}, u32[]{:S(2)}, u32[]{:S(2)}) %collective-permute-start) | collective-permute-done | bytes 32800 | tf_op jit(solution)/shard_map/ppermute | solution.py:43
  14.7 5.6 %shard_map.169 = (bf16[512,1024]{1,0:T(8,128)(2,1)}, f32[512,256]{1,0:T(8,128)}, f32[512,256]{1,0:T(8,128)}, f32[512,256]{1,0:T(8,128)}, bf16[512,256]{1,0:T(8,1...) custom-call(s32[1]{0:T(128)} %bitcast.s_ref, ...), custom_call_target="tpu_custom_call" | custom-call | tf_op jit(solution)/shard_map/pallas_call | solution.py:143
  21.8 2.9 %collective-permute-start.2 = (bf16[128,1024]{1,0:T(8,128)(2,1)}, bf16[128,1024]{1,0:T(8,128)(2,1)S(1)}, u32[]{:S(2)}, u32[]{:S(2)}) collective-permute-start(bf16[128,1024]{1,0:T(8,128)(2,1)} %get-tuple-element.71), channel_id=1, source_target_pairs={{0,2},{1,3},{2,0},{3,1},{4,6},{5,7},{6,4},{7,5},{8,10},{9,11},{10,... | collective-permute-start | bytes 786440 | tf_op jit(solution)/shard_map/ppermute | solution.py:64
  26.1 3.7 %collective-permute-done.1.r1_ref = bf16[128,1024]{1,0:T(8,128)(2,1)S(1)} collective-permute-done((bf16[128,1024]{1,0:T(8,128)(2,1)}, bf16[128,1024]{1,0:T(8,128)(2,1)S(1)}, u32[]{:S(2)}, u32[]{:S(2)}) %collective-permute-start.1) | collective-permute-done | bytes 262176 | tf_op jit(solution)/shard_map/ppermute | solution.py:64
  29.8 3.3 %copy.21 = bf16[128,8,2,1152]{3,1,2,0:T(8,128)(2,1)S(1)} copy(bf16[128,8,2,1152]{3,2,1,0:T(2,128)(2,1)} %bitcast.45) | data formatting | bytes 9437184
  33.1 2.9 %collective-permute-done.2.r2_ref = bf16[128,1024]{1,0:T(8,128)(2,1)S(1)} collective-permute-done((bf16[128,1024]{1,0:T(8,128)(2,1)}, bf16[128,1024]{1,0:T(8,128)(2,1)S(1)}, u32[]{:S(2)}, u32[]{:S(2)}) %collective-permute-start.2) | collective-permute-done | bytes 262176 | tf_op jit(solution)/shard_map/ppermute | solution.py:64
  37.0 2.1 %collective-permute-start.4 = (bf16[128,1024]{1,0:T(8,128)(2,1)S(1)}, bf16[128,1024]{1,0:T(8,128)(2,1)S(1)}, u32[]{:S(2)}, u32[]{:S(2)}) collective-permute-start(bf16[128,1024]{1,0:T(8,128)(2,1)S(1)} %get-tuple-element.77.c0_ref), channel_id=1, source_target_pairs={{0,3},{1,0},{2,1},{3,2},{4,7},{5,4},{6,5},{7,6},{8,11},{9,8},{10,9... | collective-permute-start | bytes 786440 | tf_op jit(solution)/shard_map/ppermute | solution.py:68
  39.2 4.0 %collective-permute-start.6 = (bf16[128,1024]{1,0:T(8,128)(2,1)S(1)}, bf16[128,1024]{1,0:T(8,128)(2,1)S(1)}, u32[]{:S(2)}, u32[]{:S(2)}) collective-permute-start(bf16[128,1024]{1,0:T(8,128)(2,1)S(1)} %get-tuple-element.77.c0_ref), channel_id=1, source_target_pairs={{0,2},{1,3},{2,0},{3,1},{4,6},{5,7},{6,4},{7,5},{8,10},{9,11},{10,... | collective-permute-start | bytes 786440 | tf_op jit(solution)/shard_map/ppermute | solution.py:68
  44.9 5.5 %collective-permute-done.4.c1_ref = bf16[128,1024]{1,0:T(8,128)(2,1)S(1)} collective-permute-done((bf16[128,1024]{1,0:T(8,128)(2,1)S(1)}, bf16[128,1024]{1,0:T(8,128)(2,1)S(1)}, u32[]{:S(2)}, u32[]{:S(2)}) %collective-permute-start.4) | collective-permute-done | bytes 262176 | tf_op jit(solution)/shard_map/ppermute | solution.py:68
  50.4 3.4 %collective-permute-done.5.c3_ref = bf16[128,1024]{1,0:T(8,128)(2,1)S(1)} collective-permute-done((bf16[128,1024]{1,0:T(8,128)(2,1)S(1)}, bf16[128,1024]{1,0:T(8,128)(2,1)S(1)}, u32[]{:S(2)}, u32[]{:S(2)}) %collective-permute-start.5) | collective-permute-done | bytes 262176 | tf_op jit(solution)/shard_map/ppermute | solution.py:68
  57.6 2.0 fusion.7
  63.1 2.4 %convolution_convert_fusion = bf16[128,1024]{1,0:T(8,128)(2,1)} fusion(bf16[1024,2304]{1,0:T(8,128)(2,1)S(1)} %bitcast.42, bf16[128,1152]{1,0:T(8,128)(2,1)S(1)} %get-tuple-element.146, bf16[128,1152]{1,0:T(8,128)(2,1)S(1)} %get-tuple-element.145), kind=kOutput, calls=%fused_computation.15 | convolution fusion | flops 605290496 | bytes 5570560 | tf_op jit(solution)/shard_map/dot_general | solution.py:56
  75.2 4.5 %shard_map.171 = bf16[512,1024]{1,0:T(8,128)(2,1)} custom-call(s32[1]{0:T(128)} %bitcast.s_ref, s32[1]{0:T(128)S(6)} %copy.26.t_ref, bf16[512,1152]{1,0:T(8,128)(2,1)} %pad_maximum_fusion.active_ref, bf16[1152,1024]{1,0:T(8,128)(2,1)} %down_ref.1), custom_call_target="tpu_custom_call" | custom-call | tf_op jit(solution)/shard_map/pallas_call | solution.py:143
  80.3 9.2 %shard_map.172 = bf16[1024,3456]{1,0:T(8,128)(2,1)} custom-call(s32[1]{0:T(128)} %bitcast.s_ref, s32[1]{0:T(128)S(6)} %copy.26.t_ref, bf16[512,1024]{1,0:T(8,128)(2,1)} %get-tuple-element.91.normed_ref, bf16[512,2304]{1,0:T(8,128)(2,1)} %maximum_maximum_fusion.grad_gu_ref, bf16[512,1024]{1,0:T(8,128)(2,1)} %get-tuple-element.93.low_ref, ...), custom_call_target="tpu_custom_call" | custom-call | tf_op jit(solution)/shard_map/pallas_call | solution.py:143
  90.2 2.8 %shard_map.173 = (f32[128,1024]{1,0:T(8,128)}, bf16[128,1024]{1,0:T(8,128)(2,1)}, f32[1,1024]{1,0:T(1,128)}) custom-call(s32[1]{0:T(128)} %bitcast.s_ref, s32[1]{0:T(128)S(6)} %copy.26.t_ref, bf16[128,1024]{1,0:T(8,128)(2,1)} %get-tuple-element.153.p0_ref, bf16[128,1024]{1,0:T(8,128)(2,1)} %copy-done.11, bf16[128,1024]{1,0:T(8,128)(2,1)} %collective-permute-done.8.r2_ref, ...), custom_call_target="tpu_custom_call" | custom-call | tf_op jit(solution)/shard_map/pallas_call | solution.py:143
  102.3 2.6 %collective-permute-start.16 = (bf16[128,1024]{1,0:T(8,128)(2,1)}, bf16[128,1024]{1,0:T(8,128)(2,1)S(1)}, u32[]{:S(2)}, u32[]{:S(2)}) collective-permute-start(bf16[128,1024]{1,0:T(8,128)(2,1)} %get-tuple-element.100.g0_ref), channel_id=1, source_target_pairs={{0,2},{1,3},{2,0},{3,1},{4,6},{5,7},{6,4},{7,5},{8,10},{9,11},{10,... | collective-permute-start | bytes 786440 | tf_op jit(solution)/shard_map/ppermute | solution.py:498
  104.9 8.5 %collective-permute-done.11.g1_ref = bf16[128,1024]{1,0:T(8,128)(2,1)S(1)} collective-permute-done((bf16[128,1024]{1,0:T(8,128)(2,1)}, bf16[128,1024]{1,0:T(8,128)(2,1)S(1)}, u32[]{:S(2)}, u32[]{:S(2)}) %collective-permute-start.11) | collective-permute-done | bytes 262176 | tf_op jit(solution)/shard_map/ppermute | solution.py:496
  113.4 4.3 %collective-permute-done.17.g3_ref = bf16[128,1024]{1,0:T(8,128)(2,1)S(1)} collective-permute-done((bf16[128,1024]{1,0:T(8,128)(2,1)}, bf16[128,1024]{1,0:T(8,128)(2,1)S(1)}, u32[]{:S(2)}, u32[]{:S(2)}) %collective-permute-start.17) | collective-permute-done | bytes 262176 | tf_op jit(solution)/shard_map/ppermute | solution.py:496
  117.8 3.6 %collective-permute-done.16.g2_ref = bf16[128,1024]{1,0:T(8,128)(2,1)S(1)} collective-permute-done((bf16[128,1024]{1,0:T(8,128)(2,1)}, bf16[128,1024]{1,0:T(8,128)(2,1)S(1)}, u32[]{:S(2)}, u32[]{:S(2)}) %collective-permute-start.16) | collective-permute-done | bytes 262176 | tf_op jit(solution)/shard_map/ppermute | solution.py:498
  122.1 8.7 %shard_map.174 = (bf16[1024,1024]{1,0:T(8,128)(2,1)}, f32[3,256]{1,0:T(4,128)}, f32[144,1024]{1,0:T(8,128)}, bf16[144,1024]{1,0:T(8,128)(2,1)}, bf16[144,1024]{1,0:T(8,128)(2,1)}, /*index=5*/bf16[144,1024]{1,0:T(8,128)(2,1)}) custom-call(s32[1]{0:T(128)} %bitcast.s_ref, s32[1]{0:T(128)S(6)} %copy.26.t_ref, bf16[128,1024]{1,0:T(8,128)(2,1)} %get-tuple-element.100.g0_ref, ...), custom_call_target="tpu_custom_call" | custom-call | tf_op jit(solution)/shard_map/pallas_call | solution.py:143
  131.0 3.0 %collective-permute-start.19 = (bf16[144,1024]{1,0:T(8,128)(2,1)}, bf16[144,1024]{1,0:T(8,128)(2,1)S(1)}, u32[]{:S(2)}, u32[]{:S(2)}) collective-permute-start(bf16[144,1024]{1,0:T(8,128)(2,1)} %get-tuple-element.115), channel_id=1, source_target_pairs={{0,2},{1,3},{2,0},{3,1},{4,6},{5,7},{6,4},{7,5},{8,10},{9,11},{10,... | collective-permute-start | bytes 884744 | tf_op jit(solution)/shard_map/ppermute | solution.py:64
  135.5 12.7 %collective-permute-done.18.r1_ref = bf16[144,1024]{1,0:T(8,128)(2,1)S(1)} collective-permute-done((bf16[144,1024]{1,0:T(8,128)(2,1)}, bf16[144,1024]{1,0:T(8,128)(2,1)S(1)}, u32[]{:S(2)}, u32[]{:S(2)}) %collective-permute-start.18) | collective-permute-done | bytes 294944 | tf_op jit(solution)/shard_map/ppermute | solution.py:64
  148.2 7.7 %collective-permute-done.19.r2_ref = bf16[144,1024]{1,0:T(8,128)(2,1)S(1)} collective-permute-done((bf16[144,1024]{1,0:T(8,128)(2,1)}, bf16[144,1024]{1,0:T(8,128)(2,1)S(1)}, u32[]{:S(2)}, u32[]{:S(2)}) %collective-permute-start.19) | collective-permute-done | bytes 294944 | tf_op jit(solution)/shard_map/ppermute | solution.py:64
  159.6 2.2 %collective-permute-start.25 = (f32[3,1024]{1,0:T(4,128)S(1)}, f32[3,1024]{1,0:T(4,128)S(1)}, u32[]{:S(2)}, u32[]{:S(2)}) collective-permute-start(f32[3,1024]{1,0:T(4,128)S(1)} %fusion.20), channel_id=1, source_target_pairs={{0,16},{4,20},{8,24},{12,28},{16,0},{20,4},{24,8},{28,12},{32,48},... | collective-permute-start | bytes 36872 | tf_op jit(solution)/shard_map/ppermute | solution.py:95
  161.9 2.0 collective-permute-start.27
  166.6 3.4 %collective-permute-start.28 = (f32[3,1024]{1,0:T(4,128)S(1)}, f32[3,1024]{1,0:T(4,128)S(1)}, u32[]{:S(2)}, u32[]{:S(2)}) collective-permute-start(f32[3,1024]{1,0:T(4,128)S(1)} %add_add_fusion.2), channel_id=1, source_target_pairs={{0,64},{4,68},{8,72},{12,76},{16,80},{20,84},{24,88},{28,92},{32,9... | collective-permute-start | bytes 36872 | tf_op jit(solution)/shard_map/ppermute | solution.py:95
  172.0 2.6 %collective-permute-start.30 = (f32[3,1024]{1,0:T(4,128)S(1)}, f32[3,1024]{1,0:T(4,128)S(1)}, u32[]{:S(2)}, u32[]{:S(2)}) collective-permute-start(f32[3,1024]{1,0:T(4,128)S(1)} %add_add_fusion.2), channel_id=1, source_target_pairs={{0,96},{4,100},{8,104},{12,108},{16,112},{20,116},{24,120},{28,124... | collective-permute-start | bytes 36872 | tf_op jit(solution)/shard_map/ppermute | solution.py:95
  176.1 3.2 %collective-permute-done.23.c3_ref = bf16[128,1024]{1,0:T(8,128)(2,1)S(1)} collective-permute-done((bf16[128,1024]{1,0:T(8,128)(2,1)S(1)}, bf16[128,1024]{1,0:T(8,128)(2,1)S(1)}, u32[]{:S(2)}, u32[]{:S(2)}) %collective-permute-start.23) | collective-permute-done | bytes 262176 | tf_op jit(solution)/shard_map/ppermute | solution.py:68
  185.4 3.6 %collective-permute-start.31 = (bf16[32,4480]{1,0:T(8,128)(2,1)S(1)}, bf16[32,4480]{1,0:T(8,128)(2,1)S(1)}, u32[]{:S(2)}, u32[]{:S(2)}) collective-permute-start(bf16[32,4480]{1,0:T(8,128)(2,1)S(1)} %get-tuple-element.148), channel_id=1, source_target_pairs={{0,64},{4,68},{8,72},{12,76},{16,80},{20,84},{24,88},{28,92},{32,9... | collective-permute-start | bytes 860168 | tf_op jit(solution)/shard_map/ppermute | solution.py:86
  189.0 3.2 %collective-permute-start.33 = (bf16[32,4480]{1,0:T(8,128)(2,1)S(1)}, bf16[32,4480]{1,0:T(8,128)(2,1)S(1)}, u32[]{:S(2)}, u32[]{:S(2)}) collective-permute-start(bf16[32,4480]{1,0:T(8,128)(2,1)S(1)} %get-tuple-element.149), channel_id=1, source_target_pairs={{0,96},{4,100},{8,104},{12,108},{16,112},{20,116},{24,120},{28,124... | collective-permute-start | bytes 860168 | tf_op jit(solution)/shard_map/ppermute | solution.py:86
  193.4 3.3 %collective-permute-done.31 = bf16[32,4480]{1,0:T(8,128)(2,1)S(1)} collective-permute-done((bf16[32,4480]{1,0:T(8,128)(2,1)S(1)}, bf16[32,4480]{1,0:T(8,128)(2,1)S(1)}, u32[]{:S(2)}, u32[]{:S(2)}) %collective-permute-start.31) | collective-permute-done | bytes 286752 | tf_op jit(solution)/shard_map/ppermute | solution.py:86
  196.7 5.4 %collective-permute-done.32 = bf16[32,4480]{1,0:T(8,128)(2,1)S(1)} collective-permute-done((bf16[32,4480]{1,0:T(8,128)(2,1)S(1)}, bf16[32,4480]{1,0:T(8,128)(2,1)S(1)}, u32[]{:S(2)}, u32[]{:S(2)}) %collective-permute-start.32) | collective-permute-done | bytes 286752 | tf_op jit(solution)/shard_map/ppermute | solution.py:86
  (135 shorter events, 59.0 us)
Async XLA Ops:
  8.0 171.3 %all-reduce.3.cloned.1.call-start = ((), (), s32[]{:S(2)}) async-start(), calls=%async_computation.2 | async-start | bytes 2097152 | tf_op jit(solution)/shard_map/psum | solution.py:460
  8.8 5.2 %collective-permute-start = (f32[8,1024]{1,0:T(8,128)S(1)}, f32[8,1024]{1,0:T(8,128)S(1)}, u32[]{:S(2)}, u32[]{:S(2)}) collective-permute-start(f32[8,1024]{1,0:T(8,128)S(1)} %slice.63), channel_id=1, source_target_pairs={{0,4},{4,8},{8,12},{12,16},{16,20},{20,24},{24,28},{28,32},{32,36}... | collective-permute-start | bytes 98312 | tf_op jit(solution)/shard_map/ppermute | solution.py:43
  20.2 9.5 %collective-permute-start.1 = (bf16[128,1024]{1,0:T(8,128)(2,1)}, bf16[128,1024]{1,0:T(8,128)(2,1)S(1)}, u32[]{:S(2)}, u32[]{:S(2)}) collective-permute-start(bf16[128,1024]{1,0:T(8,128)(2,1)} %get-tuple-element.70), channel_id=1, source_target_pairs={{0,1},{1,2},{2,3},{3,0},{4,5},{5,6},{6,7},{7,4},{8,9},{9,10},{10,1... | collective-permute-start | bytes 786440 | tf_op jit(solution)/shard_map/ppermute | solution.py:64
  21.8 14.2 %collective-permute-start.2 = (bf16[128,1024]{1,0:T(8,128)(2,1)}, bf16[128,1024]{1,0:T(8,128)(2,1)S(1)}, u32[]{:S(2)}, u32[]{:S(2)}) collective-permute-start(bf16[128,1024]{1,0:T(8,128)(2,1)} %get-tuple-element.71), channel_id=1, source_target_pairs={{0,2},{1,3},{2,0},{3,1},{4,6},{5,7},{6,4},{7,5},{8,10},{9,11},{10,... | collective-permute-start | bytes 786440 | tf_op jit(solution)/shard_map/ppermute | solution.py:64
  24.7 11.3 %collective-permute-start.3 = (bf16[128,1024]{1,0:T(8,128)(2,1)}, bf16[128,1024]{1,0:T(8,128)(2,1)S(1)}, u32[]{:S(2)}, u32[]{:S(2)}) collective-permute-start(bf16[128,1024]{1,0:T(8,128)(2,1)} %get-tuple-element.72), channel_id=1, source_target_pairs={{0,3},{1,0},{2,1},{3,2},{4,7},{5,4},{6,5},{7,6},{8,11},{9,8},{10,9... | collective-permute-start | bytes 786440 | tf_op jit(solution)/shard_map/ppermute | solution.py:64
  37.0 13.4 %collective-permute-start.4 = (bf16[128,1024]{1,0:T(8,128)(2,1)S(1)}, bf16[128,1024]{1,0:T(8,128)(2,1)S(1)}, u32[]{:S(2)}, u32[]{:S(2)}) collective-permute-start(bf16[128,1024]{1,0:T(8,128)(2,1)S(1)} %get-tuple-element.77.c0_ref), channel_id=1, source_target_pairs={{0,3},{1,0},{2,1},{3,2},{4,7},{5,4},{6,5},{7,6},{8,11},{9,8},{10,9... | collective-permute-start | bytes 786440 | tf_op jit(solution)/shard_map/ppermute | solution.py:68
  39.2 14.7 %collective-permute-start.5 = (bf16[128,1024]{1,0:T(8,128)(2,1)S(1)}, bf16[128,1024]{1,0:T(8,128)(2,1)S(1)}, u32[]{:S(2)}, u32[]{:S(2)}) collective-permute-start(bf16[128,1024]{1,0:T(8,128)(2,1)S(1)} %get-tuple-element.77.c0_ref), channel_id=1, source_target_pairs={{0,1},{1,2},{2,3},{3,0},{4,5},{5,6},{6,7},{7,4},{8,9},{9,10},{10,1... | collective-permute-start | bytes 786440 | tf_op jit(solution)/shard_map/ppermute | solution.py:68
  39.2 20.4 %collective-permute-start.6 = (bf16[128,1024]{1,0:T(8,128)(2,1)S(1)}, bf16[128,1024]{1,0:T(8,128)(2,1)S(1)}, u32[]{:S(2)}, u32[]{:S(2)}) collective-permute-start(bf16[128,1024]{1,0:T(8,128)(2,1)S(1)} %get-tuple-element.77.c0_ref), channel_id=1, source_target_pairs={{0,2},{1,3},{2,0},{3,1},{4,6},{5,7},{6,4},{7,5},{8,10},{9,11},{10,... | collective-permute-start | bytes 786440 | tf_op jit(solution)/shard_map/ppermute | solution.py:68
  66.3 14.0 %collective-permute-start.7 = (bf16[128,1024]{1,0:T(8,128)(2,1)}, bf16[128,1024]{1,0:T(8,128)(2,1)S(1)}, u32[]{:S(2)}, u32[]{:S(2)}) collective-permute-start(bf16[128,1024]{1,0:T(8,128)(2,1)} %get-tuple-element.152), channel_id=1, source_target_pairs={{0,1},{1,2},{2,3},{3,0},{4,5},{5,6},{6,7},{7,4},{8,9},{9,10},{10,1... | collective-permute-start | bytes 786440 | tf_op jit(solution)/shard_map/ppermute | solution.py:440
  67.1 22.4 %collective-permute-start.10 = (f32[8,256]{1,0:T(8,128)S(1)}, f32[8,256]{1,0:T(8,128)S(1)}, u32[]{:S(2)}, u32[]{:S(2)}) collective-permute-start(f32[8,256]{1,0:T(8,128)S(1)} %constant_dynamic-slice_fusion), channel_id=1, source_target_pairs={{4,0},{8,4},{12,8},{16,12},{20,16},{24,20},{28,24},{32,28},{36,32}... | collective-permute-start | bytes 24584 | tf_op jit(solution)/shard_map/ppermute | solution.py:43
  69.0 20.5 %collective-permute-start.9 = (bf16[128,1024]{1,0:T(8,128)(2,1)}, bf16[128,1024]{1,0:T(8,128)(2,1)}, u32[]{:S(2)}, u32[]{:S(2)}) collective-permute-start(bf16[128,1024]{1,0:T(8,128)(2,1)} %convolution_convert_fusion), channel_id=1, source_target_pairs={{0,2},{1,3},{2,0},{3,1},{4,6},{5,7},{6,4},{7,5},{8,10},{9,11},{10,... | collective-permute-start | bytes 786440 | tf_op jit(solution)/shard_map/ppermute | solution.py:446
  70.8 18.7 %collective-permute-start.8 = (bf16[128,1024]{1,0:T(8,128)(2,1)}, bf16[128,1024]{1,0:T(8,128)(2,1)}, u32[]{:S(2)}, u32[]{:S(2)}) collective-permute-start(bf16[128,1024]{1,0:T(8,128)(2,1)} %get-tuple-element.151), channel_id=1, source_target_pairs={{0,3},{1,0},{2,1},{3,2},{4,7},{5,4},{6,5},{7,6},{8,11},{9,8},{10,9... | collective-permute-start | bytes 786440 | tf_op jit(solution)/shard_map/ppermute | solution.py:441
  89.6 89.7 %reduce-scatter.3.cloned.1.call-start = ((), (), s32[]{:S(2)}) async-start(), calls=%async_computation.3 | async-start | bytes 7962624 | tf_op jit(solution)/shard_map/reduce_scatter | solution.py:103
  90.2 94.1 %reduce-scatter.5.cloned.1.call-start = ((), (), s32[]{:S(2)}) async-start(), calls=%async_computation.4 | async-start | bytes 2359296 | tf_op jit(solution)/shard_map/reduce_scatter | solution.py:103
  93.8 5.9 %collective-permute-start.12 = (bf16[16,1024]{1,0:T(8,128)(2,1)S(1)}, bf16[16,1024]{1,0:T(8,128)(2,1)S(1)}, u32[]{:S(2)}, u32[]{:S(2)}) collective-permute-start(bf16[16,1024]{1,0:T(8,128)(2,1)S(1)} %slice.73), channel_id=1, source_target_pairs={{4,0},{8,4},{12,8},{16,12},{20,16},{24,20},{28,24},{32,28},{36,32}... | collective-permute-start | bytes 98312 | tf_op jit(solution)/shard_map/ppermute | solution.py:51
  95.7 6.0 %collective-permute-start.13 = (bf16[16,1024]{1,0:T(8,128)(2,1)S(1)}, bf16[16,1024]{1,0:T(8,128)(2,1)S(1)}, u32[]{:S(2)}, u32[]{:S(2)}) collective-permute-start(bf16[16,1024]{1,0:T(8,128)(2,1)S(1)} %slice.73), channel_id=1, source_target_pairs={{4,1},{8,5},{12,9},{16,13},{20,17},{24,21},{28,25},{32,29},{36,33}... | collective-permute-start | bytes 98312 | tf_op jit(solution)/shard_map/ppermute | solution.py:51
  99.6 13.8 %collective-permute-start.11 = (bf16[128,1024]{1,0:T(8,128)(2,1)}, bf16[128,1024]{1,0:T(8,128)(2,1)S(1)}, u32[]{:S(2)}, u32[]{:S(2)}) collective-permute-start(bf16[128,1024]{1,0:T(8,128)(2,1)} %get-tuple-element.100.g0_ref), channel_id=1, source_target_pairs={{0,3},{1,0},{2,1},{3,2},{4,7},{5,4},{6,5},{7,6},{8,11},{9,8},{10,9... | collective-permute-start | bytes 786440 | tf_op jit(solution)/shard_map/ppermute | solution.py:496
  99.7 18.1 %collective-permute-start.17 = (bf16[128,1024]{1,0:T(8,128)(2,1)}, bf16[128,1024]{1,0:T(8,128)(2,1)S(1)}, u32[]{:S(2)}, u32[]{:S(2)}) collective-permute-start(bf16[128,1024]{1,0:T(8,128)(2,1)} %get-tuple-element.100.g0_ref), channel_id=1, source_target_pairs={{0,1},{1,2},{2,3},{3,0},{4,5},{5,6},{6,7},{7,4},{8,9},{9,10},{10,1... | collective-permute-start | bytes 786440 | tf_op jit(solution)/shard_map/ppermute | solution.py:496
  102.3 19.0 %collective-permute-start.16 = (bf16[128,1024]{1,0:T(8,128)(2,1)}, bf16[128,1024]{1,0:T(8,128)(2,1)S(1)}, u32[]{:S(2)}, u32[]{:S(2)}) collective-permute-start(bf16[128,1024]{1,0:T(8,128)(2,1)} %get-tuple-element.100.g0_ref), channel_id=1, source_target_pairs={{0,2},{1,3},{2,0},{3,1},{4,6},{5,7},{6,4},{7,5},{8,10},{9,11},{10,... | collective-permute-start | bytes 786440 | tf_op jit(solution)/shard_map/ppermute | solution.py:498
  130.9 17.3 %collective-permute-start.18 = (bf16[144,1024]{1,0:T(8,128)(2,1)}, bf16[144,1024]{1,0:T(8,128)(2,1)S(1)}, u32[]{:S(2)}, u32[]{:S(2)}) collective-permute-start(bf16[144,1024]{1,0:T(8,128)(2,1)} %get-tuple-element.114), channel_id=1, source_target_pairs={{0,1},{1,2},{2,3},{3,0},{4,5},{5,6},{6,7},{7,4},{8,9},{9,10},{10,1... | collective-permute-start | bytes 884744 | tf_op jit(solution)/shard_map/ppermute | solution.py:64
  131.0 24.9 %collective-permute-start.19 = (bf16[144,1024]{1,0:T(8,128)(2,1)}, bf16[144,1024]{1,0:T(8,128)(2,1)S(1)}, u32[]{:S(2)}, u32[]{:S(2)}) collective-permute-start(bf16[144,1024]{1,0:T(8,128)(2,1)} %get-tuple-element.115), channel_id=1, source_target_pairs={{0,2},{1,3},{2,0},{3,1},{4,6},{5,7},{6,4},{7,5},{8,10},{9,11},{10,... | collective-permute-start | bytes 884744 | tf_op jit(solution)/shard_map/ppermute | solution.py:64
  133.9 22.0 %collective-permute-start.20 = (bf16[144,1024]{1,0:T(8,128)(2,1)}, bf16[144,1024]{1,0:T(8,128)(2,1)S(1)}, u32[]{:S(2)}, u32[]{:S(2)}) collective-permute-start(bf16[144,1024]{1,0:T(8,128)(2,1)} %get-tuple-element.116), channel_id=1, source_target_pairs={{0,3},{1,0},{2,1},{3,2},{4,7},{5,4},{6,5},{7,6},{8,11},{9,8},{10,9... | collective-permute-start | bytes 884744 | tf_op jit(solution)/shard_map/ppermute | solution.py:64
  159.6 6.5 %collective-permute-start.25 = (f32[3,1024]{1,0:T(4,128)S(1)}, f32[3,1024]{1,0:T(4,128)S(1)}, u32[]{:S(2)}, u32[]{:S(2)}) collective-permute-start(f32[3,1024]{1,0:T(4,128)S(1)} %fusion.20), channel_id=1, source_target_pairs={{0,16},{4,20},{8,24},{12,28},{16,0},{20,4},{24,8},{28,12},{32,48},... | collective-permute-start | bytes 36872 | tf_op jit(solution)/shard_map/ppermute | solution.py:95
  161.9 4.8 %collective-permute-start.26 = (f32[3,1024]{1,0:T(4,128)S(1)}, f32[3,1024]{1,0:T(4,128)S(1)}, u32[]{:S(2)}, u32[]{:S(2)}) collective-permute-start(f32[3,1024]{1,0:T(4,128)S(1)} %fusion.20), channel_id=1, source_target_pairs={{0,8},{4,12},{8,16},{12,20},{16,24},{20,28},{24,0},{28,4},{32,40},... | collective-permute-start | bytes 36872 | tf_op jit(solution)/shard_map/ppermute | solution.py:95
  163.9 12.2 %collective-permute-start.21 = (bf16[128,1024]{1,0:T(8,128)(2,1)S(1)}, bf16[128,1024]{1,0:T(8,128)(2,1)S(1)}, u32[]{:S(2)}, u32[]{:S(2)}) collective-permute-start(bf16[128,1024]{1,0:T(8,128)(2,1)S(1)} %get-tuple-element.118.c0_ref), channel_id=1, source_target_pairs={{0,3},{1,0},{2,1},{3,2},{4,7},{5,4},{6,5},{7,6},{8,11},{9,8},{10,9... | collective-permute-start | bytes 786440 | tf_op jit(solution)/shard_map/ppermute | solution.py:68
  164.9 11.2 %collective-permute-start.22 = (bf16[128,1024]{1,0:T(8,128)(2,1)S(1)}, bf16[128,1024]{1,0:T(8,128)(2,1)S(1)}, u32[]{:S(2)}, u32[]{:S(2)}) collective-permute-start(bf16[128,1024]{1,0:T(8,128)(2,1)S(1)} %get-tuple-element.118.c0_ref), channel_id=1, source_target_pairs={{0,2},{1,3},{2,0},{3,1},{4,6},{5,7},{6,4},{7,5},{8,10},{9,11},{10,... | collective-permute-start | bytes 786440 | tf_op jit(solution)/shard_map/ppermute | solution.py:68
  166.2 13.1 %collective-permute-start.23 = (bf16[128,1024]{1,0:T(8,128)(2,1)S(1)}, bf16[128,1024]{1,0:T(8,128)(2,1)S(1)}, u32[]{:S(2)}, u32[]{:S(2)}) collective-permute-start(bf16[128,1024]{1,0:T(8,128)(2,1)S(1)} %get-tuple-element.118.c0_ref), channel_id=1, source_target_pairs={{0,1},{1,2},{2,3},{3,0},{4,5},{5,6},{6,7},{7,4},{8,9},{9,10},{10,1... | collective-permute-start | bytes 786440 | tf_op jit(solution)/shard_map/ppermute | solution.py:68
  166.6 5.3 %collective-permute-start.28 = (f32[3,1024]{1,0:T(4,128)S(1)}, f32[3,1024]{1,0:T(4,128)S(1)}, u32[]{:S(2)}, u32[]{:S(2)}) collective-permute-start(f32[3,1024]{1,0:T(4,128)S(1)} %add_add_fusion.2), channel_id=1, source_target_pairs={{0,64},{4,68},{8,72},{12,76},{16,80},{20,84},{24,88},{28,92},{32,9... | collective-permute-start | bytes 36872 | tf_op jit(solution)/shard_map/ppermute | solution.py:95
  170.0 4.9 %collective-permute-start.29 = (f32[3,1024]{1,0:T(4,128)S(1)}, f32[3,1024]{1,0:T(4,128)S(1)}, u32[]{:S(2)}, u32[]{:S(2)}) collective-permute-start(f32[3,1024]{1,0:T(4,128)S(1)} %add_add_fusion.2), channel_id=1, source_target_pairs={{0,32},{4,36},{8,40},{12,44},{16,48},{20,52},{24,56},{28,60},{32,6... | collective-permute-start | bytes 36872 | tf_op jit(solution)/shard_map/ppermute | solution.py:95
  185.4 11.3 %collective-permute-start.31 = (bf16[32,4480]{1,0:T(8,128)(2,1)S(1)}, bf16[32,4480]{1,0:T(8,128)(2,1)S(1)}, u32[]{:S(2)}, u32[]{:S(2)}) collective-permute-start(bf16[32,4480]{1,0:T(8,128)(2,1)S(1)} %get-tuple-element.148), channel_id=1, source_target_pairs={{0,64},{4,68},{8,72},{12,76},{16,80},{20,84},{24,88},{28,92},{32,9... | collective-permute-start | bytes 860168 | tf_op jit(solution)/shard_map/ppermute | solution.py:86
  189.0 13.2 %collective-permute-start.32 = (bf16[32,4480]{1,0:T(8,128)(2,1)S(1)}, bf16[32,4480]{1,0:T(8,128)(2,1)S(1)}, u32[]{:S(2)}, u32[]{:S(2)}) collective-permute-start(bf16[32,4480]{1,0:T(8,128)(2,1)S(1)} %get-tuple-element.150), channel_id=1, source_target_pairs={{0,32},{4,36},{8,40},{12,44},{16,48},{20,52},{24,56},{28,60},{32,6... | collective-permute-start | bytes 860168 | tf_op jit(solution)/shard_map/ppermute | solution.py:86
  189.0 13.2 %collective-permute-start.33 = (bf16[32,4480]{1,0:T(8,128)(2,1)S(1)}, bf16[32,4480]{1,0:T(8,128)(2,1)S(1)}, u32[]{:S(2)}, u32[]{:S(2)}) collective-permute-start(bf16[32,4480]{1,0:T(8,128)(2,1)S(1)} %get-tuple-element.149), channel_id=1, source_target_pairs={{0,96},{4,100},{8,104},{12,108},{16,112},{20,116},{24,120},{28,124... | collective-permute-start | bytes 860168 | tf_op jit(solution)/shard_map/ppermute | solution.py:86
  (25 other events, 133.0 us)
Sparse Core Ops, SparseCore 0:
  89.7 66.9 all-reduce.2
Sparse Core Ops, SparseCore 1:
  92.6 44.7 reduce-scatter.2
  139.7 32.5 reduce-scatter.4

commit v3 on v2

--- a/solution.py
+++ b/solution.py
@@ -13,6 +13,7 @@
 FULL = jnp.float32
 MP = 4
 X_DIM = 4
+LANES = 128
 ORDER = (0, 1, 3, 2)
 Z_DIM = 4
 
@@ -77,25 +78,6 @@
     return me % 2, (me // 2) % X_DIM, me // (2 * X_DIM)
 
 
-def line_sum(part, name):
-    _, x, z = seq_place()
-    mine = x if name == "x" else z
-    total = take(part, mine, 0).astype(FULL)
-    for o in (2, 1, 3):
-        shift = seq_shift(0, o, 0) if name == "x" else seq_shift(o, 0, 0)
-        came = lax.ppermute(take(part, (mine + o) % 4, 0).astype(LOW), "seq", shift)
-        total = total + came.astype(FULL)
-    return total
-
-
-def all_sum(value):
-    value = value + lax.ppermute(value, "seq", seq_shift(0, 0, 1))
-    for dz, dx in ((0, 1), (1, 0)):
-        shifts = [seq_shift(dz * o, dx * o, 0) for o in (2, 1, 3)]
-        value = value + sum(lax.ppermute(value, "seq", shift) for shift in shifts)
-    return value
-
-
 def chip_line_scatter(part):
     groups = [
         [seq_index(z, x, core) for x in range(X_DIM) for core in range(2)] for z in range(Z_DIM)
@@ -132,7 +114,7 @@
     return pl.BlockSpec((rows, width), lambda i, s, t: ((s[0] + o) % MP, 0))
 
 
-def call(kernel, place, inputs, outs, grid=1, vmem=0, scratch=()):
+def call(kernel, place, inputs, outs, grid=1, vmem=0, scratch=(), flops=0):
     in_specs = [spec or whole(array.shape) for array, spec in inputs]
     out_specs = [spec or whole(shape) for shape, _, spec in outs]
     held = 0
@@ -148,7 +130,7 @@
         ),
         out_shape=[jax.ShapeDtypeStruct(shape, dtype) for shape, dtype, _ in outs],
         compiler_params=pltpu.CompilerParams(vmem_limit_bytes=vmem or 2 * held + (8 << 20)),
-        cost_estimate=pl.CostEstimate(flops=0, bytes_accessed=0, transcendentals=0),
+        cost_estimate=pl.CostEstimate(flops=flops, bytes_accessed=0, transcendentals=0),
     )(*place, *[array for array, _ in inputs])
 
 
@@ -286,7 +268,7 @@
 def mix_back_kernel(
     s_ref, t_ref, g0_ref, g1_ref, g2_ref, g3_ref, gated_ref, head_ref, head_c_ref, b_ref, c_ref, x_ref,
     convolved_ref, tail_mixed_ref, conv_ref, out_ref, w_ref, normed_ref, gain_ref,
-    ffn_gain_ref, part_ref, conv_part_ref, p0_ref, p1_ref, p2_ref, p3_ref,
+    ffn_gain_ref, part_ref, p0_ref, p1_ref, p2_ref, p3_ref,
 ):
     out_weight = out_ref[...]
     conv = conv_ref[...]
@@ -301,9 +283,9 @@
     place, keep_one, keep_two, tap_one, tap_two = taps(s_ref, t_ref, mixed, tail_mixed_ref[...])
     rows = mixed.shape[0]
     grad_conv = grad_gated * c_part
-    conv_part_ref[...] = jnp.concatenate(
-        [jnp.sum(grad_conv * tap, axis=0, keepdims=True) for tap in (tap_two, tap_one, mixed)], 0
-    )
+    conv_part = [
+        jnp.sum(grad_conv * tap, axis=0, keepdims=True) for tap in (tap_two, tap_one, mixed)
+    ]
     to_one = jnp.where(keep_one, conv[1:2] * grad_conv, 0.0)
     to_two = jnp.where(keep_two, conv[0:1] * grad_conv, 0.0)
     from_one = pltpu.roll(to_one, rows - 1, 0)
@@ -327,7 +309,7 @@
             dot(turned, grad).astype(LOW), SCATTER_ORDER
         )
     branch = jnp.concatenate([ref[...] for ref in (g0_ref, g1_ref, g2_ref, g3_ref)], 0)
-    part_ref[:, 3 * columns :] = slabs_of(
+    part_ref[:, 3 * columns : 4 * columns] = slabs_of(
         dot(jnp.transpose(branch), gated_ref[...]).astype(LOW), SCATTER_ORDER
     )
     quarter_rows = rows // MP
@@ -336,29 +318,46 @@
     for o, ref in enumerate(sends):
         cut = slice(o * quarter_rows, (o + 1) * quarter_rows)
         part = sum(dot(grads[k][cut], w_ref[k], BY_ROWS) for k in range(3))
-        ref[:quarter_rows, :] = part.astype(ref.dtype)
+        ref[...] = part.astype(ref.dtype)
         gain_part = gain_part + jnp.sum(
             part * normed_ref[cut, :].astype(FULL), axis=0, keepdims=True
         )
-    spare = jnp.zeros((14, gain_part.shape[1]), FULL)
-    small = jnp.concatenate([gain_part / gain_ref[...], ffn_gain_ref[...], spare], 0)
-    for ref in sends:
-        ref[quarter_rows:, :] = small.astype(ref.dtype)
+    conv_row = jnp.concatenate([*conv_part, jnp.zeros_like(conv_part[0])], 1)
+    small = [gain_part / gain_ref[...], ffn_gain_ref[...], conv_row]
+    lanes = part_ref.shape[1] - 4 * columns
+    pieces = [row[:, i : i + lanes] for row in small for i in range(0, row.shape[1], lanes)]
+    tile = jnp.concatenate([*pieces, jnp.zeros((8, lanes), FULL)], 0).astype(LOW)
+    part_ref[:, 4 * columns :] = jnp.concatenate([tile] * (part_ref.shape[0] // 32), 0)
 
 
 def hidden_kernel(
-    s_ref, t_ref, p0_ref, r1_ref, r2_ref, r3_ref, hidden_ref, gain_ref, grad_ref,
-    low_ref, small_ref,
+    s_ref, t_ref, p0_ref, r1_ref, r2_ref, r3_ref, hidden_ref, gain_ref, grad_ref, low_ref
 ):
     total = p0_ref[...]
     for ref in (r1_ref, r2_ref, r3_ref):
         total = total + ref[...].astype(FULL)
-    rows = hidden_ref.shape[0]
-    small_ref[...] = total[rows:]
     hidden = hidden_ref[...]
     inv = inv_rms(hidden)
-    grad = grad_ref[...] + norm_back(total[:rows] * gain_ref[...], hidden * inv, inv)
+    grad = grad_ref[...] + norm_back(total * gain_ref[...], hidden * inv, inv)
     low_ref[...] = grad.astype(LOW)
+
+
+def finish_kernel(s_ref, t_ref, *refs):
+    in_ref, out_ref, gate_up_ref, down_ref, small_ref = refs[8:]
+
+    def total(parts, start, size):
+        return sum(ref[:, start : start + size].astype(FULL) for ref in parts)
+
+    ffn_parts, mix_parts = refs[:4], refs[4:8]
+    units = down_ref.shape[1]
+    channels = out_ref.shape[1]
+    for k in range(2):
+        gate_up_ref[k] = total(ffn_parts, k * units, units)
+    down_ref[...] = total(ffn_parts, 2 * units, units)
+    for k in range(3):
+        in_ref[k] = total(mix_parts, k * channels, channels)
+    out_ref[...] = total(mix_parts, 3 * channels, channels)
+    small_ref[...] = total(mix_parts, 4 * channels, LANES)
 
 
 def on_device(
@@ -458,7 +457,9 @@
         vmem=BIG,
     )[0]
     ffn_out = lax.psum(ffn_part, "mp")
-    normed_two, active, grad_gu, grad_low = after(
+    head_c = lax.dynamic_slice_in_dim(after(c_part, came_near[0]), natural, 8, 0)
+    head_c = slab_shift(head_c, -1)
+    normed_two, active_late, grad_gu, grad_low = after(
         (normed_two, active, grad_gu, grad_low), came_near[0]
     )
     block = hidden_units
@@ -468,7 +469,7 @@
     ffn_grad_part = call(
         functools.partial(ffn_grad_kernel, steps),
         place,
-        [(normed_two, None), (grad_gu, gate_up_block), (grad_low, None), (active, down_block)],
+        [(normed_two, None), (grad_gu, gate_up_block), (grad_low, None), (active_late, down_block)],
         [
             (
                 (width, 3 * hidden_units),
@@ -479,10 +480,9 @@
         grid=3 * hidden_units // block,
         scratch=[pltpu.VMEM((width, rows), LOW)],
         vmem=BIG,
+        flops=10**10,
     )[0]
     ffn_line = chip_line_scatter(ffn_grad_part)
-    head_c = lax.dynamic_slice_in_dim(after(c_part, near_low), natural, 8, 0)
-    head_c = slab_shift(head_c, -1)
     came, ffn_part, head_c, ffn_grad_part = lax.optimization_barrier(
         (tuple(came), ffn_part, head_c, ffn_grad_part)
     )
@@ -493,9 +493,8 @@
         [quarter_full, quarter_low, ((1, width), FULL, None)],
         vmem=BIG,
     )
-    branches = {o: lax.ppermute(grad_branch, "mp", ring_shift(MP, -o)) for o in (1, 3)}
+    branches = gather_rows(grad_branch)
     head = head_spread(grad_branch[:16])
-    branches[2] = lax.ppermute(after(grad_branch, head), "mp", ring_shift(MP, 2))
     branches, head = lax.optimization_barrier((branches, head))
 
     outs = call(
@@ -510,24 +509,53 @@
                 out_weight, w_in, normed, mix_gain, ffn_gain_part,
             )
         ],
-        [((width, 4 * channels), LOW, None), ((3, channels), FULL, None)]
-        + [((mine + 16, width), LOW if o else FULL, None) for o in range(MP)],
+        [((width, 4 * channels + LANES), LOW, None)]
+        + [quarter_full, quarter_low, quarter_low, quarter_low],
         vmem=BIG,
-    )
-    in_out_part, conv_part, p0, p1, p2, p3 = outs
+        flops=10**10,
+    )
+    in_out_part, p0, p1, p2, p3 = outs
     in_out_line = chip_line_scatter(in_out_part)
     came = send_rows({1: p1, 2: p2, 3: p3})
-    hidden_low, small = call(
+    came, ffn_line, ffn_out = lax.optimization_barrier((came, ffn_line, ffn_out))
+    hidden_low = call(
         hidden_kernel,
         place,
         [(v, None) for v in (p0, came[1], came[2], came[3])]
-        + [(hidden_in, own_rows), (mix_gain, None), (grad_middle, None)],
-        [quarter_low, ((16, width), FULL, None)],
-    )
+        + [(hidden_in, own_rows)]
+        + [(v, None) for v in (mix_gain, grad_middle)],
+        [quarter_low],
+        vmem=BIG,
+    )[0]
     ends = gather_rows(hidden_low)
-    conv_row = jnp.pad(conv_part.reshape(1, -1), ((0, 0), (0, width - 3 * channels)))
-    small = all_sum(jnp.concatenate([small[:2], conv_row], 0))
-    ends, ffn_out, ffn_line = lax.optimization_barrier((ends, ffn_out, ffn_line))
+    z = seq_place()[2]
+
+    def along_z(line):
+        line = line.reshape(Z_DIM, 32, -1)
+        return [take(line, z, 0)] + [
+            lax.ppermute(take(line, (z + o) % Z_DIM, 0), "seq", seq_shift(o, 0, 0))
+            for o in (1, 2, 3)
+        ]
+
+    ffn_parts = along_z(after(ffn_line, hidden_low))
+    in_out_line, ffn_parts = lax.optimization_barrier((after(in_out_line, ends), ffn_parts))
+    lines = [*ffn_parts, *along_z(in_out_line)]
+    in_done, out_done, gate_up_done, down_done, small = call(
+        finish_kernel,
+        place,
+        [(v, None) for v in lines],
+        [
+            ((3, 32, channels), FULL, None),
+            ((32, channels), FULL, None),
+            ((2, 32, hidden_units), FULL, None),
+            ((32, hidden_units), FULL, None),
+            ((32, LANES), FULL, None),
+        ],
+    )
+    gains = small[: 2 * width // LANES]
+    gains = gains + sum(lax.ppermute(gains, "mp", ring_shift(MP, o)) for o in (2, 1, 3))
+    gains = gains.reshape(2, width)
+    taps_grad = small[2 * width // LANES : (2 * width + 3 * channels) // LANES]
     chunk = pl.BlockSpec((mine, width), lambda i, s, t: ((s[0] + i) % MP, 0))
     hidden_grad = call(
         place_kernel,
@@ -543,24 +571,16 @@
         [((rows, width), FULL, chunk)],
         grid=MP,
     )[0]
-    in_out_line, small = after((in_out_line, small), hidden_grad, hidden_out)
-    line = jnp.concatenate([ffn_line, in_out_line], 1).reshape(Z_DIM, 32, -1)
-    done = line_sum(line, "z")
-    ffn_done = done[:, : 3 * hidden_units]
-    in_out_done = done[:, 3 * hidden_units :]
-    mix_gain_grad, ffn_gain_grad = small[0], small[1]
-    conv_weight_grad = small[2, : 3 * channels].reshape(3, channels)
-    local = in_out_done.shape[0]
     return (
         hidden_out,
         hidden_grad,
-        mix_gain_grad,
-        in_out_done[:, : 3 * channels].reshape(local, 3, channels),
-        conv_weight_grad,
-        in_out_done[:, 3 * channels :].T,
-        ffn_gain_grad,
-        ffn_done[:, : 2 * hidden_units].reshape(local, 2, hidden_units),
-        ffn_done[:, 2 * hidden_units :].T,
+        gains[0],
+        jnp.transpose(in_done, (1, 0, 2)),
+        taps_grad.reshape(3, channels),
+        out_done.T,
+        gains[1],
+        jnp.transpose(gate_up_done, (1, 0, 2)),
+        down_done.T,
     )
 
 

time: 216 us -> 211 us (0.977); the launches traced: 213 us -> 210 us
  waiting for transfers between devices: 72.4 us -> 67.7 us
  Pallas kernels: 35.1 us -> 39.4 us
    ppermute x13 -> x9, waiting for transfers between devices: 29.5 us -> 5.95 us  [the longest x6 5.95 us: along_z(): lax.ppermute(take(line, (z + o) % Z_DIM, 0), 'seq', seq_shift(o, 0, 0))]
    ppermute x6 -> x9, waiting for transfers between devices: 12.1 us -> 25.5 us  [gather_rows(): return {o: lax.ppermute(rows, 'mp', ring_shift(MP, -o)) for o in order}]
    pallas_call x9 -> x10, Pallas kernels: 35.1 us -> 39.4 us  [call(): pl.pallas_call(kernel, grid_spec=pltpu.PrefetchScalarGridSpec(num_scalar_...]
    ppermute x1, waiting for transfers between devices: 0.6 us -> 4.9 us  [on_device(): lax.ppermute(near_low[mine:2 * mine], 'mp', ring_shift(MP, 1))]
    ppermute x6, waiting for transfers between devices: 27 us -> 23.8 us  [send_rows(): lax.ppermute(parts[o], 'mp', ring_shift(MP, o))]
    squeeze x1 -> x2, local copies, waits for them, and re-layouts: 0.1 us -> 3.14 us  [take(): return lax.dynamic_index_in_dim(value, index, axis, keepdims=False)]
    ppermute x13 -> x9, starting transfers between devices: 22 us -> 19.4 us  [the longest x6 12.8 us: along_z(): lax.ppermute(take(line, (z + o) % Z_DIM, 0), 'seq', seq_shift(o, 0, 0))]
    ppermute x6 -> x9, starting transfers between devices: 8.87 us -> 10.8 us  [gather_rows(): return {o: lax.ppermute(rows, 'mp', ring_shift(MP, -o)) for o in order}]
  transfers between devices with their start and end apart: 37 -> 36, of which waited for: 18 -> 21; matrix products, arithmetic and copies ran while one was open for 8% -> 8% of each run, Pallas kernels for 14% -> 15%
where the time goes in v3:
time: 211 us; the launch traced here: 210 us
  waiting for transfers between devices  67.7 us (32%)
  starting transfers between devices  55.5 us (26%)
  Pallas kernels  39.4 us (19%)
  between operations  16.5 us (8%)
  local copies, waits for them, and re-layouts  15.1 us (7%)
  matrix products  8.05 us (4%)
  other arithmetic  7.91 us (4%)
    pallas_call x10, Pallas kernels, call(): pl.pallas_call(kernel, grid_spec=pltpu.PrefetchScalarGridSpec(num_scalar_...  39.4 us
    ppermute x9, waiting for transfers between devices, gather_rows(): return {o: lax.ppermute(rows, 'mp', ring_shift(MP, -o)) for o in order}  25.5 us
    ppermute x6, waiting for transfers between devices, send_rows(): lax.ppermute(parts[o], 'mp', ring_shift(MP, o))  23.8 us
    ppermute x6, starting transfers between devices, along_z(): lax.ppermute(take(line, (z + o) % Z_DIM, 0), 'seq', seq_shift(o, 0, 0))  12.8 us
    ppermute x6, starting transfers between devices, send_rows(): lax.ppermute(parts[o], 'mp', ring_shift(MP, o))  12.1 us
    ppermute x9, starting transfers between devices, gather_rows(): return {o: lax.ppermute(rows, 'mp', ring_shift(MP, -o)) for o in order}  10.8 us
    dot_general x5, matrix products, dot(): lax.dot_general(left, right, (contract, ((), ())), preferred_element_type...  8.05 us
    unnamed x50, local copies, waits for them, and re-layouts  7.65 us
  transfers between devices with their start and end apart: 36, of which 21 were waited for; matrix products, arithmetic and copies ran while one was open for 8% of the time, Pallas kernels for 15%

profile of v3, /device:TPU:2, one launch (start us, length us, event | category | flops | bytes accessed | tf_op | source)
XLA Modules:
  0.0 210.3 jit_solution(2922022624773849974)
XLA Ops:
  11.4 2.7 %collective-permute-done.tail_ref = f32[8,1024]{1,0:T(8,128)S(1)} collective-permute-done((f32[8,1024]{1,0:T(8,128)S(1)}, f32[8,1024]{1,0:T(8,128)S(1)}, u32[]{:S(2)}, u32[]{:S(2)}) %collective-permute-start) | collective-permute-done | bytes 32800 | tf_op jit(solution)/shard_map/ppermute | solution.py:44
  14.7 5.6 %shard_map.169 = (bf16[512,1024]{1,0:T(8,128)(2,1)}, f32[512,256]{1,0:T(8,128)}, f32[512,256]{1,0:T(8,128)}, f32[512,256]{1,0:T(8,128)}, bf16[512,256]{1,0:T(8,1...) custom-call(s32[1]{0:T(128)} %bitcast.s_ref, ...), custom_call_target="tpu_custom_call" | custom-call | tf_op jit(solution)/shard_map/pallas_call | solution.py:125
  21.8 2.9 %collective-permute-start.2 = (bf16[128,1024]{1,0:T(8,128)(2,1)}, bf16[128,1024]{1,0:T(8,128)(2,1)S(1)}, u32[]{:S(2)}, u32[]{:S(2)}) collective-permute-start(bf16[128,1024]{1,0:T(8,128)(2,1)} %get-tuple-element.77), channel_id=1, source_target_pairs={{0,2},{1,3},{2,0},{3,1},{4,6},{5,7},{6,4},{7,5},{8,10},{9,11},{10,... | collective-permute-start | bytes 786440 | tf_op jit(solution)/shard_map/ppermute | solution.py:65
  26.1 3.7 %collective-permute-done.1.r1_ref = bf16[128,1024]{1,0:T(8,128)(2,1)S(1)} collective-permute-done((bf16[128,1024]{1,0:T(8,128)(2,1)}, bf16[128,1024]{1,0:T(8,128)(2,1)S(1)}, u32[]{:S(2)}, u32[]{:S(2)}) %collective-permute-start.1) | collective-permute-done | bytes 262176 | tf_op jit(solution)/shard_map/ppermute | solution.py:65
  29.8 3.3 %copy.20 = bf16[128,8,2,1152]{3,1,2,0:T(8,128)(2,1)S(1)} copy(bf16[128,8,2,1152]{3,2,1,0:T(2,128)(2,1)} %bitcast.44) | data formatting | bytes 9437184
  33.1 2.9 %collective-permute-done.2.r2_ref = bf16[128,1024]{1,0:T(8,128)(2,1)S(1)} collective-permute-done((bf16[128,1024]{1,0:T(8,128)(2,1)}, bf16[128,1024]{1,0:T(8,128)(2,1)S(1)}, u32[]{:S(2)}, u32[]{:S(2)}) %collective-permute-start.2) | collective-permute-done | bytes 262176 | tf_op jit(solution)/shard_map/ppermute | solution.py:65
  37.0 2.1 %collective-permute-start.4 = (bf16[128,1024]{1,0:T(8,128)(2,1)S(1)}, bf16[128,1024]{1,0:T(8,128)(2,1)S(1)}, u32[]{:S(2)}, u32[]{:S(2)}) collective-permute-start(bf16[128,1024]{1,0:T(8,128)(2,1)S(1)} %get-tuple-element.83.c0_ref), channel_id=1, source_target_pairs={{0,3},{1,0},{2,1},{3,2},{4,7},{5,4},{6,5},{7,6},{8,11},{9,8},{10,9... | collective-permute-start | bytes 786440 | tf_op jit(solution)/shard_map/ppermute | solution.py:69
  39.2 4.0 %collective-permute-start.6 = (bf16[128,1024]{1,0:T(8,128)(2,1)S(1)}, bf16[128,1024]{1,0:T(8,128)(2,1)S(1)}, u32[]{:S(2)}, u32[]{:S(2)}) collective-permute-start(bf16[128,1024]{1,0:T(8,128)(2,1)S(1)} %get-tuple-element.83.c0_ref), channel_id=1, source_target_pairs={{0,2},{1,3},{2,0},{3,1},{4,6},{5,7},{6,4},{7,5},{8,10},{9,11},{10,... | collective-permute-start | bytes 786440 | tf_op jit(solution)/shard_map/ppermute | solution.py:69
  44.9 5.5 %collective-permute-done.4.c1_ref = bf16[128,1024]{1,0:T(8,128)(2,1)S(1)} collective-permute-done((bf16[128,1024]{1,0:T(8,128)(2,1)S(1)}, bf16[128,1024]{1,0:T(8,128)(2,1)S(1)}, u32[]{:S(2)}, u32[]{:S(2)}) %collective-permute-start.4) | collective-permute-done | bytes 262176 | tf_op jit(solution)/shard_map/ppermute | solution.py:69
  50.4 3.4 %collective-permute-done.5.c3_ref = bf16[128,1024]{1,0:T(8,128)(2,1)S(1)} collective-permute-done((bf16[128,1024]{1,0:T(8,128)(2,1)S(1)}, bf16[128,1024]{1,0:T(8,128)(2,1)S(1)}, u32[]{:S(2)}, u32[]{:S(2)}) %collective-permute-start.5) | collective-permute-done | bytes 262176 | tf_op jit(solution)/shard_map/ppermute | solution.py:69
  57.6 2.0 fusion.7
  69.5 4.5 %shard_map.171 = bf16[512,1024]{1,0:T(8,128)(2,1)} custom-call(s32[1]{0:T(128)} %bitcast.s_ref, s32[1]{0:T(128)S(6)} %copy.22.t_ref, bf16[512,1152]{1,0:T(8,128)(2,1)} %pad_maximum_fusion.active_ref, bf16[1152,1024]{1,0:T(8,128)(2,1)} %down_ref.1), custom_call_target="tpu_custom_call" | custom-call | tf_op jit(solution)/shard_map/pallas_call | solution.py:125
  75.5 4.9 %collective-permute-done.7.r1_ref = bf16[128,1024]{1,0:T(8,128)(2,1)S(1)} collective-permute-done((bf16[128,1024]{1,0:T(8,128)(2,1)S(1)}, bf16[128,1024]{1,0:T(8,128)(2,1)S(1)}, u32[]{:S(2)}, u32[]{:S(2)}) %collective-permute-start.7) | collective-permute-done | bytes 262176 | tf_op jit(solution)/shard_map/ppermute | solution.py:439
  81.2 2.1 %collective-permute-start.10 = (f32[8,256]{1,0:T(8,128)S(1)}, f32[8,256]{1,0:T(8,128)S(1)}, u32[]{:S(2)}, u32[]{:S(2)}) collective-permute-start(f32[8,256]{1,0:T(8,128)S(1)} %constant_dynamic-slice_fusion), channel_id=1, source_target_pairs={{4,0},{8,4},{12,8},{16,12},{20,16},{24,20},{28,24},{32,28},{36,32}... | collective-permute-start | bytes 24584 | tf_op jit(solution)/shard_map/ppermute | solution.py:44
  83.3 9.1 %shard_map.172 = bf16[1024,3456]{1,0:T(8,128)(2,1)} custom-call(s32[1]{0:T(128)} %bitcast.s_ref, s32[1]{0:T(128)S(6)} %copy.22.t_ref, bf16[512,1024]{1,0:T(8,128)(2,1)} %get-tuple-element.97.normed_ref, bf16[512,2304]{1,0:T(8,128)(2,1)} %maximum_maximum_fusion.grad_gu_ref, bf16[512,1024]{1,0:T(8,128)(2,1)} %get-tuple-element.99.low_ref, ...), custom_call_target="tpu_custom_call" | custom-call | flops 10000000000 | tf_op jit(solution)/shard_map/pallas_call | solution.py:125
  93.2 2.8 %shard_map.173 = (f32[128,1024]{1,0:T(8,128)}, bf16[128,1024]{1,0:T(8,128)(2,1)}, f32[1,1024]{1,0:T(1,128)}) custom-call(s32[1]{0:T(128)} %bitcast.s_ref, s32[1]{0:T(128)S(6)} %copy.22.t_ref, bf16[128,1024]{1,0:T(8,128)(2,1)} %get-tuple-element.166.p0_ref, bf16[128,1024]{1,0:T(8,128)(2,1)} %copy-done.9, bf16[128,1024]{1,0:T(8,128)(2,1)} %copy-done.11, ...), custom_call_target="tpu_custom_call" | custom-call | tf_op jit(solution)/shard_map/pallas_call | solution.py:125
  107.0 7.6 %collective-permute-done.11.g1_ref = bf16[128,1024]{1,0:T(8,128)(2,1)S(1)} collective-permute-done((bf16[128,1024]{1,0:T(8,128)(2,1)}, bf16[128,1024]{1,0:T(8,128)(2,1)S(1)}, u32[]{:S(2)}, u32[]{:S(2)}) %collective-permute-start.11) | collective-permute-done | bytes 262176 | tf_op jit(solution)/shard_map/ppermute | solution.py:69
  115.4 6.9 %collective-permute-done.13.g3_ref = bf16[128,1024]{1,0:T(8,128)(2,1)S(1)} collective-permute-done((bf16[128,1024]{1,0:T(8,128)(2,1)}, bf16[128,1024]{1,0:T(8,128)(2,1)S(1)}, u32[]{:S(2)}, u32[]{:S(2)}) %collective-permute-start.13) | collective-permute-done | bytes 262176 | tf_op jit(solution)/shard_map/ppermute | solution.py:69
  123.1 9.2 %shard_map.174 = (bf16[1024,1152]{1,0:T(8,128)(2,1)}, f32[128,1024]{1,0:T(8,128)}, bf16[128,1024]{1,0:T(8,128)(2,1)}, bf16[128,1024]{1,0:T(8,128)(2,1)}, bf16[128,1024]{1,0:T(8,128)(2,1)}) custom-call(s32[1]{0:T(128)} %bitcast.s_ref, s32[1]{0:T(128)S(6)} %copy.22.t_ref, bf16[128,1024]{1,0:T(8,128)(2,1)} %get-tuple-element.105.g0_ref, ...), custom_call_target="tpu_custom_call" | custom-call | flops 10000000000 | tf_op jit(solution)/shard_map/pallas_call | solution.py:125
  133.9 3.1 %collective-permute-start.19 = (bf16[128,1024]{1,0:T(8,128)(2,1)S(1)}, bf16[128,1024]{1,0:T(8,128)(2,1)S(1)}, u32[]{:S(2)}, u32[]{:S(2)}) collective-permute-start(bf16[128,1024]{1,0:T(8,128)(2,1)S(1)} %copy-done.18), channel_id=1, source_target_pairs={{0,2},{1,3},{2,0},{3,1},{4,6},{5,7},{6,4},{7,5},{8,10},{9,11},{10,... | collective-permute-start | bytes 786440 | tf_op jit(solution)/shard_map/ppermute | solution.py:65
  137.0 2.5 %collective-permute-start.20 = (bf16[128,1024]{1,0:T(8,128)(2,1)S(1)}, bf16[128,1024]{1,0:T(8,128)(2,1)S(1)}, u32[]{:S(2)}, u32[]{:S(2)}) collective-permute-start(bf16[128,1024]{1,0:T(8,128)(2,1)S(1)} %copy-done.17), channel_id=1, source_target_pairs={{0,3},{1,0},{2,1},{3,2},{4,7},{5,4},{6,5},{7,6},{8,11},{9,8},{10,9... | collective-permute-start | bytes 786440 | tf_op jit(solution)/shard_map/ppermute | solution.py:65
  139.5 9.2 %collective-permute-done.18.r1_ref = bf16[128,1024]{1,0:T(8,128)(2,1)S(1)} collective-permute-done((bf16[128,1024]{1,0:T(8,128)(2,1)S(1)}, bf16[128,1024]{1,0:T(8,128)(2,1)S(1)}, u32[]{:S(2)}, u32[]{:S(2)}) %collective-permute-start.18) | collective-permute-done | bytes 262176 | tf_op jit(solution)/shard_map/ppermute | solution.py:65
  148.8 7.9 %collective-permute-done.19.r2_ref = bf16[128,1024]{1,0:T(8,128)(2,1)S(1)} collective-permute-done((bf16[128,1024]{1,0:T(8,128)(2,1)S(1)}, bf16[128,1024]{1,0:T(8,128)(2,1)S(1)}, u32[]{:S(2)}, u32[]{:S(2)}) %collective-permute-start.19) | collective-permute-done | bytes 262176 | tf_op jit(solution)/shard_map/ppermute | solution.py:65
  157.5 2.6 %shard_map.176.c0_ref = bf16[128,1024]{1,0:T(8,128)(2,1)} custom-call(s32[1]{0:T(128)} %bitcast.s_ref, s32[1]{0:T(128)S(6)} %copy.22.t_ref, f32[128,1024]{1,0:T(8,128)} %get-tuple-element.122.p0_ref, bf16[128,1024]{1,0:T(8,128)(2,1)} %copy-done.12, bf16[128,1024]{1,0:T(8,128)(2,1)} %copy-done.13, bf16[128,1024]{1,0:T(8,128)(2,1)} %copy-done.14, ...), custom_call_target="tpu_custom_call" | custom-call | tf_op jit(solution)/shard_map/pallas_call | solution.py:125
  162.7 2.1 %dynamic-slice_bitcast_fusion = (bf16[32,3456]{1,0:T(8,128)(2,1)}, bf16[32,3456]{1,0:T(8,128)(2,1)}, bf16[32,3456]{1,0:T(8,128)(2,1)}, bf16[32,3456]{1,0:T(8,128)(2,1)S(1)}) fusion(bf16[4,32,3456]{2,1,0:T(8,128)(2,1)} %bitcast.47, s32[]{:T(128)S(6)} %select_n.95, s32[]{:T(128)S(6)} %select_n.93, s32[]{:T(128)S(6)} %select_n.91, s32[]{:T(128)S(6)} %select_n.89), kind=kLoop, calls=%fused_computation.36 | loop fusion | bytes 1769488 | tf_op jit(solution)/shard_map/jit(dynamic_index_in_dim)/squeeze | solution.py:73
  166.4 2.9 %collective-permute-start.25 = (bf16[32,3456]{1,0:T(8,128)(2,1)}, bf16[32,3456]{1,0:T(8,128)(2,1)S(1)}, u32[]{:S(2)}, u32[]{:S(2)}) collective-permute-start(bf16[32,3456]{1,0:T(8,128)(2,1)} %get-tuple-element.161), channel_id=1, source_target_pairs={{0,64},{4,68},{8,72},{12,76},{16,80},{20,84},{24,88},{28,92},{32,9... | collective-permute-start | bytes 663560 | tf_op jit(solution)/shard_map/ppermute | solution.py:536
  169.5 3.0 %collective-permute-start.26 = (bf16[32,3456]{1,0:T(8,128)(2,1)}, bf16[32,3456]{1,0:T(8,128)(2,1)}, u32[]{:S(2)}, u32[]{:S(2)}) collective-permute-start(bf16[32,3456]{1,0:T(8,128)(2,1)} %get-tuple-element.160), channel_id=1, source_target_pairs={{0,96},{4,100},{8,104},{12,108},{16,112},{20,116},{24,120},{28,124... | collective-permute-start | bytes 663560 | tf_op jit(solution)/shard_map/ppermute | solution.py:536
  175.5 2.7 %collective-permute-done.25.refs_2_ = bf16[32,3456]{1,0:T(8,128)(2,1)S(1)} collective-permute-done((bf16[32,3456]{1,0:T(8,128)(2,1)}, bf16[32,3456]{1,0:T(8,128)(2,1)S(1)}, u32[]{:S(2)}, u32[]{:S(2)}) %collective-permute-start.25) | collective-permute-done | bytes 221216 | tf_op jit(solution)/shard_map/ppermute | solution.py:536
  179.3 2.1 %collective-permute-start.27 = (bf16[32,1152]{1,0:T(8,128)(2,1)S(1)}, bf16[32,1152]{1,0:T(8,128)(2,1)S(1)}, u32[]{:S(2)}, u32[]{:S(2)}) collective-permute-start(bf16[32,1152]{1,0:T(8,128)(2,1)S(1)} %get-tuple-element.169), channel_id=1, source_target_pairs={{0,32},{4,36},{8,40},{12,44},{16,48},{20,52},{24,56},{28,60},{32,6... | collective-permute-start | bytes 221192 | tf_op jit(solution)/shard_map/ppermute | solution.py:536
  181.4 2.1 %collective-permute-start.28 = (bf16[32,1152]{1,0:T(8,128)(2,1)S(1)}, bf16[32,1152]{1,0:T(8,128)(2,1)S(1)}, u32[]{:S(2)}, u32[]{:S(2)}) collective-permute-start(bf16[32,1152]{1,0:T(8,128)(2,1)S(1)} %get-tuple-element.168), channel_id=1, source_target_pairs={{0,64},{4,68},{8,72},{12,76},{16,80},{20,84},{24,88},{28,92},{32,9... | collective-permute-start | bytes 221192 | tf_op jit(solution)/shard_map/ppermute | solution.py:536
  189.6 3.4 %collective-permute-start.30 = (f32[16,128]{1,0:T(8,128)S(1)}, f32[16,128]{1,0:T(8,128)S(1)}, u32[]{:S(2)}, u32[]{:S(2)}) collective-permute-start(f32[16,128]{1,0:T(8,128)S(1)} %slice.58), channel_id=1, source_target_pairs={{0,2},{1,3},{2,0},{3,1},{4,6},{5,7},{6,4},{7,5},{8,10},{9,11},{10,... | collective-permute-start | bytes 24584 | tf_op jit(solution)/shard_map/ppermute | solution.py:556
  193.0 3.2 %collective-permute-start.32 = (f32[16,128]{1,0:T(8,128)S(1)}, f32[16,128]{1,0:T(8,128)S(1)}, u32[]{:S(2)}, u32[]{:S(2)}) collective-permute-start(f32[16,128]{1,0:T(8,128)S(1)} %slice.58), channel_id=1, source_target_pairs={{0,3},{1,0},{2,1},{3,2},{4,7},{5,4},{6,5},{7,6},{8,11},{9,8},{10,9... | collective-permute-start | bytes 24584 | tf_op jit(solution)/shard_map/ppermute | solution.py:556
  (134 shorter events, 61.5 us)
Async XLA Ops:
  8.0 149.3 %all-reduce.2.cloned.1.call-start = ((), (), s32[]{:S(2)}) async-start(), calls=%async_computation.3 | async-start | bytes 2097152 | tf_op jit(solution)/shard_map/psum | solution.py:459
  8.8 5.2 %collective-permute-start = (f32[8,1024]{1,0:T(8,128)S(1)}, f32[8,1024]{1,0:T(8,128)S(1)}, u32[]{:S(2)}, u32[]{:S(2)}) collective-permute-start(f32[8,1024]{1,0:T(8,128)S(1)} %slice.47), channel_id=1, source_target_pairs={{0,4},{4,8},{8,12},{12,16},{16,20},{20,24},{24,28},{28,32},{32,36}... | collective-permute-start | bytes 98312 | tf_op jit(solution)/shard_map/ppermute | solution.py:44
  20.2 9.5 %collective-permute-start.1 = (bf16[128,1024]{1,0:T(8,128)(2,1)}, bf16[128,1024]{1,0:T(8,128)(2,1)S(1)}, u32[]{:S(2)}, u32[]{:S(2)}) collective-permute-start(bf16[128,1024]{1,0:T(8,128)(2,1)} %get-tuple-element.76), channel_id=1, source_target_pairs={{0,1},{1,2},{2,3},{3,0},{4,5},{5,6},{6,7},{7,4},{8,9},{9,10},{10,1... | collective-permute-start | bytes 786440 | tf_op jit(solution)/shard_map/ppermute | solution.py:65
  21.8 14.2 %collective-permute-start.2 = (bf16[128,1024]{1,0:T(8,128)(2,1)}, bf16[128,1024]{1,0:T(8,128)(2,1)S(1)}, u32[]{:S(2)}, u32[]{:S(2)}) collective-permute-start(bf16[128,1024]{1,0:T(8,128)(2,1)} %get-tuple-element.77), channel_id=1, source_target_pairs={{0,2},{1,3},{2,0},{3,1},{4,6},{5,7},{6,4},{7,5},{8,10},{9,11},{10,... | collective-permute-start | bytes 786440 | tf_op jit(solution)/shard_map/ppermute | solution.py:65
  24.7 11.3 %collective-permute-start.3 = (bf16[128,1024]{1,0:T(8,128)(2,1)}, bf16[128,1024]{1,0:T(8,128)(2,1)S(1)}, u32[]{:S(2)}, u32[]{:S(2)}) collective-permute-start(bf16[128,1024]{1,0:T(8,128)(2,1)} %get-tuple-element.78), channel_id=1, source_target_pairs={{0,3},{1,0},{2,1},{3,2},{4,7},{5,4},{6,5},{7,6},{8,11},{9,8},{10,9... | collective-permute-start | bytes 786440 | tf_op jit(solution)/shard_map/ppermute | solution.py:65
  37.0 13.4 %collective-permute-start.4 = (bf16[128,1024]{1,0:T(8,128)(2,1)S(1)}, bf16[128,1024]{1,0:T(8,128)(2,1)S(1)}, u32[]{:S(2)}, u32[]{:S(2)}) collective-permute-start(bf16[128,1024]{1,0:T(8,128)(2,1)S(1)} %get-tuple-element.83.c0_ref), channel_id=1, source_target_pairs={{0,3},{1,0},{2,1},{3,2},{4,7},{5,4},{6,5},{7,6},{8,11},{9,8},{10,9... | collective-permute-start | bytes 786440 | tf_op jit(solution)/shard_map/ppermute | solution.py:69
  39.2 14.7 %collective-permute-start.5 = (bf16[128,1024]{1,0:T(8,128)(2,1)S(1)}, bf16[128,1024]{1,0:T(8,128)(2,1)S(1)}, u32[]{:S(2)}, u32[]{:S(2)}) collective-permute-start(bf16[128,1024]{1,0:T(8,128)(2,1)S(1)} %get-tuple-element.83.c0_ref), channel_id=1, source_target_pairs={{0,1},{1,2},{2,3},{3,0},{4,5},{5,6},{6,7},{7,4},{8,9},{9,10},{10,1... | collective-permute-start | bytes 786440 | tf_op jit(solution)/shard_map/ppermute | solution.py:69
  39.2 20.5 %collective-permute-start.6 = (bf16[128,1024]{1,0:T(8,128)(2,1)S(1)}, bf16[128,1024]{1,0:T(8,128)(2,1)S(1)}, u32[]{:S(2)}, u32[]{:S(2)}) collective-permute-start(bf16[128,1024]{1,0:T(8,128)(2,1)S(1)} %get-tuple-element.83.c0_ref), channel_id=1, source_target_pairs={{0,2},{1,3},{2,0},{3,1},{4,6},{5,7},{6,4},{7,5},{8,10},{9,11},{10,... | collective-permute-start | bytes 786440 | tf_op jit(solution)/shard_map/ppermute | solution.py:69
  66.7 13.8 %collective-permute-start.7 = (bf16[128,1024]{1,0:T(8,128)(2,1)S(1)}, bf16[128,1024]{1,0:T(8,128)(2,1)S(1)}, u32[]{:S(2)}, u32[]{:S(2)}) collective-permute-start(bf16[128,1024]{1,0:T(8,128)(2,1)S(1)} %get-tuple-element.165), channel_id=1, source_target_pairs={{0,1},{1,2},{2,3},{3,0},{4,5},{5,6},{6,7},{7,4},{8,9},{9,10},{10,1... | collective-permute-start | bytes 786440 | tf_op jit(solution)/shard_map/ppermute | solution.py:439
  66.7 25.7 %collective-permute-start.9 = (bf16[128,1024]{1,0:T(8,128)(2,1)S(1)}, bf16[128,1024]{1,0:T(8,128)(2,1)S(1)}, u32[]{:S(2)}, u32[]{:S(2)}) collective-permute-start(bf16[128,1024]{1,0:T(8,128)(2,1)S(1)} %convolution_convert_fusion), channel_id=1, source_target_pairs={{0,2},{1,3},{2,0},{3,1},{4,6},{5,7},{6,4},{7,5},{8,10},{9,11},{10,... | collective-permute-start | bytes 786440 | tf_op jit(solution)/shard_map/ppermute | solution.py:445
  74.0 18.4 %collective-permute-start.8 = (bf16[128,1024]{1,0:T(8,128)(2,1)S(1)}, bf16[128,1024]{1,0:T(8,128)(2,1)S(1)}, u32[]{:S(2)}, u32[]{:S(2)}) collective-permute-start(bf16[128,1024]{1,0:T(8,128)(2,1)S(1)} %get-tuple-element.164), channel_id=1, source_target_pairs={{0,3},{1,0},{2,1},{3,2},{4,7},{5,4},{6,5},{7,6},{8,11},{9,8},{10,9... | collective-permute-start | bytes 786440 | tf_op jit(solution)/shard_map/ppermute | solution.py:440
  81.2 11.3 %collective-permute-start.10 = (f32[8,256]{1,0:T(8,128)S(1)}, f32[8,256]{1,0:T(8,128)S(1)}, u32[]{:S(2)}, u32[]{:S(2)}) collective-permute-start(f32[8,256]{1,0:T(8,128)S(1)} %constant_dynamic-slice_fusion), channel_id=1, source_target_pairs={{4,0},{8,4},{12,8},{16,12},{20,16},{24,20},{28,24},{32,28},{36,32}... | collective-permute-start | bytes 24584 | tf_op jit(solution)/shard_map/ppermute | solution.py:44
  92.5 64.8 %reduce-scatter.3.cloned.1.call-start = ((), (), s32[]{:S(2)}) async-start(), calls=%async_computation.2 | async-start | bytes 7962624 | tf_op jit(solution)/shard_map/reduce_scatter | solution.py:85
  93.2 81.3 %reduce-scatter.5.cloned.1.call-start = ((), (), s32[]{:S(2)}) async-start(), calls=%async_computation.4 | async-start | bytes 2654208 | tf_op jit(solution)/shard_map/reduce_scatter | solution.py:85
  96.7 5.3 %collective-permute-start.14 = (bf16[16,1024]{1,0:T(8,128)(2,1)S(1)}, bf16[16,1024]{1,0:T(8,128)(2,1)S(1)}, u32[]{:S(2)}, u32[]{:S(2)}) collective-permute-start(bf16[16,1024]{1,0:T(8,128)(2,1)S(1)} %slice.57), channel_id=1, source_target_pairs={{4,0},{8,4},{12,8},{16,12},{20,16},{24,20},{28,24},{32,28},{36,32}... | collective-permute-start | bytes 98312 | tf_op jit(solution)/shard_map/ppermute | solution.py:52
  99.9 14.7 %collective-permute-start.11 = (bf16[128,1024]{1,0:T(8,128)(2,1)}, bf16[128,1024]{1,0:T(8,128)(2,1)S(1)}, u32[]{:S(2)}, u32[]{:S(2)}) collective-permute-start(bf16[128,1024]{1,0:T(8,128)(2,1)} %get-tuple-element.105.g0_ref), channel_id=1, source_target_pairs={{0,3},{1,0},{2,1},{3,2},{4,7},{5,4},{6,5},{7,6},{8,11},{9,8},{10,9... | collective-permute-start | bytes 786440 | tf_op jit(solution)/shard_map/ppermute | solution.py:69
  100.0 15.4 %collective-permute-start.12 = (bf16[128,1024]{1,0:T(8,128)(2,1)}, bf16[128,1024]{1,0:T(8,128)(2,1)S(1)}, u32[]{:S(2)}, u32[]{:S(2)}) collective-permute-start(bf16[128,1024]{1,0:T(8,128)(2,1)} %get-tuple-element.105.g0_ref), channel_id=1, source_target_pairs={{0,2},{1,3},{2,0},{3,1},{4,6},{5,7},{6,4},{7,5},{8,10},{9,11},{10,... | collective-permute-start | bytes 786440 | tf_op jit(solution)/shard_map/ppermute | solution.py:69
  100.1 22.2 %collective-permute-start.13 = (bf16[128,1024]{1,0:T(8,128)(2,1)}, bf16[128,1024]{1,0:T(8,128)(2,1)S(1)}, u32[]{:S(2)}, u32[]{:S(2)}) collective-permute-start(bf16[128,1024]{1,0:T(8,128)(2,1)} %get-tuple-element.105.g0_ref), channel_id=1, source_target_pairs={{0,1},{1,2},{2,3},{3,0},{4,5},{5,6},{6,7},{7,4},{8,9},{9,10},{10,1... | collective-permute-start | bytes 786440 | tf_op jit(solution)/shard_map/ppermute | solution.py:69
  133.2 15.5 %collective-permute-start.18 = (bf16[128,1024]{1,0:T(8,128)(2,1)S(1)}, bf16[128,1024]{1,0:T(8,128)(2,1)S(1)}, u32[]{:S(2)}, u32[]{:S(2)}) collective-permute-start(bf16[128,1024]{1,0:T(8,128)(2,1)S(1)} %copy-done.19), channel_id=1, source_target_pairs={{0,1},{1,2},{2,3},{3,0},{4,5},{5,6},{6,7},{7,4},{8,9},{9,10},{10,1... | collective-permute-start | bytes 786440 | tf_op jit(solution)/shard_map/ppermute | solution.py:65
  133.9 22.8 %collective-permute-start.19 = (bf16[128,1024]{1,0:T(8,128)(2,1)S(1)}, bf16[128,1024]{1,0:T(8,128)(2,1)S(1)}, u32[]{:S(2)}, u32[]{:S(2)}) collective-permute-start(bf16[128,1024]{1,0:T(8,128)(2,1)S(1)} %copy-done.18), channel_id=1, source_target_pairs={{0,2},{1,3},{2,0},{3,1},{4,6},{5,7},{6,4},{7,5},{8,10},{9,11},{10,... | collective-permute-start | bytes 786440 | tf_op jit(solution)/shard_map/ppermute | solution.py:65
  137.0 19.7 %collective-permute-start.20 = (bf16[128,1024]{1,0:T(8,128)(2,1)S(1)}, bf16[128,1024]{1,0:T(8,128)(2,1)S(1)}, u32[]{:S(2)}, u32[]{:S(2)}) collective-permute-start(bf16[128,1024]{1,0:T(8,128)(2,1)S(1)} %copy-done.17), channel_id=1, source_target_pairs={{0,3},{1,0},{2,1},{3,2},{4,7},{5,4},{6,5},{7,6},{8,11},{9,8},{10,9... | collective-permute-start | bytes 786440 | tf_op jit(solution)/shard_map/ppermute | solution.py:65
  160.1 9.4 %collective-permute-start.21 = (bf16[128,1024]{1,0:T(8,128)(2,1)}, bf16[128,1024]{1,0:T(8,128)(2,1)S(1)}, u32[]{:S(2)}, u32[]{:S(2)}) collective-permute-start(bf16[128,1024]{1,0:T(8,128)(2,1)} %shard_map.176.c0_ref), channel_id=1, source_target_pairs={{0,3},{1,0},{2,1},{3,2},{4,7},{5,4},{6,5},{7,6},{8,11},{9,8},{10,9... | collective-permute-start | bytes 786440 | tf_op jit(solution)/shard_map/ppermute | solution.py:69
  160.7 13.9 %collective-permute-start.22 = (bf16[128,1024]{1,0:T(8,128)(2,1)}, bf16[128,1024]{1,0:T(8,128)(2,1)S(1)}, u32[]{:S(2)}, u32[]{:S(2)}) collective-permute-start(bf16[128,1024]{1,0:T(8,128)(2,1)} %shard_map.176.c0_ref), channel_id=1, source_target_pairs={{0,2},{1,3},{2,0},{3,1},{4,6},{5,7},{6,4},{7,5},{8,10},{9,11},{10,... | collective-permute-start | bytes 786440 | tf_op jit(solution)/shard_map/ppermute | solution.py:69
  162.0 13.6 %collective-permute-start.23 = (bf16[128,1024]{1,0:T(8,128)(2,1)}, bf16[128,1024]{1,0:T(8,128)(2,1)S(1)}, u32[]{:S(2)}, u32[]{:S(2)}) collective-permute-start(bf16[128,1024]{1,0:T(8,128)(2,1)} %shard_map.176.c0_ref), channel_id=1, source_target_pairs={{0,1},{1,2},{2,3},{3,0},{4,5},{5,6},{6,7},{7,4},{8,9},{9,10},{10,1... | collective-permute-start | bytes 786440 | tf_op jit(solution)/shard_map/ppermute | solution.py:69
  164.8 10.7 %collective-permute-start.24 = (bf16[32,3456]{1,0:T(8,128)(2,1)}, bf16[32,3456]{1,0:T(8,128)(2,1)S(1)}, u32[]{:S(2)}, u32[]{:S(2)}) collective-permute-start(bf16[32,3456]{1,0:T(8,128)(2,1)} %get-tuple-element.162), channel_id=1, source_target_pairs={{0,32},{4,36},{8,40},{12,44},{16,48},{20,52},{24,56},{28,60},{32,6... | collective-permute-start | bytes 663560 | tf_op jit(solution)/shard_map/ppermute | solution.py:536
  166.4 11.9 %collective-permute-start.25 = (bf16[32,3456]{1,0:T(8,128)(2,1)}, bf16[32,3456]{1,0:T(8,128)(2,1)S(1)}, u32[]{:S(2)}, u32[]{:S(2)}) collective-permute-start(bf16[32,3456]{1,0:T(8,128)(2,1)} %get-tuple-element.161), channel_id=1, source_target_pairs={{0,64},{4,68},{8,72},{12,76},{16,80},{20,84},{24,88},{28,92},{32,9... | collective-permute-start | bytes 663560 | tf_op jit(solution)/shard_map/ppermute | solution.py:536
  169.5 8.8 %collective-permute-start.26 = (bf16[32,3456]{1,0:T(8,128)(2,1)}, bf16[32,3456]{1,0:T(8,128)(2,1)}, u32[]{:S(2)}, u32[]{:S(2)}) collective-permute-start(bf16[32,3456]{1,0:T(8,128)(2,1)} %get-tuple-element.160), channel_id=1, source_target_pairs={{0,96},{4,100},{8,104},{12,108},{16,112},{20,116},{24,120},{28,124... | collective-permute-start | bytes 663560 | tf_op jit(solution)/shard_map/ppermute | solution.py:536
  179.3 6.4 %collective-permute-start.27 = (bf16[32,1152]{1,0:T(8,128)(2,1)S(1)}, bf16[32,1152]{1,0:T(8,128)(2,1)S(1)}, u32[]{:S(2)}, u32[]{:S(2)}) collective-permute-start(bf16[32,1152]{1,0:T(8,128)(2,1)S(1)} %get-tuple-element.169), channel_id=1, source_target_pairs={{0,32},{4,36},{8,40},{12,44},{16,48},{20,52},{24,56},{28,60},{32,6... | collective-permute-start | bytes 221192 | tf_op jit(solution)/shard_map/ppermute | solution.py:536
  181.4 5.9 %collective-permute-start.28 = (bf16[32,1152]{1,0:T(8,128)(2,1)S(1)}, bf16[32,1152]{1,0:T(8,128)(2,1)S(1)}, u32[]{:S(2)}, u32[]{:S(2)}) collective-permute-start(bf16[32,1152]{1,0:T(8,128)(2,1)S(1)} %get-tuple-element.168), channel_id=1, source_target_pairs={{0,64},{4,68},{8,72},{12,76},{16,80},{20,84},{24,88},{28,92},{32,9... | collective-permute-start | bytes 221192 | tf_op jit(solution)/shard_map/ppermute | solution.py:536
  189.6 11.9 %collective-permute-start.30 = (f32[16,128]{1,0:T(8,128)S(1)}, f32[16,128]{1,0:T(8,128)S(1)}, u32[]{:S(2)}, u32[]{:S(2)}) collective-permute-start(f32[16,128]{1,0:T(8,128)S(1)} %slice.58), channel_id=1, source_target_pairs={{0,2},{1,3},{2,0},{3,1},{4,6},{5,7},{6,4},{7,5},{8,10},{9,11},{10,... | collective-permute-start | bytes 24584 | tf_op jit(solution)/shard_map/ppermute | solution.py:556
  193.0 8.5 %collective-permute-start.31 = (f32[16,128]{1,0:T(8,128)S(1)}, f32[16,128]{1,0:T(8,128)S(1)}, u32[]{:S(2)}, u32[]{:S(2)}) collective-permute-start(f32[16,128]{1,0:T(8,128)S(1)} %slice.58), channel_id=1, source_target_pairs={{0,1},{1,2},{2,3},{3,0},{4,5},{5,6},{6,7},{7,4},{8,9},{9,10},{10,1... | collective-permute-start | bytes 24584 | tf_op jit(solution)/shard_map/ppermute | solution.py:556
  193.0 8.5 %collective-permute-start.32 = (f32[16,128]{1,0:T(8,128)S(1)}, f32[16,128]{1,0:T(8,128)S(1)}, u32[]{:S(2)}, u32[]{:S(2)}) collective-permute-start(f32[16,128]{1,0:T(8,128)S(1)} %slice.58), channel_id=1, source_target_pairs={{0,3},{1,0},{2,1},{3,2},{4,7},{5,4},{6,5},{7,6},{8,11},{9,8},{10,9... | collective-permute-start | bytes 24584 | tf_op jit(solution)/shard_map/ppermute | solution.py:556
  (29 other events, 175.2 us)
Sparse Core Ops, SparseCore 0:
  92.6 64.6 all-reduce.1
Sparse Core Ops, SparseCore 1:
  95.5 44.0 reduce-scatter.2
  142.0 32.5 reduce-scatter.4

commit v4 on v3

--- a/solution.py
+++ b/solution.py
@@ -537,8 +537,23 @@
             for o in (1, 2, 3)
         ]
 
+    chunk = pl.BlockSpec((mine, width), lambda i, s, t: ((s[0] + i) % MP, 0))
+    hidden_grad = call(
+        place_kernel,
+        place,
+        [(v, None) for v in (hidden_low, ends[1], ends[2], ends[3])],
+        [((rows, width), FULL, chunk)],
+        grid=MP,
+    )[0]
+    hidden_out = call(
+        place_add_kernel,
+        place,
+        [(mids[o], None) for o in range(MP)] + [(ffn_out, chunk)],
+        [((rows, width), FULL, chunk)],
+        grid=MP,
+    )[0]
     ffn_parts = along_z(after(ffn_line, hidden_low))
-    in_out_line, ffn_parts = lax.optimization_barrier((after(in_out_line, ends), ffn_parts))
+    in_out_line, ffn_parts = lax.optimization_barrier((after(in_out_line, hidden_grad, hidden_out), ffn_parts))
     lines = [*ffn_parts, *along_z(in_out_line)]
     in_done, out_done, gate_up_done, down_done, small = call(
         finish_kernel,
@@ -556,21 +571,6 @@
     gains = gains + sum(lax.ppermute(gains, "mp", ring_shift(MP, o)) for o in (2, 1, 3))
     gains = gains.reshape(2, width)
     taps_grad = small[2 * width // LANES : (2 * width + 3 * channels) // LANES]
-    chunk = pl.BlockSpec((mine, width), lambda i, s, t: ((s[0] + i) % MP, 0))
-    hidden_grad = call(
-        place_kernel,
-        place,
-        [(v, None) for v in (hidden_low, ends[1], ends[2], ends[3])],
-        [((rows, width), FULL, chunk)],
-        grid=MP,
-    )[0]
-    hidden_out = call(
-        place_add_kernel,
-        place,
-        [(mids[o], None) for o in range(MP)] + [(ffn_out, chunk)],
-        [((rows, width), FULL, chunk)],
-        grid=MP,
-    )[0]
     return (
         hidden_out,
         hidden_grad,

time: 211 us -> 205 us (0.972)
  waiting for transfers between devices: 67.7 us -> 64.1 us
    unnamed x50 -> x48, local copies, waits for them, and re-layouts: 7.65 us -> 7.77 us
  transfers between devices with their start and end apart: 36 -> 36, of which waited for: 21 -> 21; matrix products, arithmetic and copies ran while one was open for 8% -> 9% of each run, Pallas kernels for 15% -> 16%
where the time goes in v4:
time: 205 us
  waiting for transfers between devices  64.1 us (31%)
  starting transfers between devices  54.9 us (27%)
  Pallas kernels  38.6 us (19%)
  between operations  16.5 us (8%)
  local copies, waits for them, and re-layouts  15.2 us (7%)
  matrix products  8.04 us (4%)
  other arithmetic  7.25 us (4%)
    pallas_call x10, Pallas kernels, call(): pl.pallas_call(kernel, grid_spec=pltpu.PrefetchScalarGridSpec(num_scalar_...  38.6 us
    ppermute x9, waiting for transfers between devices, gather_rows(): return {o: lax.ppermute(rows, 'mp', ring_shift(MP, -o)) for o in order}  25.7 us
    ppermute x6, waiting for transfers between devices, send_rows(): lax.ppermute(parts[o], 'mp', ring_shift(MP, o))  23.8 us
    ppermute x6, starting transfers between devices, along_z(): lax.ppermute(take(line, (z + o) % Z_DIM, 0), 'seq', seq_shift(o, 0, 0))  12.5 us
    ppermute x6, starting transfers between devices, send_rows(): lax.ppermute(parts[o], 'mp', ring_shift(MP, o))  12.1 us
    ppermute x9, starting transfers between devices, gather_rows(): return {o: lax.ppermute(rows, 'mp', ring_shift(MP, -o)) for o in order}  10.8 us
    dot_general x5, matrix products, dot(): lax.dot_general(left, right, (contract, ((), ())), preferred_element_type...  8.04 us
    unnamed x48, local copies, waits for them, and re-layouts  7.77 us
  transfers between devices with their start and end apart: 36, of which 21 were waited for; matrix products, arithmetic and copies ran while one was open for 9% of the time, Pallas kernels for 16%

profile of v4, /device:TPU:2, one launch (start us, length us, event | category | flops | bytes accessed | tf_op | source)
XLA Modules:
  0.0 204.6 jit_solution(16969268693476663165)
XLA Ops:
  11.4 2.7 %collective-permute-done.tail_ref = f32[8,1024]{1,0:T(8,128)S(1)} collective-permute-done((f32[8,1024]{1,0:T(8,128)S(1)}, f32[8,1024]{1,0:T(8,128)S(1)}, u32[]{:S(2)}, u32[]{:S(2)}) %collective-permute-start) | collective-permute-done | bytes 32800 | tf_op jit(solution)/shard_map/ppermute | solution.py:44
  14.7 5.6 %shard_map.169 = (bf16[512,1024]{1,0:T(8,128)(2,1)}, f32[512,256]{1,0:T(8,128)}, f32[512,256]{1,0:T(8,128)}, f32[512,256]{1,0:T(8,128)}, bf16[512,256]{1,0:T(8,1...) custom-call(s32[1]{0:T(128)} %bitcast.s_ref, ...), custom_call_target="tpu_custom_call" | custom-call | tf_op jit(solution)/shard_map/pallas_call | solution.py:125
  21.8 2.9 %collective-permute-start.2 = (bf16[128,1024]{1,0:T(8,128)(2,1)}, bf16[128,1024]{1,0:T(8,128)(2,1)S(1)}, u32[]{:S(2)}, u32[]{:S(2)}) collective-permute-start(bf16[128,1024]{1,0:T(8,128)(2,1)} %get-tuple-element.77), channel_id=1, source_target_pairs={{0,2},{1,3},{2,0},{3,1},{4,6},{5,7},{6,4},{7,5},{8,10},{9,11},{10,... | collective-permute-start | bytes 786440 | tf_op jit(solution)/shard_map/ppermute | solution.py:65
  26.0 3.7 %collective-permute-done.1.r1_ref = bf16[128,1024]{1,0:T(8,128)(2,1)S(1)} collective-permute-done((bf16[128,1024]{1,0:T(8,128)(2,1)}, bf16[128,1024]{1,0:T(8,128)(2,1)S(1)}, u32[]{:S(2)}, u32[]{:S(2)}) %collective-permute-start.1) | collective-permute-done | bytes 262176 | tf_op jit(solution)/shard_map/ppermute | solution.py:65
  29.8 3.3 %copy.20 = bf16[128,8,2,1152]{3,1,2,0:T(8,128)(2,1)S(1)} copy(bf16[128,8,2,1152]{3,2,1,0:T(2,128)(2,1)} %bitcast.44) | data formatting | bytes 9437184
  33.1 2.9 %collective-permute-done.2.r2_ref = bf16[128,1024]{1,0:T(8,128)(2,1)S(1)} collective-permute-done((bf16[128,1024]{1,0:T(8,128)(2,1)}, bf16[128,1024]{1,0:T(8,128)(2,1)S(1)}, u32[]{:S(2)}, u32[]{:S(2)}) %collective-permute-start.2) | collective-permute-done | bytes 262176 | tf_op jit(solution)/shard_map/ppermute | solution.py:65
  37.0 2.1 %collective-permute-start.4 = (bf16[128,1024]{1,0:T(8,128)(2,1)S(1)}, bf16[128,1024]{1,0:T(8,128)(2,1)S(1)}, u32[]{:S(2)}, u32[]{:S(2)}) collective-permute-start(bf16[128,1024]{1,0:T(8,128)(2,1)S(1)} %get-tuple-element.83.c0_ref), channel_id=1, source_target_pairs={{0,3},{1,0},{2,1},{3,2},{4,7},{5,4},{6,5},{7,6},{8,11},{9,8},{10,9... | collective-permute-start | bytes 786440 | tf_op jit(solution)/shard_map/ppermute | solution.py:69
  39.2 4.0 %collective-permute-start.6 = (bf16[128,1024]{1,0:T(8,128)(2,1)S(1)}, bf16[128,1024]{1,0:T(8,128)(2,1)S(1)}, u32[]{:S(2)}, u32[]{:S(2)}) collective-permute-start(bf16[128,1024]{1,0:T(8,128)(2,1)S(1)} %get-tuple-element.83.c0_ref), channel_id=1, source_target_pairs={{0,2},{1,3},{2,0},{3,1},{4,6},{5,7},{6,4},{7,5},{8,10},{9,11},{10,... | collective-permute-start | bytes 786440 | tf_op jit(solution)/shard_map/ppermute | solution.py:69
  44.9 5.5 %collective-permute-done.4.c1_ref = bf16[128,1024]{1,0:T(8,128)(2,1)S(1)} collective-permute-done((bf16[128,1024]{1,0:T(8,128)(2,1)S(1)}, bf16[128,1024]{1,0:T(8,128)(2,1)S(1)}, u32[]{:S(2)}, u32[]{:S(2)}) %collective-permute-start.4) | collective-permute-done | bytes 262176 | tf_op jit(solution)/shard_map/ppermute | solution.py:69
  50.4 3.4 %collective-permute-done.5.c3_ref = bf16[128,1024]{1,0:T(8,128)(2,1)S(1)} collective-permute-done((bf16[128,1024]{1,0:T(8,128)(2,1)S(1)}, bf16[128,1024]{1,0:T(8,128)(2,1)S(1)}, u32[]{:S(2)}, u32[]{:S(2)}) %collective-permute-start.5) | collective-permute-done | bytes 262176 | tf_op jit(solution)/shard_map/ppermute | solution.py:69
  54.3 2.0 fusion.20
  57.6 2.0 fusion.7
  69.5 4.5 %shard_map.171 = bf16[512,1024]{1,0:T(8,128)(2,1)} custom-call(s32[1]{0:T(128)} %bitcast.s_ref, s32[1]{0:T(128)S(6)} %copy.22.t_ref, bf16[512,1152]{1,0:T(8,128)(2,1)} %pad_maximum_fusion.active_ref, bf16[1152,1024]{1,0:T(8,128)(2,1)} %down_ref.1), custom_call_target="tpu_custom_call" | custom-call | tf_op jit(solution)/shard_map/pallas_call | solution.py:125
  75.5 4.9 %collective-permute-done.7.r1_ref = bf16[128,1024]{1,0:T(8,128)(2,1)S(1)} collective-permute-done((bf16[128,1024]{1,0:T(8,128)(2,1)S(1)}, bf16[128,1024]{1,0:T(8,128)(2,1)S(1)}, u32[]{:S(2)}, u32[]{:S(2)}) %collective-permute-start.7) | collective-permute-done | bytes 262176 | tf_op jit(solution)/shard_map/ppermute | solution.py:439
  81.2 2.1 %collective-permute-start.10 = (f32[8,256]{1,0:T(8,128)S(1)}, f32[8,256]{1,0:T(8,128)S(1)}, u32[]{:S(2)}, u32[]{:S(2)}) collective-permute-start(f32[8,256]{1,0:T(8,128)S(1)} %constant_dynamic-slice_fusion), channel_id=1, source_target_pairs={{4,0},{8,4},{12,8},{16,12},{20,16},{24,20},{28,24},{32,28},{36,32}... | collective-permute-start | bytes 24584 | tf_op jit(solution)/shard_map/ppermute | solution.py:44
  83.3 9.2 %shard_map.172 = bf16[1024,3456]{1,0:T(8,128)(2,1)} custom-call(s32[1]{0:T(128)} %bitcast.s_ref, s32[1]{0:T(128)S(6)} %copy.22.t_ref, bf16[512,1024]{1,0:T(8,128)(2,1)} %get-tuple-element.97.normed_ref, bf16[512,2304]{1,0:T(8,128)(2,1)} %maximum_maximum_fusion.grad_gu_ref, bf16[512,1024]{1,0:T(8,128)(2,1)} %get-tuple-element.99.low_ref, ...), custom_call_target="tpu_custom_call" | custom-call | flops 10000000000 | tf_op jit(solution)/shard_map/pallas_call | solution.py:125
  93.3 2.8 %shard_map.173 = (f32[128,1024]{1,0:T(8,128)}, bf16[128,1024]{1,0:T(8,128)(2,1)}, f32[1,1024]{1,0:T(1,128)}) custom-call(s32[1]{0:T(128)} %bitcast.s_ref, s32[1]{0:T(128)S(6)} %copy.22.t_ref, bf16[128,1024]{1,0:T(8,128)(2,1)} %get-tuple-element.166.p0_ref, bf16[128,1024]{1,0:T(8,128)(2,1)} %copy-done.8, bf16[128,1024]{1,0:T(8,128)(2,1)} %copy-done.10, ...), custom_call_target="tpu_custom_call" | custom-call | tf_op jit(solution)/shard_map/pallas_call | solution.py:125
  100.2 1.9 collective-permute-start.13
  107.1 7.6 %collective-permute-done.11.g1_ref = bf16[128,1024]{1,0:T(8,128)(2,1)S(1)} collective-permute-done((bf16[128,1024]{1,0:T(8,128)(2,1)}, bf16[128,1024]{1,0:T(8,128)(2,1)S(1)}, u32[]{:S(2)}, u32[]{:S(2)}) %collective-permute-start.11) | collective-permute-done | bytes 262176 | tf_op jit(solution)/shard_map/ppermute | solution.py:69
  115.5 6.9 %collective-permute-done.13.g3_ref = bf16[128,1024]{1,0:T(8,128)(2,1)S(1)} collective-permute-done((bf16[128,1024]{1,0:T(8,128)(2,1)}, bf16[128,1024]{1,0:T(8,128)(2,1)S(1)}, u32[]{:S(2)}, u32[]{:S(2)}) %collective-permute-start.13) | collective-permute-done | bytes 262176 | tf_op jit(solution)/shard_map/ppermute | solution.py:69
  123.1 9.2 %shard_map.174 = (bf16[1024,1152]{1,0:T(8,128)(2,1)}, f32[128,1024]{1,0:T(8,128)}, bf16[128,1024]{1,0:T(8,128)(2,1)}, bf16[128,1024]{1,0:T(8,128)(2,1)}, bf16[128,1024]{1,0:T(8,128)(2,1)}) custom-call(s32[1]{0:T(128)} %bitcast.s_ref, s32[1]{0:T(128)S(6)} %copy.22.t_ref, bf16[128,1024]{1,0:T(8,128)(2,1)} %get-tuple-element.105.g0_ref, ...), custom_call_target="tpu_custom_call" | custom-call | flops 10000000000 | tf_op jit(solution)/shard_map/pallas_call | solution.py:125
  133.9 3.1 %collective-permute-start.19 = (bf16[128,1024]{1,0:T(8,128)(2,1)S(1)}, bf16[128,1024]{1,0:T(8,128)(2,1)S(1)}, u32[]{:S(2)}, u32[]{:S(2)}) collective-permute-start(bf16[128,1024]{1,0:T(8,128)(2,1)S(1)} %copy-done.17), channel_id=1, source_target_pairs={{0,2},{1,3},{2,0},{3,1},{4,6},{5,7},{6,4},{7,5},{8,10},{9,11},{10,... | collective-permute-start | bytes 786440 | tf_op jit(solution)/shard_map/ppermute | solution.py:65
  137.0 2.5 %collective-permute-start.20 = (bf16[128,1024]{1,0:T(8,128)(2,1)S(1)}, bf16[128,1024]{1,0:T(8,128)(2,1)S(1)}, u32[]{:S(2)}, u32[]{:S(2)}) collective-permute-start(bf16[128,1024]{1,0:T(8,128)(2,1)S(1)} %copy-done.16), channel_id=1, source_target_pairs={{0,3},{1,0},{2,1},{3,2},{4,7},{5,4},{6,5},{7,6},{8,11},{9,8},{10,9... | collective-permute-start | bytes 786440 | tf_op jit(solution)/shard_map/ppermute | solution.py:65
  139.5 9.3 %collective-permute-done.18.r1_ref = bf16[128,1024]{1,0:T(8,128)(2,1)S(1)} collective-permute-done((bf16[128,1024]{1,0:T(8,128)(2,1)S(1)}, bf16[128,1024]{1,0:T(8,128)(2,1)S(1)}, u32[]{:S(2)}, u32[]{:S(2)}) %collective-permute-start.18) | collective-permute-done | bytes 262176 | tf_op jit(solution)/shard_map/ppermute | solution.py:65
  148.8 7.9 %collective-permute-done.19.r2_ref = bf16[128,1024]{1,0:T(8,128)(2,1)S(1)} collective-permute-done((bf16[128,1024]{1,0:T(8,128)(2,1)S(1)}, bf16[128,1024]{1,0:T(8,128)(2,1)S(1)}, u32[]{:S(2)}, u32[]{:S(2)}) %collective-permute-start.19) | collective-permute-done | bytes 262176 | tf_op jit(solution)/shard_map/ppermute | solution.py:65
  157.5 2.7 %shard_map.176.c0_ref = bf16[128,1024]{1,0:T(8,128)(2,1)} custom-call(s32[1]{0:T(128)} %bitcast.s_ref, s32[1]{0:T(128)S(6)} %copy.22.t_ref, f32[128,1024]{1,0:T(8,128)} %get-tuple-element.122.p0_ref, bf16[128,1024]{1,0:T(8,128)(2,1)} %copy-done.11, bf16[128,1024]{1,0:T(8,128)(2,1)} %copy-done.12, bf16[128,1024]{1,0:T(8,128)(2,1)} %copy-done.13, ...), custom_call_target="tpu_custom_call" | custom-call | tf_op jit(solution)/shard_map/pallas_call | solution.py:125
  162.9 2.0 dynamic-slice_bitcast_fusion
  166.5 2.9 %collective-permute-start.25 = (bf16[32,3456]{1,0:T(8,128)(2,1)S(1)}, bf16[32,3456]{1,0:T(8,128)(2,1)S(1)}, u32[]{:S(2)}, u32[]{:S(2)}) collective-permute-start(bf16[32,3456]{1,0:T(8,128)(2,1)S(1)} %get-tuple-element.161), channel_id=1, source_target_pairs={{0,64},{4,68},{8,72},{12,76},{16,80},{20,84},{24,88},{28,92},{32,9... | collective-permute-start | bytes 663560 | tf_op jit(solution)/shard_map/ppermute | solution.py:536
  169.7 3.0 %collective-permute-start.26 = (bf16[32,3456]{1,0:T(8,128)(2,1)S(1)}, bf16[32,3456]{1,0:T(8,128)(2,1)S(1)}, u32[]{:S(2)}, u32[]{:S(2)}) collective-permute-start(bf16[32,3456]{1,0:T(8,128)(2,1)S(1)} %get-tuple-element.160), channel_id=1, source_target_pairs={{0,96},{4,100},{8,104},{12,108},{16,112},{20,116},{24,120},{28,124... | collective-permute-start | bytes 663560 | tf_op jit(solution)/shard_map/ppermute | solution.py:536
  181.1 2.3 %collective-permute-start.28 = (bf16[32,1152]{1,0:T(8,128)(2,1)S(1)}, bf16[32,1152]{1,0:T(8,128)(2,1)S(1)}, u32[]{:S(2)}, u32[]{:S(2)}) collective-permute-start(bf16[32,1152]{1,0:T(8,128)(2,1)S(1)} %get-tuple-element.168), channel_id=1, source_target_pairs={{0,64},{4,68},{8,72},{12,76},{16,80},{20,84},{24,88},{28,92},{32,9... | collective-permute-start | bytes 221192 | tf_op jit(solution)/shard_map/ppermute | solution.py:536
  188.5 3.1 %collective-permute-start.30 = (f32[16,128]{1,0:T(8,128)S(1)}, f32[16,128]{1,0:T(8,128)S(1)}, u32[]{:S(2)}, u32[]{:S(2)}) collective-permute-start(f32[16,128]{1,0:T(8,128)S(1)} %slice.58), channel_id=1, source_target_pairs={{0,2},{1,3},{2,0},{3,1},{4,6},{5,7},{6,4},{7,5},{8,10},{9,11},{10,... | collective-permute-start | bytes 24584 | tf_op jit(solution)/shard_map/ppermute | solution.py:571
  191.7 3.2 %collective-permute-start.32 = (f32[16,128]{1,0:T(8,128)S(1)}, f32[16,128]{1,0:T(8,128)S(1)}, u32[]{:S(2)}, u32[]{:S(2)}) collective-permute-start(f32[16,128]{1,0:T(8,128)S(1)} %slice.58), channel_id=1, source_target_pairs={{0,3},{1,0},{2,1},{3,2},{4,7},{5,4},{6,5},{7,6},{8,11},{9,8},{10,9... | collective-permute-start | bytes 24584 | tf_op jit(solution)/shard_map/ppermute | solution.py:571
  (132 shorter events, 56.8 us)
Async XLA Ops:
  8.0 149.3 %all-reduce.2.cloned.1.call-start = ((), (), s32[]{:S(2)}) async-start(), calls=%async_computation.3 | async-start | bytes 2097152 | tf_op jit(solution)/shard_map/psum | solution.py:459
  8.8 5.2 %collective-permute-start = (f32[8,1024]{1,0:T(8,128)S(1)}, f32[8,1024]{1,0:T(8,128)S(1)}, u32[]{:S(2)}, u32[]{:S(2)}) collective-permute-start(f32[8,1024]{1,0:T(8,128)S(1)} %slice.47), channel_id=1, source_target_pairs={{0,4},{4,8},{8,12},{12,16},{16,20},{20,24},{24,28},{28,32},{32,36}... | collective-permute-start | bytes 98312 | tf_op jit(solution)/shard_map/ppermute | solution.py:44
  20.2 9.5 %collective-permute-start.1 = (bf16[128,1024]{1,0:T(8,128)(2,1)}, bf16[128,1024]{1,0:T(8,128)(2,1)S(1)}, u32[]{:S(2)}, u32[]{:S(2)}) collective-permute-start(bf16[128,1024]{1,0:T(8,128)(2,1)} %get-tuple-element.76), channel_id=1, source_target_pairs={{0,1},{1,2},{2,3},{3,0},{4,5},{5,6},{6,7},{7,4},{8,9},{9,10},{10,1... | collective-permute-start | bytes 786440 | tf_op jit(solution)/shard_map/ppermute | solution.py:65
  21.8 14.2 %collective-permute-start.2 = (bf16[128,1024]{1,0:T(8,128)(2,1)}, bf16[128,1024]{1,0:T(8,128)(2,1)S(1)}, u32[]{:S(2)}, u32[]{:S(2)}) collective-permute-start(bf16[128,1024]{1,0:T(8,128)(2,1)} %get-tuple-element.77), channel_id=1, source_target_pairs={{0,2},{1,3},{2,0},{3,1},{4,6},{5,7},{6,4},{7,5},{8,10},{9,11},{10,... | collective-permute-start | bytes 786440 | tf_op jit(solution)/shard_map/ppermute | solution.py:65
  24.7 11.3 %collective-permute-start.3 = (bf16[128,1024]{1,0:T(8,128)(2,1)}, bf16[128,1024]{1,0:T(8,128)(2,1)S(1)}, u32[]{:S(2)}, u32[]{:S(2)}) collective-permute-start(bf16[128,1024]{1,0:T(8,128)(2,1)} %get-tuple-element.78), channel_id=1, source_target_pairs={{0,3},{1,0},{2,1},{3,2},{4,7},{5,4},{6,5},{7,6},{8,11},{9,8},{10,9... | collective-permute-start | bytes 786440 | tf_op jit(solution)/shard_map/ppermute | solution.py:65
  37.0 13.4 %collective-permute-start.4 = (bf16[128,1024]{1,0:T(8,128)(2,1)S(1)}, bf16[128,1024]{1,0:T(8,128)(2,1)S(1)}, u32[]{:S(2)}, u32[]{:S(2)}) collective-permute-start(bf16[128,1024]{1,0:T(8,128)(2,1)S(1)} %get-tuple-element.83.c0_ref), channel_id=1, source_target_pairs={{0,3},{1,0},{2,1},{3,2},{4,7},{5,4},{6,5},{7,6},{8,11},{9,8},{10,9... | collective-permute-start | bytes 786440 | tf_op jit(solution)/shard_map/ppermute | solution.py:69
  39.2 14.7 %collective-permute-start.5 = (bf16[128,1024]{1,0:T(8,128)(2,1)S(1)}, bf16[128,1024]{1,0:T(8,128)(2,1)S(1)}, u32[]{:S(2)}, u32[]{:S(2)}) collective-permute-start(bf16[128,1024]{1,0:T(8,128)(2,1)S(1)} %get-tuple-element.83.c0_ref), channel_id=1, source_target_pairs={{0,1},{1,2},{2,3},{3,0},{4,5},{5,6},{6,7},{7,4},{8,9},{9,10},{10,1... | collective-permute-start | bytes 786440 | tf_op jit(solution)/shard_map/ppermute | solution.py:69
  39.2 20.5 %collective-permute-start.6 = (bf16[128,1024]{1,0:T(8,128)(2,1)S(1)}, bf16[128,1024]{1,0:T(8,128)(2,1)S(1)}, u32[]{:S(2)}, u32[]{:S(2)}) collective-permute-start(bf16[128,1024]{1,0:T(8,128)(2,1)S(1)} %get-tuple-element.83.c0_ref), channel_id=1, source_target_pairs={{0,2},{1,3},{2,0},{3,1},{4,6},{5,7},{6,4},{7,5},{8,10},{9,11},{10,... | collective-permute-start | bytes 786440 | tf_op jit(solution)/shard_map/ppermute | solution.py:69
  66.7 13.8 %collective-permute-start.7 = (bf16[128,1024]{1,0:T(8,128)(2,1)S(1)}, bf16[128,1024]{1,0:T(8,128)(2,1)S(1)}, u32[]{:S(2)}, u32[]{:S(2)}) collective-permute-start(bf16[128,1024]{1,0:T(8,128)(2,1)S(1)} %get-tuple-element.165), channel_id=1, source_target_pairs={{0,1},{1,2},{2,3},{3,0},{4,5},{5,6},{6,7},{7,4},{8,9},{9,10},{10,1... | collective-permute-start | bytes 786440 | tf_op jit(solution)/shard_map/ppermute | solution.py:439
  66.7 25.8 %collective-permute-start.9 = (bf16[128,1024]{1,0:T(8,128)(2,1)S(1)}, bf16[128,1024]{1,0:T(8,128)(2,1)S(1)}, u32[]{:S(2)}, u32[]{:S(2)}) collective-permute-start(bf16[128,1024]{1,0:T(8,128)(2,1)S(1)} %convolution_convert_fusion), channel_id=1, source_target_pairs={{0,2},{1,3},{2,0},{3,1},{4,6},{5,7},{6,4},{7,5},{8,10},{9,11},{10,... | collective-permute-start | bytes 786440 | tf_op jit(solution)/shard_map/ppermute | solution.py:445
  74.0 18.4 %collective-permute-start.8 = (bf16[128,1024]{1,0:T(8,128)(2,1)S(1)}, bf16[128,1024]{1,0:T(8,128)(2,1)S(1)}, u32[]{:S(2)}, u32[]{:S(2)}) collective-permute-start(bf16[128,1024]{1,0:T(8,128)(2,1)S(1)} %get-tuple-element.164), channel_id=1, source_target_pairs={{0,3},{1,0},{2,1},{3,2},{4,7},{5,4},{6,5},{7,6},{8,11},{9,8},{10,9... | collective-permute-start | bytes 786440 | tf_op jit(solution)/shard_map/ppermute | solution.py:440
  81.2 11.3 %collective-permute-start.10 = (f32[8,256]{1,0:T(8,128)S(1)}, f32[8,256]{1,0:T(8,128)S(1)}, u32[]{:S(2)}, u32[]{:S(2)}) collective-permute-start(f32[8,256]{1,0:T(8,128)S(1)} %constant_dynamic-slice_fusion), channel_id=1, source_target_pairs={{4,0},{8,4},{12,8},{16,12},{20,16},{24,20},{28,24},{32,28},{36,32}... | collective-permute-start | bytes 24584 | tf_op jit(solution)/shard_map/ppermute | solution.py:44
  92.5 64.7 %reduce-scatter.3.cloned.1.call-start = ((), (), s32[]{:S(2)}) async-start(), calls=%async_computation.2 | async-start | bytes 7962624 | tf_op jit(solution)/shard_map/reduce_scatter | solution.py:85
  93.3 84.2 %reduce-scatter.5.cloned.1.call-start = ((), (), s32[]{:S(2)}) async-start(), calls=%async_computation.4 | async-start | bytes 2654208 | tf_op jit(solution)/shard_map/reduce_scatter | solution.py:85
  96.8 5.3 %collective-permute-start.14 = (bf16[16,1024]{1,0:T(8,128)(2,1)S(1)}, bf16[16,1024]{1,0:T(8,128)(2,1)S(1)}, u32[]{:S(2)}, u32[]{:S(2)}) collective-permute-start(bf16[16,1024]{1,0:T(8,128)(2,1)S(1)} %slice.57), channel_id=1, source_target_pairs={{4,0},{8,4},{12,8},{16,12},{20,16},{24,20},{28,24},{32,28},{36,32}... | collective-permute-start | bytes 98312 | tf_op jit(solution)/shard_map/ppermute | solution.py:52
  100.0 14.7 %collective-permute-start.11 = (bf16[128,1024]{1,0:T(8,128)(2,1)}, bf16[128,1024]{1,0:T(8,128)(2,1)S(1)}, u32[]{:S(2)}, u32[]{:S(2)}) collective-permute-start(bf16[128,1024]{1,0:T(8,128)(2,1)} %get-tuple-element.105.g0_ref), channel_id=1, source_target_pairs={{0,3},{1,0},{2,1},{3,2},{4,7},{5,4},{6,5},{7,6},{8,11},{9,8},{10,9... | collective-permute-start | bytes 786440 | tf_op jit(solution)/shard_map/ppermute | solution.py:69
  100.1 15.4 %collective-permute-start.12 = (bf16[128,1024]{1,0:T(8,128)(2,1)}, bf16[128,1024]{1,0:T(8,128)(2,1)S(1)}, u32[]{:S(2)}, u32[]{:S(2)}) collective-permute-start(bf16[128,1024]{1,0:T(8,128)(2,1)} %get-tuple-element.105.g0_ref), channel_id=1, source_target_pairs={{0,2},{1,3},{2,0},{3,1},{4,6},{5,7},{6,4},{7,5},{8,10},{9,11},{10,... | collective-permute-start | bytes 786440 | tf_op jit(solution)/shard_map/ppermute | solution.py:69
  100.2 22.2 %collective-permute-start.13 = (bf16[128,1024]{1,0:T(8,128)(2,1)}, bf16[128,1024]{1,0:T(8,128)(2,1)S(1)}, u32[]{:S(2)}, u32[]{:S(2)}) collective-permute-start(bf16[128,1024]{1,0:T(8,128)(2,1)} %get-tuple-element.105.g0_ref), channel_id=1, source_target_pairs={{0,1},{1,2},{2,3},{3,0},{4,5},{5,6},{6,7},{7,4},{8,9},{9,10},{10,1... | collective-permute-start | bytes 786440 | tf_op jit(solution)/shard_map/ppermute | solution.py:69
  133.2 15.6 %collective-permute-start.18 = (bf16[128,1024]{1,0:T(8,128)(2,1)S(1)}, bf16[128,1024]{1,0:T(8,128)(2,1)S(1)}, u32[]{:S(2)}, u32[]{:S(2)}) collective-permute-start(bf16[128,1024]{1,0:T(8,128)(2,1)S(1)} %copy-done.18), channel_id=1, source_target_pairs={{0,1},{1,2},{2,3},{3,0},{4,5},{5,6},{6,7},{7,4},{8,9},{9,10},{10,1... | collective-permute-start | bytes 786440 | tf_op jit(solution)/shard_map/ppermute | solution.py:65
  133.9 22.8 %collective-permute-start.19 = (bf16[128,1024]{1,0:T(8,128)(2,1)S(1)}, bf16[128,1024]{1,0:T(8,128)(2,1)S(1)}, u32[]{:S(2)}, u32[]{:S(2)}) collective-permute-start(bf16[128,1024]{1,0:T(8,128)(2,1)S(1)} %copy-done.17), channel_id=1, source_target_pairs={{0,2},{1,3},{2,0},{3,1},{4,6},{5,7},{6,4},{7,5},{8,10},{9,11},{10,... | collective-permute-start | bytes 786440 | tf_op jit(solution)/shard_map/ppermute | solution.py:65
  137.0 19.7 %collective-permute-start.20 = (bf16[128,1024]{1,0:T(8,128)(2,1)S(1)}, bf16[128,1024]{1,0:T(8,128)(2,1)S(1)}, u32[]{:S(2)}, u32[]{:S(2)}) collective-permute-start(bf16[128,1024]{1,0:T(8,128)(2,1)S(1)} %copy-done.16), channel_id=1, source_target_pairs={{0,3},{1,0},{2,1},{3,2},{4,7},{5,4},{6,5},{7,6},{8,11},{9,8},{10,9... | collective-permute-start | bytes 786440 | tf_op jit(solution)/shard_map/ppermute | solution.py:65
  160.3 9.4 %collective-permute-start.21 = (bf16[128,1024]{1,0:T(8,128)(2,1)}, bf16[128,1024]{1,0:T(8,128)(2,1)S(1)}, u32[]{:S(2)}, u32[]{:S(2)}) collective-permute-start(bf16[128,1024]{1,0:T(8,128)(2,1)} %shard_map.176.c0_ref), channel_id=1, source_target_pairs={{0,3},{1,0},{2,1},{3,2},{4,7},{5,4},{6,5},{7,6},{8,11},{9,8},{10,9... | collective-permute-start | bytes 786440 | tf_op jit(solution)/shard_map/ppermute | solution.py:69
  160.8 13.7 %collective-permute-start.22 = (bf16[128,1024]{1,0:T(8,128)(2,1)}, bf16[128,1024]{1,0:T(8,128)(2,1)S(1)}, u32[]{:S(2)}, u32[]{:S(2)}) collective-permute-start(bf16[128,1024]{1,0:T(8,128)(2,1)} %shard_map.176.c0_ref), channel_id=1, source_target_pairs={{0,2},{1,3},{2,0},{3,1},{4,6},{5,7},{6,4},{7,5},{8,10},{9,11},{10,... | collective-permute-start | bytes 786440 | tf_op jit(solution)/shard_map/ppermute | solution.py:69
  162.1 13.5 %collective-permute-start.23 = (bf16[128,1024]{1,0:T(8,128)(2,1)}, bf16[128,1024]{1,0:T(8,128)(2,1)S(1)}, u32[]{:S(2)}, u32[]{:S(2)}) collective-permute-start(bf16[128,1024]{1,0:T(8,128)(2,1)} %shard_map.176.c0_ref), channel_id=1, source_target_pairs={{0,1},{1,2},{2,3},{3,0},{4,5},{5,6},{6,7},{7,4},{8,9},{9,10},{10,1... | collective-permute-start | bytes 786440 | tf_op jit(solution)/shard_map/ppermute | solution.py:69
  164.9 12.6 %collective-permute-start.24 = (bf16[32,3456]{1,0:T(8,128)(2,1)}, bf16[32,3456]{1,0:T(8,128)(2,1)S(1)}, u32[]{:S(2)}, u32[]{:S(2)}) collective-permute-start(bf16[32,3456]{1,0:T(8,128)(2,1)} %get-tuple-element.162), channel_id=1, source_target_pairs={{0,32},{4,36},{8,40},{12,44},{16,48},{20,52},{24,56},{28,60},{32,6... | collective-permute-start | bytes 663560 | tf_op jit(solution)/shard_map/ppermute | solution.py:536
  166.5 11.8 %collective-permute-start.25 = (bf16[32,3456]{1,0:T(8,128)(2,1)S(1)}, bf16[32,3456]{1,0:T(8,128)(2,1)S(1)}, u32[]{:S(2)}, u32[]{:S(2)}) collective-permute-start(bf16[32,3456]{1,0:T(8,128)(2,1)S(1)} %get-tuple-element.161), channel_id=1, source_target_pairs={{0,64},{4,68},{8,72},{12,76},{16,80},{20,84},{24,88},{28,92},{32,9... | collective-permute-start | bytes 663560 | tf_op jit(solution)/shard_map/ppermute | solution.py:536
  169.7 8.6 %collective-permute-start.26 = (bf16[32,3456]{1,0:T(8,128)(2,1)S(1)}, bf16[32,3456]{1,0:T(8,128)(2,1)S(1)}, u32[]{:S(2)}, u32[]{:S(2)}) collective-permute-start(bf16[32,3456]{1,0:T(8,128)(2,1)S(1)} %get-tuple-element.160), channel_id=1, source_target_pairs={{0,96},{4,100},{8,104},{12,108},{16,112},{20,116},{24,120},{28,124... | collective-permute-start | bytes 663560 | tf_op jit(solution)/shard_map/ppermute | solution.py:536
  179.3 6.4 %collective-permute-start.27 = (bf16[32,1152]{1,0:T(8,128)(2,1)S(1)}, bf16[32,1152]{1,0:T(8,128)(2,1)S(1)}, u32[]{:S(2)}, u32[]{:S(2)}) collective-permute-start(bf16[32,1152]{1,0:T(8,128)(2,1)S(1)} %get-tuple-element.169), channel_id=1, source_target_pairs={{0,32},{4,36},{8,40},{12,44},{16,48},{20,52},{24,56},{28,60},{32,6... | collective-permute-start | bytes 221192 | tf_op jit(solution)/shard_map/ppermute | solution.py:536
  181.1 5.9 %collective-permute-start.28 = (bf16[32,1152]{1,0:T(8,128)(2,1)S(1)}, bf16[32,1152]{1,0:T(8,128)(2,1)S(1)}, u32[]{:S(2)}, u32[]{:S(2)}) collective-permute-start(bf16[32,1152]{1,0:T(8,128)(2,1)S(1)} %get-tuple-element.168), channel_id=1, source_target_pairs={{0,64},{4,68},{8,72},{12,76},{16,80},{20,84},{24,88},{28,92},{32,9... | collective-permute-start | bytes 221192 | tf_op jit(solution)/shard_map/ppermute | solution.py:536
  188.5 7.9 %collective-permute-start.30 = (f32[16,128]{1,0:T(8,128)S(1)}, f32[16,128]{1,0:T(8,128)S(1)}, u32[]{:S(2)}, u32[]{:S(2)}) collective-permute-start(f32[16,128]{1,0:T(8,128)S(1)} %slice.58), channel_id=1, source_target_pairs={{0,2},{1,3},{2,0},{3,1},{4,6},{5,7},{6,4},{7,5},{8,10},{9,11},{10,... | collective-permute-start | bytes 24584 | tf_op jit(solution)/shard_map/ppermute | solution.py:571
  191.7 4.9 %collective-permute-start.31 = (f32[16,128]{1,0:T(8,128)S(1)}, f32[16,128]{1,0:T(8,128)S(1)}, u32[]{:S(2)}, u32[]{:S(2)}) collective-permute-start(f32[16,128]{1,0:T(8,128)S(1)} %slice.58), channel_id=1, source_target_pairs={{0,1},{1,2},{2,3},{3,0},{4,5},{5,6},{6,7},{7,4},{8,9},{9,10},{10,1... | collective-permute-start | bytes 24584 | tf_op jit(solution)/shard_map/ppermute | solution.py:571
  191.7 4.9 %collective-permute-start.32 = (f32[16,128]{1,0:T(8,128)S(1)}, f32[16,128]{1,0:T(8,128)S(1)}, u32[]{:S(2)}, u32[]{:S(2)}) collective-permute-start(f32[16,128]{1,0:T(8,128)S(1)} %slice.58), channel_id=1, source_target_pairs={{0,3},{1,0},{2,1},{3,2},{4,7},{5,4},{6,5},{7,6},{8,11},{9,8},{10,9... | collective-permute-start | bytes 24584 | tf_op jit(solution)/shard_map/ppermute | solution.py:571
  (28 other events, 141.2 us)
Sparse Core Ops, SparseCore 0:
  92.7 64.5 all-reduce.1
Sparse Core Ops, SparseCore 1:
  95.6 43.9 reduce-scatter.2
  142.0 32.2 reduce-scatter.4
